TPU v7x, 32 devices: a whole 2x2x4 slice. The times are simulated.
32 devices in a mesh: dp: 8 (over z, y), seq: 4 (over x, core).
Axes of the slice: x: 2, y: 2, z: 4, core: 2. Of those that a mesh axis runs over, the one named last changes fastest.
Arguments:
- tokens: bfloat16 [8, 512, 1536], P('dp', 'seq'), may hold values from -6 to 6
- cotangent: bfloat16 [8, 512, 1536], P('dp', 'seq'), may hold values from -6 to 6
- timesteps: int32 [8], replicated, may hold values from 0 to 999
- grid_widths: int32 [8], P('dp'), may hold values from 16 to 64, as said below
- scan_path: int32 [8, 512], P('dp', 'seq'), may hold values from 0 to 511, as said below
- ada_weight: bfloat16 [1536, 4608], P(None, 'dp'), may hold values from -0.15625 to 0.15625
- ada_bias: float32 [4608], P('dp'), may hold values from -3 to 3
- edge: float32 [1536], replicated, may hold values from -5 to 5
- in_weight: bfloat16 [1536, 6144], replicated, may hold values from -0.15625 to 0.15625
- conv_weight: float32 [2, 4, 3072], replicated, may hold values from -3 to 3
- conv_bias: float32 [2, 3072], replicated, may hold values from -3 to 3
- xproj_weight: bfloat16 [2, 3072, 128], replicated, may hold values from -0.109375 to 0.109375
- dt_weight: bfloat16 [2, 96, 3072], replicated, may hold values from -0.625 to 0.625
- dt_bias: float32 [2, 3072], replicated, may hold values from -12 to -2
- a_log: float32 [2, 3072, 16], replicated, may hold values from 0 to 2.77
- skip: float32 [2, 3072], replicated, may hold values from 0.5 to 1.5
- out_weight: bfloat16 [3072, 1536], replicated, may hold values from -0.109375 to 0.109375
Outputs:
- result: bfloat16 [8, 512, 1536], P('dp', 'seq')
- grad_tokens: bfloat16 [8, 512, 1536], P('dp', 'seq')
- grad_ada_weight: float32 [1536, 4608], P(None, 'dp')
- grad_ada_bias: float32 [4608], P('dp')
- grad_edge: float32 [1536], replicated
- grad_in_weight: float32 [1536, 6144], P(('dp', 'seq'))
- grad_conv_weight: float32 [2, 4, 3072], replicated
- grad_conv_bias: float32 [2, 3072], replicated
- grad_xproj_weight: float32 [2, 3072, 128], replicated
- grad_dt_weight: float32 [2, 96, 3072], replicated
- grad_dt_bias: float32 [2, 3072], replicated
- grad_a_log: float32 [2, 3072, 16], replicated
- grad_skip: float32 [2, 3072], replicated
- grad_out_weight: float32 [3072, 1536], P(('dp', 'seq'))
Inputs may be any that keep to these rules, and one draw needn't show every extreme that they name: `grid_widths`: each is one of 16, 32 and 64; each of the three occurs. `scan_path`: for each image a permutation of its 512 raster indices that visits the grid's rows in order, each row left to right or right to left.
All inputs are finite; a program needn't handle non-finite values.
Results may differ from a plain program's by a relative error of at most 0.012.
The roundings to bfloat16 on the way count: a program that leaves them out, or rounds other values in their place, can miss the bound.
Values may be sent and summed in bfloat16 or wider, within the bound.
A program may use at most 256 MiB of HBM per device.

v0:
```python
import functools
import math

import jax
import jax.numpy as jnp
from jax import lax
from jax.experimental import pallas as pl
from jax.experimental.pallas import tpu as pltpu
from jax.sharding import PartitionSpec as P

STATE = 16
U = 16
TILE = 128
PARTS = 3
LOG2E = 1.4426950408889634
LN2 = 0.6931471805599453
F32 = jnp.float32
BF = jnp.bfloat16
epsilon = 1e-06
highest = lax.Precision.HIGHEST
MESH = pl.DeviceIdType.MESH
VMEM_SPEC = pl.BlockSpec(memory_space=pltpu.VMEM)


def iota(shape, dim):
    return lax.broadcasted_iota(jnp.int32, shape, dim)


def dot(a, b):
    return lax.dot_general(a, b, (((1,), (0,)), ((), ())), preferred_element_type=F32)


def dot_nt(a, b):
    return lax.dot_general(a, b, (((1,), (1,)), ((), ())), preferred_element_type=F32)


def dot_tn(a, b):
    return lax.dot_general(a, b, (((0,), (0,)), ((), ())), preferred_element_type=F32)


def softplus(x):
    return jnp.maximum(x, 0.0) + jnp.log1p(jnp.exp(-jnp.abs(x)))


def diag_of(rows, first):
    k = U * STATE
    pick = (iota((128, k), 0) - first == lax.rem(iota((128, k), 1), STATE)).astype(F32).astype(BF)
    keep = (iota((U, k), 1) // STATE == iota((U, k), 0)).astype(F32)
    return (dot(rows.astype(BF), pick) * keep).astype(BF)


def over_lanes(x, t):
    return jnp.broadcast_to(x[:, t : t + 1], (x.shape[0], 128))


def wide(x, n):
    return jnp.concatenate([x] * n, axis=1)


def lane_fold(x):
    acc = x[:, :128]
    for j in range(1, x.shape[1] // 128):
        acc = acc + x[:, 128 * j : 128 * (j + 1)]
    return acc


def interleave(steps, pieces):
    done = 0
    for i, step in enumerate(steps):
        step()
        while done < (i + 1) * len(pieces) // len(steps):
            pieces[done]()
            done += 1


def pipeline(groups, work, drain):
    interleave(work(0, 0), [])

    def two(p, carry):
        interleave(work(2 * p + 1, 1), drain(2 * p, 0))
        interleave(work(2 * p + 2, 0), drain(2 * p + 1, 1))
        return carry

    lax.fori_loop(0, groups // 2 - 1, two, 0)
    interleave(work(groups - 1, 1), drain(groups - 2, 0))
    interleave([lambda: None], drain(groups - 1, 1))


def forward_block(rev, dl, act, coef, a2, proj, dy, hp, put_y, dread, h_sc, hb_sc, slots, rows, red):
    length, chans = dl.shape
    groups = length // U
    part_width = chans // PARTS
    dlu, duu, dyu = rows
    dread[...] = jnp.zeros_like(dread)

    def place(k):
        return (groups - 1 - k) if rev else k

    def work(k, slot):
        g = place(k)
        t0 = pl.multiple_of(g * U, U)
        at = pl.ds(t0, U)
        dlu[...] = dl[at, :]
        duu[...] = dl[at, :] * act[at, :].astype(F32)
        dyu[...] = dy[at, :]
        inflow = coef[g][:STATE]
        spread = [over_lanes(inflow, t) for t in range(U)]
        hbuf = slots[slot]
        v = {}

        def token(part, i):
            col = pl.ds(part * part_width, part_width)
            if i == 0:
                v["a"], v["h"], v["hb"] = a2[:, col], h_sc[:, col], hb_sc[:, col]
            loc = (U - 1 - i) if rev else i
            one = pl.ds(loc, 1)
            h = jnp.exp2(dlu[one, col] * v["a"]) * v["h"] + duu[one, col] * wide(
                spread[loc], part_width // 128
            )
            hp[pl.ds(pl.multiple_of((t0 + loc) * STATE, STATE), STATE), col] = v["hb"]
            hb = h.astype(BF)
            hbuf[pl.ds(loc * STATE, STATE), col] = hb
            v["h"], v["hb"] = h, hb
            total = lane_fold(dyu[one, col] * h)
            if part:
                total = red[loc] + total
            if part < PARTS - 1:
                red[loc] = total
            else:
                here = iota((STATE, TILE), 1) == g * U + loc
                v["sum"] = jnp.where(here, jnp.sum(total, axis=1, keepdims=True), v.get("sum", 0.0))
                if i == U - 1:
                    dread[...] += v["sum"]
            if i == U - 1:
                h_sc[:, col] = h
                hb_sc[:, col] = hb

        return [functools.partial(token, part, i) for part in range(PARTS) for i in range(U)]

    def drain(k, slot):
        at = pl.ds(pl.multiple_of(place(k) * U, U), U)
        hbuf = slots[slot]
        v = {}

        def first():
            v["c"] = diag_of(proj[at, :], 128 - STATE)

        def out(c):
            col = pl.ds(256 * c, 256)
            put_y(at, col, dot(v["c"], hbuf[:, col]))

        return [first] + [functools.partial(out, c) for c in range(chans // 256)]

    pipeline(groups, work, drain)


def backward_block(
    rev, dl, act, coef, a2, proj, dy, skip, hp, dpre, dact, dflow, dalog, sums, g_sc, slots, rows, red
):
    length, chans = dl.shape
    groups = length // U
    part_width = chans // PARTS
    dlu, duu, dyu = rows
    dflow[...] = jnp.zeros_like(dflow)

    def place(k):
        return k if rev else (groups - 1 - k)

    def work(k, slot):
        g = place(k)
        t0 = pl.multiple_of(g * U, U)
        at = pl.ds(t0, U)
        dlu[...] = dl[at, :]
        duu[...] = dl[at, :] * act[at, :].astype(F32)
        dyu[...] = dy[at, :]
        readout = coef[g][STATE:]
        spread = [over_lanes(readout, t) for t in range(U)]
        gbuf, qbuf = slots[slot]
        v = {}

        def token(part, i):
            col = pl.ds(part * part_width, part_width)
            if i == 0:
                v["a"], v["car"], v["acc"] = a2[:, col], g_sc[:, col], dalog[:, col]
            loc = i if rev else (U - 1 - i)
            one = pl.ds(loc, 1)
            step = dlu[one, col]
            g_t = dyu[one, col] * wide(spread[loc], part_width // 128) + v["car"]
            car = jnp.exp2(step * v["a"]) * g_t
            before = hp[pl.ds(pl.multiple_of((t0 + loc) * STATE, STATE), STATE), col].astype(F32)
            q = car * before
            v["acc"] = v["acc"] + q * step
            v["car"] = car
            gbuf[pl.ds(loc * STATE, STATE), col] = g_t.astype(BF)
            total = lane_fold(duu[one, col] * g_t)
            if part:
                total = red[loc] + total
            if part < PARTS - 1:
                red[loc] = total
            else:
                here = iota((STATE, TILE), 1) == g * U + loc
                v["sum"] = jnp.where(here, jnp.sum(total, axis=1, keepdims=True), v.get("sum", 0.0))
                if i == U - 1:
                    dflow[...] += v["sum"]
            qa = q * v["a"]
            qa = qa[:8] + qa[8:]
            if i % 2 == 0:
                v["held"] = qa
            else:
                pair = [v["held"], qa] if rev else [qa, v["held"]]
                qbuf[pl.ds((loc // 2) * STATE, STATE), col] = jnp.concatenate(pair, 0).astype(BF)
            if i == U - 1:
                g_sc[:, col] = v["car"]
                dalog[:, col] = v["acc"]

        return [functools.partial(token, part, i) for part in range(PARTS) for i in range(U)]

    def drain(k, slot):
        at = pl.ds(pl.multiple_of(place(k) * U, U), U)
        gbuf, qbuf = slots[slot]
        v = {}

        def first():
            v["b"] = diag_of(proj[at, :], 128 - 2 * STATE)
            v["ones"] = (iota((U, U * 8), 1) // 8 == iota((U, U * 8), 0)).astype(F32).astype(BF)

        def cols(c):
            col = pl.ds(256 * c, 256)
            s = dot(v["b"], gbuf[:, col])
            q = dot(v["ones"], qbuf[:, col]) * LN2
            a = act[at, col].astype(F32)
            step = dl[at, col]
            grad = dy[at, col]
            pre = ((q + a * s) * (1.0 - jnp.exp(-step))).astype(BF)
            dpre[at, col] = pre
            dact[at, col] = step * s + skip[:, col] * grad
            sums[0, :, col] += pre.astype(F32)
            sums[1, :, col] += grad * a

        return [first] + [functools.partial(cols, c) for c in range(chans // 256)]

    pipeline(groups, work, drain)


def forward_kernel(
    proj, act, coef, dtw, dtb, a2, skip, dy, silu_z, slope_z, hidden, grad_branch, w_out,
    hp, dl, dread, branch, out_part, z_part, grad_z,
    y, h_sc, hb_sc, h_a, h_b, r0, r1, r2, red, gated,
):
    j = pl.program_id(0)
    blocks = pl.num_programs(0) // 2
    length, chans = dl.shape[1:]

    @pl.when(lax.rem(j, blocks) == 0)
    def _():
        h_sc[...] = jnp.zeros_like(h_sc)
        hb_sc[...] = jnp.zeros_like(hb_sc)

    pre = dot(proj[0].astype(BF), dtw[0]) + dtb[0]
    dl[0] = softplus(pre)

    def run(rev):
        base = (2 * blocks - 1 - j if rev else j) * length
        dy_block = dy.at[pl.ds(pl.multiple_of(base, length), length)]

        def put_y(at, col, value):
            value = value + skip[0, :, col] * act[0, at, col].astype(F32)
            rows = pl.ds(pl.multiple_of(base + at.start, U), U)
            if rev:
                value = value + y[rows, col]
            y[rows, col] = value

        forward_block(
            rev, dl.at[0], act.at[0], coef.at[0], a2.at[0], proj.at[0], dy_block, hp.at[0], put_y,
            dread.at[0, 0], h_sc, hb_sc, (h_a, h_b), (r0, r1, r2), red,
        )

    pl.when(j < blocks)(lambda: run(False))
    pl.when(j >= blocks)(lambda: run(True))

    @pl.when(j == 2 * blocks - 1)
    def _():
        total = y.shape[0]

        def rows_of(c, carry):
            at = pl.ds(pl.multiple_of(c * 64, 64), 64)
            value = y[at, :]
            gated[at, :] = (value * silu_z[at, :]).astype(BF)
            grad_z[at, :] = (value * slope_z[at, :]).astype(BF)
            return carry

        lax.fori_loop(0, total // 64, rows_of, 0)
        width = w_out.shape[1]

        def out_rows(c, carry):
            at = pl.ds(pl.multiple_of(c * 128, 128), 128)
            branch[at, :] = dot(gated[at, :], w_out[...]).astype(BF)
            return carry

        lax.fori_loop(0, total // 128, out_rows, 0)

        def out_cols(c, carry):
            at = pl.ds(pl.multiple_of(c * 128, 128), 128)
            out_part[at, :] = dot_tn(gated[:, at], grad_branch[...]).astype(BF)
            return carry

        lax.fori_loop(0, chans // 128, out_cols, 0)

        def z_cols(c, carry):
            at = pl.ds(pl.multiple_of(c * 128, 128), 128)
            z_part[at, :] = dot_tn(hidden[:, at], grad_z[...]).astype(BF)
            return carry

        lax.fori_loop(0, width // 128, z_cols, 0)


def scan_forward(proj, act, coef, dtw, dtb, a2, skip, dy, silu_z, slope_z, hidden, grad_branch, w_out):
    total, chans = dy.shape
    width = w_out.shape[1]
    blocks = total // TILE

    def place(j):
        d = j // blocks
        b = lax.rem(j, blocks)
        return d, b + d * (blocks - 1 - 2 * b)

    def tokens_of(j):
        d, b = place(j)
        return d, b, 0

    def direction_of(j):
        return j // blocks, 0, 0

    def cells(j):
        d, b = place(j)
        return d, b, 0, 0

    whole = VMEM_SPEC
    in_specs = [
        pl.BlockSpec((1, TILE, 128), tokens_of),
        pl.BlockSpec((1, TILE, chans), tokens_of),
        pl.BlockSpec((1, TILE // U, 2 * STATE, U), cells),
        pl.BlockSpec((1, 128, chans), direction_of),
        pl.BlockSpec((1, 1, chans), direction_of),
        pl.BlockSpec((1, STATE, chans), direction_of),
        pl.BlockSpec((1, 1, chans), direction_of),
    ] + [whole] * 6
    out_specs = [
        pl.BlockSpec((1, TILE * STATE, chans), tokens_of),
        pl.BlockSpec((1, TILE, chans), tokens_of),
        pl.BlockSpec((1, 1, STATE, TILE), cells),
    ] + [whole] * 4
    out_shape = [
        jax.ShapeDtypeStruct((2, total * STATE, chans), BF),
        jax.ShapeDtypeStruct((2, total, chans), F32),
        jax.ShapeDtypeStruct((2, blocks, STATE, TILE), F32),
        jax.ShapeDtypeStruct((total, width), BF),
        jax.ShapeDtypeStruct((chans, width), BF),
        jax.ShapeDtypeStruct((width, chans), BF),
        jax.ShapeDtypeStruct((total, chans), BF),
    ]
    return pl.pallas_call(
        forward_kernel,
        grid=(2 * blocks,),
        in_specs=in_specs,
        out_specs=out_specs,
        out_shape=out_shape,
        scratch_shapes=[
            pltpu.VMEM((total, chans), F32),
            pltpu.VMEM((STATE, chans), F32),
            pltpu.VMEM((STATE, chans), BF),
            pltpu.VMEM((U * STATE, chans), BF),
            pltpu.VMEM((U * STATE, chans), BF),
        ]
        + [pltpu.VMEM((U, chans), F32)] * 3
        + [pltpu.VMEM((U, STATE, 128), F32), pltpu.VMEM((total, chans), BF)],
        compiler_params=pltpu.CompilerParams(vmem_limit_bytes=60 << 20),
        name="scan_forward",
    )(proj, act, coef, dtw, dtb, a2, skip, dy, silu_z, slope_z, hidden, grad_branch, w_out)


def pre_kernel(
    s_ref, tok, cot, mod, flags, edge, w_x, w_z, w_out, conv_w, conv_b, xproj,
    hidden, grad_branch, xin, dy, silu_z, slope_z, act, slope, part, pad,
):
    j = pl.program_id(0)
    rows, width = tok.shape
    total, chans = xin.shape
    at = pl.ds(pl.multiple_of(j * rows, rows), rows)
    shift, scale, gate = (mod[:, k * width : (k + 1) * width] for k in range(3))
    tokens = tok[...].astype(F32)
    centred = tokens - jnp.mean(tokens, axis=1, keepdims=True)
    normed = centred * lax.rsqrt(jnp.mean(centred * centred, axis=1, keepdims=True) + epsilon)
    hid = (normed * (1.0 + scale) + shift + flags[...] * edge[...]).astype(BF)
    hidden[...] = hid
    grad = (cot[...].astype(F32) * gate).astype(BF)
    grad_branch[...] = grad
    xin[at, :] = dot(hid, w_x[...]).astype(BF)
    z = dot(hid, w_z[...])
    sigma = jax.nn.sigmoid(z)
    grad_gated = dot_nt(grad, w_out[...])
    silu_z[...] = z * sigma
    dy[...] = grad_gated * (z * sigma)
    slope_z[...] = grad_gated * (sigma * (1.0 + z * (1.0 - sigma)))

    @pl.when(j == pl.num_programs(0) - 1)
    def _():
        pad[:16, :] = jnp.zeros((16, chans), F32)
        pad[total + 16 :, :] = jnp.zeros((16, chans), F32)
        pad[16 : total + 16, :] = xin[...].astype(F32)
        step = 64

        def chunk(c, carry):
            base = pl.multiple_of(c * step, step)
            window = pad[pl.ds(base, step + 32), :]
            here = pl.ds(base, step)
            for d in range(2):
                value = conv_b[d : d + 1, :]
                for tap in range(4):
                    first = 13 + tap if d == 0 else 19 - tap
                    value = value + conv_w[d, tap : tap + 1, :] * window[first : first + step]
                sig = jax.nn.sigmoid(value)
                acted = (value * sig).astype(BF)
                act[d, here, :] = acted
                slope[d, here, :] = sig * (1.0 + value * (1.0 - sig))
                part[d, here, :] = dot(acted, xproj[d])
            return carry

        lax.fori_loop(0, total // step, chunk, 0)


def prepare(seq_index, tok, cot, mod, flags, edge, in_weight, out_weight, conv_w, conv_b, xproj):
    total, width = tok.shape
    inner = out_weight.shape[0]
    chans = inner // 4
    rows = 128

    def by_rows(j, s):
        return j, 0

    def fixed(j, s):
        return 0, 0

    token_rows = pl.BlockSpec((rows, width), by_rows)
    channel_rows = pl.BlockSpec((rows, chans), by_rows)
    in_specs = [
        token_rows,
        token_rows,
        pl.BlockSpec((1, 3 * width), fixed),
        pl.BlockSpec((rows, 1), by_rows),
        pl.BlockSpec((1, width), fixed),
        pl.BlockSpec((width, chans), lambda j, s: (0, s[0])),
        pl.BlockSpec((width, chans), lambda j, s: (0, 4 + s[0])),
        pl.BlockSpec((chans, width), lambda j, s: (s[0], 0)),
        pl.BlockSpec((2, 4, chans), lambda j, s: (0, 0, s[0])),
        pl.BlockSpec((2, chans), lambda j, s: (0, s[0])),
        pl.BlockSpec((2, chans, 128), lambda j, s: (0, s[0], 0)),
    ]
    out_specs = [token_rows, token_rows, pl.BlockSpec((total, chans), fixed)]
    out_specs += [channel_rows] * 3
    out_specs += [
        pl.BlockSpec((2, total, chans), lambda j, s: (0, 0, 0)),
        pl.BlockSpec((2, total, chans), lambda j, s: (0, 0, 0)),
        pl.BlockSpec((2, total, 128), lambda j, s: (0, 0, 0)),
    ]
    shape = jax.ShapeDtypeStruct
    out_shape = [
        shape((total, width), BF),
        shape((total, width), BF),
        shape((total, chans), BF),
        shape((total, chans), F32),
        shape((total, chans), F32),
        shape((total, chans), F32),
        shape((2, total, chans), BF),
        shape((2, total, chans), F32),
        shape((2, total, 128), F32),
    ]
    return pl.pallas_call(
        pre_kernel,
        grid_spec=pltpu.PrefetchScalarGridSpec(
            num_scalar_prefetch=1,
            grid=(total // rows,),
            in_specs=in_specs,
            out_specs=out_specs,
            scratch_shapes=[pltpu.VMEM((total + 32, chans), F32)],
        ),
        out_shape=out_shape,
        compiler_params=pltpu.CompilerParams(vmem_limit_bytes=60 << 20),
        name="prepare",
    )(seq_index, tok, cot, mod, flags, edge, in_weight, in_weight, out_weight, conv_w, conv_b, xproj)


def sibling_of(s):
    return s + 1 - 2 * lax.rem(s, 2)


def across_of(s):
    return lax.rem(s + 2, 4)


def remote(src, dst, sems, slot, peer):
    return pltpu.make_async_remote_copy(
        src_ref=src,
        dst_ref=dst,
        send_sem=sems[0].at[slot],
        recv_sem=sems[1].at[slot],
        device_id=peer,
        device_id_type=MESH,
    )


def greet(peers):
    barrier = pltpu.get_barrier_semaphore()
    for peer in peers:
        pl.semaphore_signal(barrier, inc=1, device_id=peer, device_id_type=MESH)
    pl.semaphore_wait(barrier, len(peers))


def comm_params(collective_id, mib=48):
    return pltpu.CompilerParams(
        collective_id=collective_id, has_side_effects=True, vmem_limit_bytes=mib << 20
    )


def gather_kernel(n_dp, tok_ref, mod_ref, all_ref, row_ref, send, recv, msend, mrecv, lsem):
    d, s = lax.axis_index("dp"), lax.axis_index("seq")
    sib, far = sibling_of(s), across_of(s)
    others = [lax.rem(d + k, n_dp) for k in range(1, n_dp)]
    greet([{"seq": sib}, {"seq": far}] + [{"dp": other} for other in others])
    sems = (send, recv)
    to_far = remote(tok_ref, all_ref.at[s], sems, 0, {"seq": far})
    to_sib = remote(tok_ref, all_ref.at[s], sems, 1, {"seq": sib})
    own = pltpu.make_async_copy(tok_ref, all_ref.at[s], lsem.at[0])
    own_row = pltpu.make_async_copy(mod_ref.at[d], row_ref.at[d], lsem.at[1])
    to_far.start()
    rows = []
    for k, other in enumerate(others):
        copy = remote(mod_ref.at[other], row_ref.at[d], (msend, mrecv), k, {"dp": other})
        copy.start()
        rows.append(copy)
    to_sib.start()
    own.start()
    own_row.start()
    to_far.wait()
    forward = remote(all_ref.at[far], all_ref.at[far], sems, 2, {"seq": sib})
    forward.start()
    for copy in rows:
        copy.wait()
    own.wait()
    own_row.wait()
    to_sib.wait()
    forward.wait()


def gather_tokens(tokens, mod_rows):
    n_dp = mod_rows.shape[0]
    dma = pltpu.SemaphoreType.DMA
    return pl.pallas_call(
        functools.partial(gather_kernel, n_dp),
        out_shape=[
            jax.ShapeDtypeStruct((4,) + tokens.shape, tokens.dtype),
            jax.ShapeDtypeStruct(mod_rows.shape, mod_rows.dtype),
        ],
        in_specs=[VMEM_SPEC] * 2,
        out_specs=[VMEM_SPEC] * 2,
        scratch_shapes=[dma((3,)), dma((3,)), dma((n_dp,)), dma((n_dp,)), dma((2,))],
        compiler_params=comm_params(0),
        name="gather_tokens",
    )(tokens, mod_rows)


def reduce_kernel(x_ref, out_ref, from_sib, half, from_x, send, recv):
    s = lax.axis_index("seq")
    sib, far = sibling_of(s), across_of(s)
    c = lax.rem(s, 2)
    greet([{"seq": sib}, {"seq": far}])
    sems = (send, recv)
    first = remote(x_ref.at[1 - c], from_sib, sems, 0, {"seq": sib})
    first.start()
    first.wait()
    half[...] = x_ref[c] + from_sib[...]
    second = remote(half, from_x, sems, 1, {"seq": far})
    second.start()
    second.wait()
    out_ref[c] = half[...] + from_x[...]
    third = remote(out_ref.at[c], out_ref.at[c], sems, 2, {"seq": sib})
    third.start()
    third.wait()


def seq_reduce(x, collective_id):
    _, rows, width = x.shape
    dma = pltpu.SemaphoreType.DMA
    return pl.pallas_call(
        reduce_kernel,
        out_shape=jax.ShapeDtypeStruct(x.shape, F32),
        in_specs=[VMEM_SPEC],
        out_specs=VMEM_SPEC,
        scratch_shapes=[pltpu.VMEM((rows, width), F32)] * 3 + [dma((3,)), dma((3,))],
        compiler_params=comm_params(collective_id),
        name="seq_reduce",
    )(x)


class DpScatter:
    def __init__(self, x, got, acc, far, sems):
        self.x, self.got, self.acc, self.far = x, got, acc, far
        self.sems = sems
        d = lax.axis_index("dp")
        n = lax.axis_size("dp") // 2
        self.n = n
        self.y = lax.rem(d, 2)
        self.z = d // 2
        self.order = [lax.rem(self.z + k, n) for k in range(1, n + 1)]

    @staticmethod
    def scratch(n_dp, block):
        n = n_dp // 2
        dma = pltpu.SemaphoreType.DMA
        return [pltpu.VMEM((n,) + block, BF)] * 3 + [dma((4, n))]

    def near_copy(self, k):
        z = self.order[k]
        peer = 2 * self.z + 1 - self.y
        return pltpu.make_async_remote_copy(
            src_ref=self.x.at[2 * z + 1 - self.y],
            dst_ref=self.got.at[z],
            send_sem=self.sems.at[0, k],
            recv_sem=self.sems.at[1, k],
            device_id={"dp": peer},
            device_id_type=MESH,
        )

    def near_arrival(self, k):
        return self.near_copy(k)

    def far_copy(self, k):
        z = self.order[k]
        return pltpu.make_async_remote_copy(
            src_ref=self.acc.at[z],
            dst_ref=self.far.at[k],
            send_sem=self.sems.at[2, k],
            recv_sem=self.sems.at[3, k],
            device_id={"dp": 2 * z + self.y},
            device_id_type=MESH,
        )

    def start(self):
        for k in range(self.n):
            self.near_copy(k).start()

    def pair(self, k):
        z = self.order[k]
        self.near_copy(k).wait()
        self.acc[z] = (self.x[2 * z + self.y].astype(F32) + self.got[z].astype(F32)).astype(BF)
        if k < self.n - 1:
            self.far_copy(k).start()

    def finish(self):
        for k in range(self.n - 1):
            self.far_copy(k).wait()
        total = self.x[2 * self.z + self.y].astype(F32) + self.got[self.z].astype(F32)
        for k in range(self.n - 1):
            total = total + self.far[k].astype(F32)
        return total


class SeqScatter:
    def __init__(self, x, from_sib, to_x, from_x, sems):
        s = lax.axis_index("seq")
        self.s, self.far = s, across_of(s)
        sib = sibling_of(s)
        self.x, self.from_sib, self.to_x, self.from_x = x, from_sib, to_x, from_x
        pair = (sems.at[0], sems.at[1])
        self.first = remote(x.at[across_of(sib)], from_sib.at[0], pair, 0, {"seq": sib})
        self.second = remote(x.at[sib], from_sib.at[1], pair, 1, {"seq": sib})
        self.third = remote(to_x, from_x, pair, 2, {"seq": self.far})

    @staticmethod
    def scratch(rows, width):
        return [
            pltpu.VMEM((2, rows, width), BF),
            pltpu.VMEM((rows, width), BF),
            pltpu.VMEM((rows, width), BF),
            pltpu.SemaphoreType.DMA((2, 3)),
        ]

    def start(self):
        self.first.start()
        self.second.start()

    def cross(self):
        self.first.wait()
        self.to_x[...] = (self.x[self.far].astype(F32) + self.from_sib[0].astype(F32)).astype(BF)
        self.third.start()

    def finish(self):
        self.second.wait()
        self.third.wait()
        return (
            self.x[self.s].astype(F32) + self.from_sib[1].astype(F32) + self.from_x[...].astype(F32)
        )


class SeqSwap:
    def __init__(self, src, dst, sems):
        s = lax.axis_index("seq")
        self.s, self.src, self.dst = s, src, dst
        pair = (sems.at[0], sems.at[1])
        self.copies = [
            remote(src.at[lax.rem(s + k, 4)], dst.at[s], pair, k - 1, {"seq": lax.rem(s + k, 4)})
            for k in (2, 1, 3)
        ]

    def start(self):
        for copy in self.copies:
            copy.start()
        self.dst[self.s] = self.src[self.s]

    def finish(self):
        for copy in self.copies:
            copy.wait()


def dp_others():
    n = lax.axis_size("dp")
    d = lax.axis_index("dp")
    return [lax.rem(d + k, n) for k in range(1, n)]


def seq_others():
    s = lax.axis_index("seq")
    return [lax.rem(s + k, 4) for k in (1, 2, 3)]


def greet_all():
    greet([{"seq": other} for other in seq_others()] + [{"dp": other} for other in dp_others()])


def last_kernel(*refs):
    (hid_in, x_in, small_in, tok_ref, cot_ref, flag_ref, scale_ref, gate_ref) = refs[:8]
    x_ref, small_ref, tokg_ref, table_ref = refs[8:12]
    seq = SeqScatter(hid_in, *refs[12:16])
    xs = DpScatter(x_in, *refs[16:20])
    smalls = DpScatter(small_in, *refs[20:24])
    red, swap_sems, row, rows_in, row_sems, table_sems, spread_sems = refs[24:]
    swap = SeqSwap(red, x_ref, swap_sems)
    d, s = lax.axis_index("dp"), lax.axis_index("seq")
    sib, far = sibling_of(s), across_of(s)
    n = smalls.n
    y, z = smalls.y, smalls.z
    greet_all()
    seq.start()
    smalls.start()
    seq.cross()
    xs.start()
    for k in range(n):
        smalls.pair(k)
    for k in range(n):
        xs.pair(k)

    width = tok_ref.shape[1]
    grad = seq.finish()
    tokens = tok_ref[...].astype(F32)
    centred = tokens - jnp.mean(tokens, axis=1, keepdims=True)
    inv_std = lax.rsqrt(jnp.mean(centred * centred, axis=1, keepdims=True) + epsilon)
    normed = centred * inv_std
    grad_normed = grad * (1.0 + scale_ref[...])
    inner_product = jnp.mean(grad_normed * normed, axis=1, keepdims=True)
    tokg_ref[...] = (
        cot_ref[...].astype(F32)
        + inv_std * (grad_normed - jnp.mean(grad_normed, axis=1, keepdims=True) - normed * inner_product)
    ).astype(BF)
    row[:, :width] = jnp.sum(grad, axis=0, keepdims=True)
    row[:, width : 2 * width] = jnp.sum(grad * normed, axis=0, keepdims=True)
    row[:, 2 * width : 3 * width] = gate_ref[...]
    row[:, 3 * width :] = jnp.sum(grad * flag_ref[...], axis=0, keepdims=True)
    pair = (row_sems.at[0], row_sems.at[1])
    row_copies = [
        remote(row, rows_in.at[k], pair, k, {"seq": other}) for k, other in enumerate(seq_others())
    ]
    for copy in row_copies:
        copy.start()

    small_ref[s, y, z] = smalls.finish().astype(BF)
    block = small_ref.at[s, y, z]
    spread_pair = (spread_sems.at[0], spread_sems.at[1])
    along_z = [
        remote(block, block, spread_pair, k, {"dp": 2 * smalls.order[k] + y}) for k in range(n - 1)
    ]
    for copy in along_z:
        copy.start()

    for copy in row_copies:
        copy.wait()
    total = row[...] + rows_in[1] + (rows_in[0] + rows_in[2])
    table_ref[d] = total
    table_pair = (table_sems.at[0], table_sems.at[1])
    table_copies = [
        remote(table_ref.at[d], table_ref.at[d], table_pair, k, {"dp": other})
        for k, other in enumerate(dp_others())
    ]
    for copy in table_copies:
        copy.start()

    for copy in along_z:
        copy.wait()
    plane = small_ref.at[s, y]
    along_y = remote(plane, plane, spread_pair, n - 1, {"dp": 2 * z + 1 - y})
    along_y.start()

    red[...] = xs.finish().astype(BF)
    swap.start()

    along_y.wait()
    mine = small_ref.at[s]
    along_x = remote(mine, mine, spread_pair, n, {"seq": far})
    to_sib = remote(mine, mine, spread_pair, n + 1, {"seq": sib})
    along_x.start()
    to_sib.start()
    along_x.wait()
    others = small_ref.at[far]
    forward = remote(others, others, spread_pair, n + 2, {"seq": sib})
    forward.start()
    swap.finish()
    for copy in table_copies:
        copy.wait()
    to_sib.wait()
    forward.wait()


def last_exchange(hid, x_part, small, tokens, cot, flags, scale, gate, collective_id):
    n_dp = x_part.shape[0]
    n = n_dp // 2
    _, rows, width = hid.shape
    dma = pltpu.SemaphoreType.DMA
    shapes = [
        jax.ShapeDtypeStruct(x_part.shape[1:], BF),
        jax.ShapeDtypeStruct((4, 2, n) + small.shape[1:], BF),
        jax.ShapeDtypeStruct((rows, width), BF),
        jax.ShapeDtypeStruct((n_dp, 1, 4 * width), F32),
    ]
    return pl.pallas_call(
        last_kernel,
        out_shape=shapes,
        in_specs=[VMEM_SPEC] * 8,
        out_specs=[VMEM_SPEC] * 4,
        scratch_shapes=SeqScatter.scratch(rows, width)
        + DpScatter.scratch(n_dp, x_part.shape[1:])
        + DpScatter.scratch(n_dp, small.shape[1:])
        + [
            pltpu.VMEM(x_part.shape[1:], BF),
            dma((2, 3)),
            pltpu.VMEM((1, 4 * width), F32),
            pltpu.VMEM((3, 1, 4 * width), F32),
            dma((2, 3)),
            dma((2, n_dp)),
            dma((2, n + 3)),
        ],
        compiler_params=comm_params(collective_id),
        name="last_exchange",
    )(hid, x_part, small, tokens, cot, flags, scale, gate)


def backward_kernel(*refs):
    (proj, act, coef, a2, skip, dl, hp, dy, branch_in, out_in, z_in) = refs[:11]
    (dpre, dact, dflow, dalog, sums, branch_ref, out_ref, z_ref) = refs[11:19]
    g_sc, g_a, g_b, q_a, q_b, r0, r1, r2, red = refs[19:28]
    seq = SeqScatter(branch_in, *refs[28:32])
    outs = DpScatter(out_in, *refs[32:36])
    zs = DpScatter(z_in, *refs[36:40])
    z_red, z_got, swap_sems = refs[40:]
    swap = SeqSwap(z_red, z_got, swap_sems)
    j = pl.program_id(0)
    blocks = pl.num_programs(0) // 2
    length = dl.shape[1]
    n = outs.n

    @pl.when(j == 0)
    def _():
        greet_all()
        seq.start()
        outs.start()

    @pl.when(j == 1)
    def _():
        seq.cross()

    for k in range(n):

        @pl.when(j == 2 + (k * 2) // n)
        def _(k=k):
            outs.pair(k)
            zs.near_copy(k).start()

        @pl.when(j == 5 + (k * 2) // n)
        def _(k=k):
            zs.pair(k)

    @pl.when(lax.rem(j, blocks) == 0)
    def _():
        g_sc[...] = jnp.zeros_like(g_sc)
        dalog[...] = jnp.zeros_like(dalog)
        sums[...] = jnp.zeros_like(sums)

    def run(rev):
        base = (j - blocks if rev else blocks - 1 - j) * length
        dy_block = dy.at[pl.ds(pl.multiple_of(base, length), length)]
        backward_block(
            rev, dl.at[0], act.at[0], coef.at[0], a2.at[0], proj.at[0], dy_block, skip.at[0], hp.at[0],
            dpre.at[0], dact.at[0], dflow.at[0, 0], dalog.at[0], sums.at[0], g_sc,
            ((g_a, q_a), (g_b, q_b)), (r0, r1, r2), red,
        )

    pl.when(j < blocks)(lambda: run(False))
    pl.when(j >= blocks)(lambda: run(True))

    @pl.when(j == 2 * blocks - 1)
    def _():
        branch_ref[...] = seq.finish()
        out_ref[...] = outs.finish().astype(BF)
        z_red[...] = zs.finish().astype(BF)
        swap.start()
        swap.finish()
        z_ref[...] = z_got[...]


def scan_backward(proj, act, coef, a2, skip, dl, hp, dy, branch, out_part, z_part, collective_id):
    total, chans = dy.shape
    blocks = total // TILE
    n_dp = out_part.shape[0]
    _, rows, width = branch.shape

    def place(j):
        d = j // blocks
        b = lax.rem(j, blocks)
        return d, blocks - 1 - b + d * (2 * b - blocks + 1)

    def tokens_of(j):
        d, b = place(j)
        return d, b, 0

    def direction_of(j):
        return j // blocks, 0, 0

    def cells(j):
        d, b = place(j)
        return d, b, 0, 0

    whole = VMEM_SPEC
    in_specs = [
        pl.BlockSpec((1, TILE, 128), tokens_of),
        pl.BlockSpec((1, TILE, chans), tokens_of),
        pl.BlockSpec((1, TILE // U, 2 * STATE, U), cells),
        pl.BlockSpec((1, STATE, chans), direction_of),
        pl.BlockSpec((1, 1, chans), direction_of),
        pl.BlockSpec((1, TILE, chans), tokens_of),
        pl.BlockSpec((1, TILE * STATE, chans), tokens_of),
    ] + [whole] * 4
    out_specs = [
        pl.BlockSpec((1, TILE, chans), tokens_of),
        pl.BlockSpec((1, TILE, chans), tokens_of),
        pl.BlockSpec((1, 1, STATE, TILE), cells),
        pl.BlockSpec((1, STATE, chans), direction_of),
        pl.BlockSpec((1, 2, U, chans), lambda j: (j // blocks, 0, 0, 0)),
    ] + [whole] * 3
    shape = jax.ShapeDtypeStruct
    out_shape = [
        shape((2, total, chans), BF),
        shape((2, total, chans), F32),
        shape((2, blocks, STATE, TILE), F32),
        shape((2, STATE, chans), F32),
        shape((2, 2, U, chans), F32),
        shape((rows, width), F32),
        shape(out_part.shape[1:], BF),
        shape(z_part.shape[1:], BF),
    ]
    return pl.pallas_call(
        backward_kernel,
        grid=(2 * blocks,),
        in_specs=in_specs,
        out_specs=out_specs,
        out_shape=out_shape,
        scratch_shapes=[
            pltpu.VMEM((STATE, chans), F32),
            pltpu.VMEM((U * STATE, chans), BF),
            pltpu.VMEM((U * STATE, chans), BF),
            pltpu.VMEM((U * 8, chans), BF),
            pltpu.VMEM((U * 8, chans), BF),
        ]
        + [pltpu.VMEM((U, chans), F32)] * 3
        + [pltpu.VMEM((U, STATE, 128), F32)]
        + SeqScatter.scratch(rows, width)
        + DpScatter.scratch(n_dp, out_part.shape[1:])
        + DpScatter.scratch(n_dp, z_part.shape[1:])
        + [pltpu.VMEM(z_part.shape[1:], BF)] * 2
        + [pltpu.SemaphoreType.DMA((2, 3))],
        compiler_params=comm_params(collective_id, 60),
        name="scan_backward",
    )(proj, act, coef, a2, skip, dl, hp, dy, branch, out_part, z_part)


def time_embedding(step_ids, model_width):
    halfway = model_width // 2
    frequency = jnp.exp(-math.log(10000.0) * jnp.arange(halfway, dtype=jnp.float32) / halfway)
    angles = step_ids.astype(jnp.float32)[:, None] * frequency[None, :]
    return jnp.concatenate([jnp.cos(angles), jnp.sin(angles)], axis=1)


def silu_slope(values):
    sigma = jax.nn.sigmoid(values)
    return sigma * (1.0 + values * (1.0 - sigma))


def shards(
    tokens,
    cotangent,
    timesteps,
    grid_widths,
    scan_path,
    ada_weight,
    ada_bias,
    edge,
    in_weight,
    conv_weight,
    conv_bias,
    xproj_weight,
    dt_weight,
    dt_bias,
    a_log,
    skip,
    out_weight,
):
    seg_len, width = tokens.shape[1:]
    inner = in_weight.shape[1] // 2
    rank = dt_weight.shape[1]
    taps = conv_weight.shape[1]
    rim = taps - 1
    columns = ada_weight.shape[1]
    n_seq = lax.axis_size("seq")
    n_dp = lax.axis_size("dp")
    dp_index = lax.axis_index("dp")
    seq_index = lax.axis_index("seq")
    length = seg_len * n_seq
    chans = inner // n_seq

    def mine(weight, dim, first=0):
        return lax.dynamic_slice_in_dim(weight, first + seq_index * chans, chans, dim)

    embedded = jax.nn.silu(time_embedding(timesteps, width)).astype(BF)
    modulation_part = jnp.dot(embedded, ada_weight, preferred_element_type=F32) + ada_bias
    gathered, modulation_own = gather_tokens(tokens[0], modulation_part[:, None, :])
    tokens_all = gathered.reshape(length, width)
    modulation_own = modulation_own.reshape(1, -1)
    scale_term = modulation_own[:, width : 2 * width]
    gate_term = modulation_own[:, 2 * width :]

    cotangent_all = lax.all_gather(cotangent[0], "seq", axis=0, tiled=True)
    path = lax.all_gather(scan_path[0], "seq", axis=0, tiled=True)

    def norm(values):
        values = values.astype(F32)
        centred = values - jnp.mean(values, axis=1, keepdims=True)
        inv_std = lax.rsqrt(jnp.mean(centred * centred, axis=1, keepdims=True) + epsilon)
        return centred * inv_std, inv_std

    def flags_of(item):
        return (jnp.remainder(item, grid_widths[0]) == grid_widths[0] - 1).astype(F32)[:, None]

    hidden, grad_branch, xin, dy, silu_z, slope_z, act, slope, part = prepare(
        seq_index.astype(jnp.int32)[None],
        tokens_all,
        cotangent_all,
        modulation_own,
        flags_of(path),
        edge[None],
        in_weight,
        out_weight,
        conv_weight,
        conv_bias,
        xproj_weight,
    )
    w_x, w_z = mine(in_weight, 1), mine(in_weight, 1, inner)
    w_out = mine(out_weight, 0)
    conv_w = mine(conv_weight, 2)
    padded = jnp.pad(xin, ((rim, rim), (0, 0))).astype(F32)
    starts = [list(range(taps)), [2 * rim - tap for tap in range(taps)]]
    xproj = mine(xproj_weight, 1)
    proj = seq_reduce(part, 1)
    dtw = jnp.pad(mine(dt_weight, 2), ((0, 0), (0, 128 - rank), (0, 0)))
    dtb = mine(dt_bias, 1)
    decay = -jnp.exp(jnp.swapaxes(mine(a_log, 1), 1, 2))
    decay2 = decay * LOG2E
    skips = mine(skip, 1)

    coef = jnp.swapaxes(proj[:, :, 128 - 2 * STATE :].reshape(2, length // U, U, 2 * STATE), 2, 3)
    held, delta, dread, branch, out_part, z_part, grad_z = scan_forward(
        proj, act, coef, dtw, dtb[:, None], decay2, skips[:, None], dy, silu_z, slope_z, hidden,
        grad_branch, w_out,
    )
    total = n_dp * n_seq

    def product(left, right):
        return lax.dot_general(
            left, right, (((0,), (0,)), ((), ())), preferred_element_type=F32
        ).astype(BF)

    def in_blocks(grad):
        return grad.reshape(n_dp, n_seq, width // total, chans)

    dpre, dact, dflow, dalog, sums, branch, out_rows, in_z = scan_backward(
        proj, act, coef, decay2, skips[:, None], delta, held, dy,
        branch.reshape(n_seq, seg_len, width),
        out_part.reshape(n_dp, chans // n_dp, width),
        in_blocks(z_part),
        2,
    )
    out_grad = lax.ppermute(
        out_rows,
        ("dp", "seq"),
        [(d * n_seq + s, s * n_dp + d) for d in range(n_dp) for s in range(n_seq)],
    ).astype(F32)
    tok_float = tokens[0].astype(F32)
    cot_float = cotangent[0].astype(F32)
    result = (tok_float + gate_term * branch).astype(BF)
    gate_grad = jnp.sum(cot_float * branch, axis=0, keepdims=True)

    coef_grad = jnp.concatenate([dflow, dread], axis=2)
    coef_grad = jnp.swapaxes(coef_grad, 2, 3).reshape(2, length, 2 * STATE)
    partial = jnp.stack(
        [
            lax.dot_general(dpre[d], dtw[d], (((1,), (1,)), ((), ())), preferred_element_type=F32)
            for d in range(2)
        ]
    ) + jnp.pad(coef_grad, ((0, 0), (0, 0), (128 - 2 * STATE, 0)))
    dproj = seq_reduce(partial, 3).astype(BF)
    dalog = dalog * decay
    sums = jnp.sum(sums, axis=2)
    grad_conv, small, xproj_grads = [], [], []
    for d in range(2):
        grad_act = (
            lax.dot_general(dproj[d], xproj[d], (((1,), (1,)), ((), ())), preferred_element_type=F32)
            + dact[d]
        )
        dconv = grad_act * slope[d]
        grad_conv.append(dconv)
        xproj_grads.append(
            lax.dot_general(
                dproj[d], act[d], (((0,), (0,)), ((), ())), preferred_element_type=F32
            )
        )
        dtw_grad = lax.dot_general(
            proj[d].astype(BF), dpre[d], (((0,), (0,)), ((), ())), preferred_element_type=F32
        )[:rank]
        conv_rows = jnp.stack(
            [jnp.sum(dconv * padded[first : first + length], axis=0) for first in starts[d]]
        )
        vectors = jnp.concatenate([jnp.sum(dconv, axis=0)[None], sums[d]], axis=0)
        small.append(jnp.concatenate([dtw_grad, dalog[d], conv_rows, vectors], axis=0))
    dxin = 0.0
    for d in range(2):
        for tap in range(taps):
            first = starts[d][tap]
            dxin = dxin + jnp.pad(
                conv_w[d, tap] * grad_conv[d], ((first, 2 * rim - first), (0, 0))
            )
    dxin = dxin[rim : rim + length].astype(BF)
    grad_hidden = (
        lax.dot_general(dxin, w_x, (((1,), (1,)), ((), ())), preferred_element_type=F32)
        + lax.dot_general(grad_z, w_z, (((1,), (1,)), ((), ())), preferred_element_type=F32)
    ).astype(BF)
    rows = jnp.concatenate(
        [xproj_grads[0], small[0], xproj_grads[1], small[1]], axis=0
    )
    n_rows = rows.shape[0]
    rows = jnp.pad(rows.astype(BF), ((0, -n_rows % (16 * n_dp)), (0, 0)))
    in_x, rows, grad_tok, table = last_exchange(
        grad_hidden.reshape(n_seq, seg_len, width),
        in_blocks(product(hidden, dxin)),
        rows.reshape(n_dp, -1, chans),
        tokens[0],
        cotangent[0],
        flags_of(scan_path[0]),
        scale_term,
        gate_grad,
        4,
    )
    in_grad = jnp.concatenate([in_x, in_z], axis=0)
    in_grad = jnp.swapaxes(in_grad, 0, 1).reshape(-1, 2 * inner).astype(F32)
    table = table.reshape(n_dp, -1)
    edge_grad = jnp.sum(table[:, 3 * width :], axis=0)
    mod_columns = lax.dynamic_slice_in_dim(table[:, : 3 * width], dp_index * columns, columns, 1)
    ada_b_grad = jnp.sum(mod_columns, axis=0)
    ada_w_grad = jnp.dot(embedded.astype(F32).T, mod_columns, precision=highest)

    rows = jnp.transpose(rows, (2, 1, 3, 0, 4)).reshape(-1, inner)[:n_rows]
    rows = rows.reshape(2, -1, inner).astype(F32)
    cuts = [128, 128 + rank, 128 + rank + STATE, 128 + rank + STATE + taps]
    xproj_grad = jnp.swapaxes(rows[:, : cuts[0]], 1, 2)
    dtw_grad = rows[:, cuts[0] : cuts[1]]
    alog_grad = jnp.swapaxes(rows[:, cuts[1] : cuts[2]], 1, 2)
    convw_grad = rows[:, cuts[2] : cuts[3]]
    last = cuts[3]
    return (
        result[None],
        grad_tok[None],
        ada_w_grad,
        ada_b_grad,
        edge_grad,
        in_grad,
        convw_grad,
        rows[:, last],
        xproj_grad,
        dtw_grad,
        rows[:, last + 1],
        alog_grad,
        rows[:, last + 2],
        out_grad,
    )


def solution(mesh):
    in_specs = (
        P("dp", "seq", None),
        P("dp", "seq", None),
        P(),
        P("dp"),
        P("dp", "seq"),
        P(None, "dp"),
        P("dp"),
        P(),
        P(),
        P(),
        P(),
        P(),
        P(),
        P(),
        P(),
        P(),
        P(),
    )
    out_specs = (
        P("dp", "seq", None),
        P("dp", "seq", None),
        P(None, "dp"),
        P("dp"),
        P(),
        P(("dp", "seq"), None),
        P(),
        P(),
        P(),
        P(),
        P(),
        P(),
        P(),
        P(("dp", "seq"), None),
    )
    return jax.shard_map(shards, mesh=mesh, in_specs=in_specs, out_specs=out_specs, check_vma=False)
```

profile of v0, /device:TPU:11, one launch (start us, length us, event | category | flops | bytes accessed | tf_op | source)
XLA Modules:
  0.0 396.6 jit_solution(6107823826726813802)
XLA Ops:
  8.6 5.6 %all-gather.1 = s32[1,512]{1,0:T(1,128)S(1)} all-gather(s32[1,128]{1,0:T(1,128)} %param.21), channel_id=3, replica_groups=mesh['dp'=8,'seq'=4] {'seq'}, dimensions={1}, use_global_device_ids=true | all-gather | bytes 2560 | tf_op jit(solution)/shard_map/all_gather | solution.py:1059
  14.5 0.9 copy.50.flags
  16.2 1.2 convolution_add_fusion.1
  17.5 21.1 %gather_tokens.1 = (bf16[4,128,1536]{2,1,0:T(8,128)(2,1)S(1)}, f32[8,1,576]{2,1,0:T(1,128)S(1)}) custom-call(bf16[128,1536]{1,0:T(8,128)(2,1)S(1)} %bitcast.133, f32[8,1,576]{2,1,0:T(1,128)S(1)} %broadcast_in_dim.42.mod_ref), custom_call_target="tpu_custom_call" | custom-call | tf_op jit(solution)/shard_map/gather_tokens/pallas_call | solution.py:558
  38.6 1.1 copy-done.6
  40.5 0.7 constant_dynamic-slice_fusion.6
  42.6 1.0 constant_dynamic-slice_fusion.7
  43.6 0.8 pad.47.dtw
  44.4 1.0 fusion.42
  45.4 1.6 bitcast_multiply_fusion.3.a2.refs_3_
  47.0 3.2 constant_dynamic-slice_fusion.5.w_out
  50.3 19.1 %prepare.1 = (bf16[512,1536]{1,0:T(8,128)(2,1)}, bf16[512,1536]{1,0:T(8,128)(2,1)}, bf16[512,768]{1,0:T(8,128)(2,1)}, f32[512,768]{1,0:T(8,128)}, f32[512,768]{1...) custom-call(s32[1]{0:T(128)} %bitcast.1.s_ref, ...), custom_call_target="tpu_custom_call" | custom-call | tf_op jit(solution)/shard_map/prepare/pallas_call | solution.py:478
  69.4 1.0 copy-done.7
  70.4 11.3 %seq_reduce.2.proj.refs_0_ = f32[2,512,128]{2,1,0:T(8,128)S(1)} custom-call(f32[2,512,128]{2,1,0:T(8,128)S(1)} %copy-done.7), custom_call_target="tpu_custom_call" | custom-call | tf_op jit(solution)/shard_map/seq_reduce/pallas_call | solution.py:594
  82.0 1.3 copy.51
  83.3 42.3 %scan_forward.1 = (bf16[2,8192,768]{2,1,0:T(8,128)(2,1)}, f32[2,512,768]{2,1,0:T(8,128)}, f32[2,4,16,128]{3,2,1,0:T(8,128)}, bf16[512,1536]{1,0:T(8,128)(2,1)}, ...) custom-call(f32[2,512,128]{2,1,0:T(8,128)} %copy-done.2, ...), custom_call_target="tpu_custom_call" | custom-call | tf_op jit(solution)/shard_map/scan_forward/pallas_call | solution.py:362
  125.6 77.4 %scan_backward.1 = (bf16[2,512,768]{2,1,0:T(8,128)(2,1)}, f32[2,512,768]{2,1,0:T(8,128)}, f32[2,4,16,128]{3,2,1,0:T(8,128)}, f32[2,16,768]{2,1,0:T(8,128)}, f32[...) custom-call(f32[2,512,128]{2,1,0:T(8,128)} %copy-done.2, ...), custom_call_target="tpu_custom_call" | custom-call | tf_op jit(solution)/shard_map/scan_backward/pallas_call | solution.py:978
  203.1 1.5 convolution_bitcast_fusion
  204.6 1.5 convolution_bitcast_fusion.1
  206.6 11.2 %seq_reduce.3 = f32[2,512,128]{2,1,0:T(8,128)S(1)} custom-call(f32[2,512,128]{2,1,0:T(8,128)S(1)} %maximum_add_fusion.x_ref), custom_call_target="tpu_custom_call" | custom-call | tf_op jit(solution)/shard_map/seq_reduce/pallas_call | solution.py:594
  220.3 1.4 copy-done.16
  221.7 2.0 bitcast_multiply_fusion.1
  224.2 7.0 %multiply_reduce_fusion = (bf16[768]{0:T(1024)(128)(2,1)S(1)}, bf16[768]{0:T(1024)(128)(2,1)S(1)}, bf16[768]{0:T(1024)(128)(2,1)S(1)}, bf16[768]{0:T(1024)(128)(...) fusion(f32[518,768]{1,0:T(8,128)S(1)} %pad_convert_fusion, ...), kind=kOutput, calls=%fused_computation.31 | convolution fusion | flops 111665664 | bytes 28687368 | tf_op jit(solution)/shard_map/dot_general | solution.py:1142
  231.3 0.9 fusion.30
  232.4 1.2 concatenate.15
  233.6 2.8 pad_add_fusion
  238.3 0.9 fusion.10
  239.7 2.8 convolution_convert_fusion
  242.5 3.2 fusion.2
  245.7 0.9 multiply_reduce_fusion.2
  246.8 3.1 fusion
  250.0 91.1 %last_exchange.1 = (bf16[4,48,768]{2,1,0:T(8,128)(2,1)S(1)}, bf16[4,2,4,64,768]{4,3,2,1,0:T(8,128)(2,1)}, bf16[128,1536]{1,0:T(8,128)(2,1)S(1)}, f32[8,1,6144]{2,1,0:T(1,128)S(1)}) custom-call(bf16[4,128,1536]{2,1,0:T(8,128)(2,1)S(1)} %bitcast.138, bf16[8,4,48,768]{3,2,1,0:T(8,128)(2,1)} %bitcast.147, bf16[8,64,768]{2,1,0:T(8,128)(2,1)S(1)} %bitcast.136, ...), custom_call_target="tpu_custom_call" | custom-call | tf_op jit(solution)/shard_map/last_exchange/pallas_call | solution.py:843
  341.0 4.3 %copy.60 = bf16[4,2,64,4,768]{4,3,2,1,0:T(4,128)(2,1)S(1)} copy(bf16[4,2,64,4,768]{4,2,0,1,3:T(8,128)(2,1)} %bitcast.144) | data formatting | bytes 6291456 | tf_op jit(solution)/shard_map/transpose | solution.py:1196
  346.0 3.4 slice_convert_fusion
  349.4 5.9 %reshape.137 = f32[2,247,3072]{2,1,0:T(8,128)} reshape(f32[494,3072]{1,0:T(8,128)} %slice_convert_fusion) | data formatting | bytes 12140544 | tf_op jit(solution)/shard_map/convert_element_type | solution.py:1197
  355.3 3.9 slice_bitcast_fusion
  359.2 3.3 slice.244
  362.5 1.8 slice_bitcast_fusion.1
  364.3 1.2 fusion.51
  365.5 1.6 slice.241
  367.1 3.6 copy.61
  372.6 1.1 copy.81
  373.8 1.9 collective-permute-start
  375.8 0.7 dynamic-slice_reduce_fusion
  377.1 3.6 fusion.33
  380.6 7.5 %collective-permute-done = bf16[96,1536]{1,0:T(8,128)(2,1)S(1)} collective-permute-done((bf16[96,1536]{1,0:T(8,128)(2,1)S(1)}, bf16[96,1536]{1,0:T(8,128)(2,1)S(1)}, u32[]{:S(2)}, u32[]{:S(2)}) %collective-permute-start) | collective-permute-done | bytes 294944 | tf_op jit(solution)/shard_map/ppermute | solution.py:1118
  388.1 0.9 convert_element_type.107
  389.0 0.7 copy.93
  (111 shorter events, 13.5 us)
Async XLA Ops:
  7.2 9.0 %copy-start = (bf16[1536,576]{0,1:T(8,128)(2,1)S(1)}, bf16[1536,576]{0,1:T(8,128)(2,1)}, u32[]{:S(2)}) copy-start(bf16[1536,576]{0,1:T(8,128)(2,1)} %param.22) | copy-start | bytes 5308420
  7.2 35.2 %copy-start.27 = (s32[1,128]{1,0:T(1,128)S(1)}, s32[1,128]{1,0:T(1,128)}, u32[]{:S(2)}) copy-start(s32[1,128]{1,0:T(1,128)} %param.21) | copy-start | bytes 1540
  7.2 10.3 %copy-start.4 = (bf16[1,128,1536]{2,1,0:T(8,128)(2,1)S(1)}, bf16[1,128,1536]{2,1,0:T(8,128)(2,1)}, u32[]{:S(2)}) copy-start(bf16[1,128,1536]{2,1,0:T(8,128)(2,1)} %param.17) | copy-start | bytes 1179652
  7.2 32.6 %copy-start.26 = (f32[1536]{0:T(1024)S(1)}, f32[1536]{0:T(1024)}, u32[]{:S(2)}) copy-start(f32[1536]{0:T(1024)} %param.24) | copy-start | bytes 18436
  7.2 43.0 %all-gather.4.cloned.1.call-start = ((), (), s32[]{:S(2)}) async-start(), calls=%async_computation | async-start | bytes 1966080 | tf_op jit(solution)/shard_map/all_gather | solution.py:1058
  38.6 1.1 copy-start.6
  39.9 10.4 %copy-start.22 = (f32[1,4608]{1,0:T(1,128)}, f32[1,4608]{1,0:T(1,128)S(1)}, u32[]{:S(2)}) copy-start(f32[1,4608]{1,0:T(1,128)S(1)} %reshape.123.mod) | copy-start | bytes 55300
  69.3 1.0 copy-start.7
  81.7 1.6 copy-start.2
  203.1 3.1 copy-start.24
  203.1 3.0 copy-start.25
  206.4 11.5 %copy-start.8 = (bf16[2,512,768]{2,1,0:T(8,128)(2,1)S(1)}, bf16[2,512,768]{2,1,0:T(8,128)(2,1)}, u32[]{:S(2)}) copy-start(bf16[2,512,768]{2,1,0:T(8,128)(2,1)} %get-tuple-element.47.act.refs_1_) | copy-start | bytes 4718596
  217.9 1.0 copy-start.3
  217.9 1.5 copy-start.14
  218.9 1.3 copy-start.19
  219.8 2.0 copy-start.16
  221.7 2.5 copy-start.17
  224.2 7.2 %copy-start.23 = (f32[2,16,768]{2,1,0:T(8,128)S(1)}, f32[2,16,768]{2,1,0:T(8,128)}, u32[]{:S(2)}) copy-start(f32[2,16,768]{2,1,0:T(8,128)} %get-tuple-element.65) | copy-start | bytes 294916
  224.2 8.1 %copy-start.21 = (f32[2,2,16,768]{3,2,1,0:T(8,128)S(1)}, f32[2,2,16,768]{3,2,1,0:T(8,128)}, u32[]{:S(2)}) copy-start(f32[2,2,16,768]{3,2,1,0:T(8,128)} %get-tuple-element.67) | copy-start | bytes 589828
  233.5 2.9 copy-start.13
  233.6 3.2 copy-start.9
  233.6 3.7 copy-start.10
  233.6 4.2 %copy-start.11 = (f32[512,768]{1,0:T(8,128)S(1)}, f32[512,768]{1,0:T(8,128)}, u32[]{:S(2)}) copy-start(f32[512,768]{1,0:T(8,128)} %get-tuple-element.146) | copy-start | bytes 4718596
  233.6 4.6 %copy-start.12 = (f32[512,768]{1,0:T(8,128)S(1)}, f32[512,768]{1,0:T(8,128)}, u32[]{:S(2)}) copy-start(f32[512,768]{1,0:T(8,128)} %get-tuple-element.147) | copy-start | bytes 4718596
  238.3 1.4 copy-start.15
  242.5 3.2 copy-start.5
  242.5 3.2 copy-start.18
  245.7 1.1 copy-start.28
  367.1 5.5 %copy-start.20 = (bf16[4,48,768]{2,1,0:T(8,128)(2,1)S(1)}, bf16[4,48,768]{2,1,0:T(8,128)(2,1)}, u32[]{:S(2)}) copy-start(bf16[4,48,768]{2,1,0:T(8,128)(2,1)} %get-tuple-element.71) | copy-start | bytes 884740
  372.6 1.2 copy-start.29
  373.8 14.3 %collective-permute-start = (bf16[96,1536]{1,0:T(8,128)(2,1)S(1)}, bf16[96,1536]{1,0:T(8,128)(2,1)S(1)}, u32[]{:S(2)}, u32[]{:S(2)}) collective-permute-start(bf16[96,1536]{1,0:T(8,128)(2,1)S(1)} %copy-done.29), channel_id=1, source_target_pairs={{0,0},{1,8},{2,16},{3,24},{4,1},{5,9},{6,17},{7,25},{8,2},{9,10},{... | collective-permute-start | bytes 884744 | tf_op jit(solution)/shard_map/ppermute | solution.py:1118
  377.1 12.7 %copy-start.1 = (bf16[1536,576]{0,1:T(8,128)(2,1)S(1)}, bf16[1536,576]{0,1:T(8,128)(2,1)}, u32[]{:S(2)}) copy-start(bf16[1536,576]{0,1:T(8,128)(2,1)} %param.22) | copy-start | bytes 5308420
Sparse Core Ops, SparseCore 0:
  9.6 26.2 all-gather.3
where the time goes:
time: 401 us; the launch traced here: 397 us
  Pallas kernels  274 us (68%)
  local copies, waits for them, and re-layouts  50.3 us (13%)
  matrix products  27.1 us (7%)
  between operations  15.4 us (4%)
  other arithmetic  14.5 us (4%)
  waiting for transfers between devices  8.18 us (2%)
  blocking collectives  5.65 us (1%)
    pallas_call x1, Pallas kernels, last_exchange(): pl.pallas_call(last_kernel, out_shape=shapes, in_specs=[VMEM_SPEC] * 8, o...  91.1 us
    pallas_call x1, Pallas kernels, scan_backward(): pl.pallas_call(backward_kernel, grid=(2 * blocks,), in_specs=in_specs, ou...  77.4 us
    pallas_call x1, Pallas kernels, scan_forward(): pl.pallas_call(forward_kernel, grid=(2 * blocks,), in_specs=in_specs, out...  42.3 us
    pallas_call x2, Pallas kernels, seq_reduce(): pl.pallas_call(reduce_kernel, out_shape=jax.ShapeDtypeStruct(x.shape, F32...  22.6 us
    pallas_call x1, Pallas kernels, gather_tokens(): pl.pallas_call(functools.partial(gather_kernel, n_dp), out_shape=[jax.Sha...  21.1 us
    pallas_call x1, Pallas kernels, prepare(): pl.pallas_call(pre_kernel, grid_spec=pltpu.PrefetchScalarGridSpec(num_sca...  19.1 us
    unnamed x67, local copies, waits for them, and re-layouts  14.5 us
    dot_general x2, matrix products, shards(): lax.dot_general(dproj[d], xproj[d], (((1,), (1,)), ((), ())), preferred_e...  9 us
  transfers between devices with their start and end apart: 2, of which 1 were waited for; matrix products, arithmetic and copies ran while one was open for 5% of the time, Pallas kernels for 5%

commit v1 on v0

--- a/solution.py
+++ b/solution.py
@@ -10,7 +10,6 @@
 
 STATE = 16
 U = 16
-TILE = 128
 PARTS = 3
 LOG2E = 1.4426950408889634
 LN2 = 0.6931471805599453
@@ -127,7 +126,7 @@
             if part < PARTS - 1:
                 red[loc] = total
             else:
-                here = iota((STATE, TILE), 1) == g * U + loc
+                here = iota(dread.shape, 1) == g * U + loc
                 v["sum"] = jnp.where(here, jnp.sum(total, axis=1, keepdims=True), v.get("sum", 0.0))
                 if i == U - 1:
                     dread[...] += v["sum"]
@@ -198,7 +197,7 @@
             if part < PARTS - 1:
                 red[loc] = total
             else:
-                here = iota((STATE, TILE), 1) == g * U + loc
+                here = iota(dflow.shape, 1) == g * U + loc
                 v["sum"] = jnp.where(here, jnp.sum(total, axis=1, keepdims=True), v.get("sum", 0.0))
                 if i == U - 1:
                     dflow[...] += v["sum"]
@@ -292,32 +291,22 @@
         lax.fori_loop(0, total // 64, rows_of, 0)
         width = w_out.shape[1]
 
-        def out_rows(c, carry):
-            at = pl.ds(pl.multiple_of(c * 128, 128), 128)
+        for c in range(2):
+            at = slice(c * total // 2, (c + 1) * total // 2)
             branch[at, :] = dot(gated[at, :], w_out[...]).astype(BF)
-            return carry
-
-        lax.fori_loop(0, total // 128, out_rows, 0)
-
-        def out_cols(c, carry):
-            at = pl.ds(pl.multiple_of(c * 128, 128), 128)
+
+        for c in range(2):
+            at = slice(c * chans // 2, (c + 1) * chans // 2)
             out_part[at, :] = dot_tn(gated[:, at], grad_branch[...]).astype(BF)
-            return carry
-
-        lax.fori_loop(0, chans // 128, out_cols, 0)
-
-        def z_cols(c, carry):
-            at = pl.ds(pl.multiple_of(c * 128, 128), 128)
+        for c in range(2):
+            at = slice(c * width // 2, (c + 1) * width // 2)
             z_part[at, :] = dot_tn(hidden[:, at], grad_z[...]).astype(BF)
-            return carry
-
-        lax.fori_loop(0, width // 128, z_cols, 0)
-
-
-def scan_forward(proj, act, coef, dtw, dtb, a2, skip, dy, silu_z, slope_z, hidden, grad_branch, w_out):
+
+
+def scan_forward(proj, act, coef, dtw, dtb, a2, skip, dy, silu_z, slope_z, hidden, grad_branch, w_out, tile):
     total, chans = dy.shape
     width = w_out.shape[1]
-    blocks = total // TILE
+    blocks = total // tile
 
     def place(j):
         d = j // blocks
@@ -337,23 +326,23 @@
 
     whole = VMEM_SPEC
     in_specs = [
-        pl.BlockSpec((1, TILE, 128), tokens_of),
-        pl.BlockSpec((1, TILE, chans), tokens_of),
-        pl.BlockSpec((1, TILE // U, 2 * STATE, U), cells),
+        pl.BlockSpec((1, tile, 128), tokens_of),
+        pl.BlockSpec((1, tile, chans), tokens_of),
+        pl.BlockSpec((1, tile // U, 2 * STATE, U), cells),
         pl.BlockSpec((1, 128, chans), direction_of),
         pl.BlockSpec((1, 1, chans), direction_of),
         pl.BlockSpec((1, STATE, chans), direction_of),
         pl.BlockSpec((1, 1, chans), direction_of),
     ] + [whole] * 6
     out_specs = [
-        pl.BlockSpec((1, TILE * STATE, chans), tokens_of),
-        pl.BlockSpec((1, TILE, chans), tokens_of),
-        pl.BlockSpec((1, 1, STATE, TILE), cells),
+        pl.BlockSpec((1, tile * STATE, chans), tokens_of),
+        pl.BlockSpec((1, tile, chans), tokens_of),
+        pl.BlockSpec((1, 1, STATE, tile), cells),
     ] + [whole] * 4
     out_shape = [
         jax.ShapeDtypeStruct((2, total * STATE, chans), BF),
         jax.ShapeDtypeStruct((2, total, chans), F32),
-        jax.ShapeDtypeStruct((2, blocks, STATE, TILE), F32),
+        jax.ShapeDtypeStruct((2, blocks, STATE, tile), F32),
         jax.ShapeDtypeStruct((total, width), BF),
         jax.ShapeDtypeStruct((chans, width), BF),
         jax.ShapeDtypeStruct((width, chans), BF),
@@ -422,7 +411,7 @@
                 sig = jax.nn.sigmoid(value)
                 acted = (value * sig).astype(BF)
                 act[d, here, :] = acted
-                slope[d, here, :] = sig * (1.0 + value * (1.0 - sig))
+                slope[d, here, :] = (sig * (1.0 + value * (1.0 - sig))).astype(BF)
                 part[d, here, :] = dot(acted, xproj[d])
             return carry
 
@@ -472,7 +461,7 @@
         shape((total, chans), F32),
         shape((total, chans), F32),
         shape((2, total, chans), BF),
-        shape((2, total, chans), F32),
+        shape((2, total, chans), BF),
         shape((2, total, 128), F32),
     ]
     return pl.pallas_call(
@@ -509,11 +498,11 @@
     )
 
 
-def greet(peers):
+def greet(peers, more=0):
     barrier = pltpu.get_barrier_semaphore()
     for peer in peers:
         pl.semaphore_signal(barrier, inc=1, device_id=peer, device_id_type=MESH)
-    pl.semaphore_wait(barrier, len(peers))
+    pl.semaphore_wait(barrier, len(peers) + more)
 
 
 def comm_params(collective_id, mib=48):
@@ -603,8 +592,9 @@
 
 
 class DpScatter:
-    def __init__(self, x, got, acc, far, sems):
+    def __init__(self, x, got, acc, far, sems, out=None):
         self.x, self.got, self.acc, self.far = x, got, acc, far
+        self.out = x if out is None else out
         self.sems = sems
         d = lax.axis_index("dp")
         n = lax.axis_size("dp") // 2
@@ -623,7 +613,7 @@
         z = self.order[k]
         peer = 2 * self.z + 1 - self.y
         return pltpu.make_async_remote_copy(
-            src_ref=self.x.at[2 * z + 1 - self.y],
+            src_ref=self.out.at[2 * z + 1 - self.y],
             dst_ref=self.got.at[z],
             send_sem=self.sems.at[0, k],
             recv_sem=self.sems.at[1, k],
@@ -659,21 +649,22 @@
     def finish(self):
         for k in range(self.n - 1):
             self.far_copy(k).wait()
-        total = self.x[2 * self.z + self.y].astype(F32) + self.got[self.z].astype(F32)
+        total = self.acc[self.z].astype(F32)
         for k in range(self.n - 1):
             total = total + self.far[k].astype(F32)
         return total
 
 
 class SeqScatter:
-    def __init__(self, x, from_sib, to_x, from_x, sems):
+    def __init__(self, x, from_sib, to_x, from_x, sems, out=None):
+        out = x if out is None else out
         s = lax.axis_index("seq")
         self.s, self.far = s, across_of(s)
         sib = sibling_of(s)
         self.x, self.from_sib, self.to_x, self.from_x = x, from_sib, to_x, from_x
         pair = (sems.at[0], sems.at[1])
-        self.first = remote(x.at[across_of(sib)], from_sib.at[0], pair, 0, {"seq": sib})
-        self.second = remote(x.at[sib], from_sib.at[1], pair, 1, {"seq": sib})
+        self.first = remote(out.at[across_of(sib)], from_sib.at[0], pair, 0, {"seq": sib})
+        self.second = remote(out.at[sib], from_sib.at[1], pair, 1, {"seq": sib})
         self.third = remote(to_x, from_x, pair, 2, {"seq": self.far})
 
     @staticmethod
@@ -733,183 +724,264 @@
     return [lax.rem(s + k, 4) for k in (1, 2, 3)]
 
 
-def greet_all():
-    greet([{"seq": other} for other in seq_others()] + [{"dp": other} for other in dp_others()])
-
-
-def last_kernel(*refs):
-    (hid_in, x_in, small_in, tok_ref, cot_ref, flag_ref, scale_ref, gate_ref) = refs[:8]
-    x_ref, small_ref, tokg_ref, table_ref = refs[8:12]
-    seq = SeqScatter(hid_in, *refs[12:16])
-    xs = DpScatter(x_in, *refs[16:20])
-    smalls = DpScatter(small_in, *refs[20:24])
-    red, swap_sems, row, rows_in, row_sems, table_sems, spread_sems = refs[24:]
-    swap = SeqSwap(red, x_ref, swap_sems)
-    d, s = lax.axis_index("dp"), lax.axis_index("seq")
-    sib, far = sibling_of(s), across_of(s)
-    n = smalls.n
-    y, z = smalls.y, smalls.z
-    greet_all()
-    seq.start()
-    smalls.start()
-    seq.cross()
-    xs.start()
-    for k in range(n):
-        smalls.pair(k)
-    for k in range(n):
-        xs.pair(k)
-
-    width = tok_ref.shape[1]
-    grad = seq.finish()
-    tokens = tok_ref[...].astype(F32)
-    centred = tokens - jnp.mean(tokens, axis=1, keepdims=True)
-    inv_std = lax.rsqrt(jnp.mean(centred * centred, axis=1, keepdims=True) + epsilon)
-    normed = centred * inv_std
-    grad_normed = grad * (1.0 + scale_ref[...])
-    inner_product = jnp.mean(grad_normed * normed, axis=1, keepdims=True)
-    tokg_ref[...] = (
-        cot_ref[...].astype(F32)
-        + inv_std * (grad_normed - jnp.mean(grad_normed, axis=1, keepdims=True) - normed * inner_product)
-    ).astype(BF)
-    row[:, :width] = jnp.sum(grad, axis=0, keepdims=True)
-    row[:, width : 2 * width] = jnp.sum(grad * normed, axis=0, keepdims=True)
-    row[:, 2 * width : 3 * width] = gate_ref[...]
-    row[:, 3 * width :] = jnp.sum(grad * flag_ref[...], axis=0, keepdims=True)
-    pair = (row_sems.at[0], row_sems.at[1])
-    row_copies = [
-        remote(row, rows_in.at[k], pair, k, {"seq": other}) for k, other in enumerate(seq_others())
-    ]
-    for copy in row_copies:
-        copy.start()
-
-    small_ref[s, y, z] = smalls.finish().astype(BF)
-    block = small_ref.at[s, y, z]
-    spread_pair = (spread_sems.at[0], spread_sems.at[1])
-    along_z = [
-        remote(block, block, spread_pair, k, {"dp": 2 * smalls.order[k] + y}) for k in range(n - 1)
-    ]
-    for copy in along_z:
-        copy.start()
-
-    for copy in row_copies:
-        copy.wait()
-    total = row[...] + rows_in[1] + (rows_in[0] + rows_in[2])
-    table_ref[d] = total
-    table_pair = (table_sems.at[0], table_sems.at[1])
-    table_copies = [
-        remote(table_ref.at[d], table_ref.at[d], table_pair, k, {"dp": other})
-        for k, other in enumerate(dp_others())
-    ]
-    for copy in table_copies:
-        copy.start()
-
-    for copy in along_z:
-        copy.wait()
-    plane = small_ref.at[s, y]
-    along_y = remote(plane, plane, spread_pair, n - 1, {"dp": 2 * z + 1 - y})
-    along_y.start()
-
-    red[...] = xs.finish().astype(BF)
-    swap.start()
-
-    along_y.wait()
-    mine = small_ref.at[s]
-    along_x = remote(mine, mine, spread_pair, n, {"seq": far})
-    to_sib = remote(mine, mine, spread_pair, n + 1, {"seq": sib})
-    along_x.start()
-    to_sib.start()
-    along_x.wait()
-    others = small_ref.at[far]
-    forward = remote(others, others, spread_pair, n + 2, {"seq": sib})
-    forward.start()
-    swap.finish()
-    for copy in table_copies:
-        copy.wait()
-    to_sib.wait()
-    forward.wait()
-
-
-def last_exchange(hid, x_part, small, tokens, cot, flags, scale, gate, collective_id):
-    n_dp = x_part.shape[0]
-    n = n_dp // 2
-    _, rows, width = hid.shape
-    dma = pltpu.SemaphoreType.DMA
-    shapes = [
-        jax.ShapeDtypeStruct(x_part.shape[1:], BF),
-        jax.ShapeDtypeStruct((4, 2, n) + small.shape[1:], BF),
-        jax.ShapeDtypeStruct((rows, width), BF),
-        jax.ShapeDtypeStruct((n_dp, 1, 4 * width), F32),
-    ]
-    return pl.pallas_call(
-        last_kernel,
-        out_shape=shapes,
-        in_specs=[VMEM_SPEC] * 8,
-        out_specs=[VMEM_SPEC] * 4,
-        scratch_shapes=SeqScatter.scratch(rows, width)
-        + DpScatter.scratch(n_dp, x_part.shape[1:])
-        + DpScatter.scratch(n_dp, small.shape[1:])
-        + [
-            pltpu.VMEM(x_part.shape[1:], BF),
-            dma((2, 3)),
-            pltpu.VMEM((1, 4 * width), F32),
-            pltpu.VMEM((3, 1, 4 * width), F32),
-            dma((2, 3)),
-            dma((2, n_dp)),
-            dma((2, n + 3)),
-        ],
-        compiler_params=comm_params(collective_id),
-        name="last_exchange",
-    )(hid, x_part, small, tokens, cot, flags, scale, gate)
+def greet_all(more=0):
+    greet([{"seq": other} for other in seq_others()] + [{"dp": other} for other in dp_others()], more)
+
+
+class Spread:
+    def __init__(self, buf, sems):
+        d, s = lax.axis_index("dp"), lax.axis_index("seq")
+        n = lax.axis_size("dp") // 2
+        y, z = lax.rem(d, 2), d // 2
+        sib, far = sibling_of(s), across_of(s)
+        pair = (sems.at[0], sems.at[1])
+        block, column, mine, other = buf.at[s, z, y], buf.at[s, :, y], buf.at[s], buf.at[far]
+        self.along_z = [
+            remote(block, block, pair, k, {"dp": 2 * lax.rem(z + k + 1, n) + y}) for k in range(n - 1)
+        ]
+        self.along_y = remote(column, column, pair, n - 1, {"dp": 2 * z + 1 - y})
+        self.along_x = remote(mine, mine, pair, n, {"seq": far})
+        self.to_sib = remote(mine, mine, pair, n + 1, {"seq": sib})
+        self.forward = remote(other, other, pair, n + 2, {"seq": sib})
+        self.place = (s, z, y)
+
+    @staticmethod
+    def scratch(n_dp, block):
+        n = n_dp // 2
+        return [pltpu.VMEM((4, n, 2) + block, BF), pltpu.SemaphoreType.DMA((2, n + 3))]
+
+    def go_z(self):
+        for copy in self.along_z:
+            copy.start()
+
+    def go_y(self):
+        for copy in self.along_z:
+            copy.wait()
+        self.along_y.start()
+
+    def go_x(self):
+        self.along_y.wait()
+        self.along_x.start()
+        self.to_sib.start()
+
+    def go_sib(self):
+        self.along_x.wait()
+        self.forward.start()
+
+    def finish(self):
+        self.to_sib.wait()
+        self.forward.wait()
+
+
+class SeqReduce:
+    def __init__(self, x, total, from_sib, half, from_x, sems):
+        s = lax.axis_index("seq")
+        self.c = c = lax.rem(s, 2)
+        sib, far = sibling_of(s), across_of(s)
+        pair = (sems.at[0], sems.at[1])
+        self.x, self.total, self.from_sib, self.half, self.from_x = x, total, from_sib, half, from_x
+        self.first = remote(x.at[1 - c], from_sib, pair, 0, {"seq": sib})
+        self.second = remote(half, from_x, pair, 1, {"seq": far})
+        self.third = remote(total.at[c], total.at[c], pair, 2, {"seq": sib})
+
+    @staticmethod
+    def scratch(rows, width):
+        return (
+            [pltpu.VMEM((2, rows, width), F32)] * 2
+            + [pltpu.VMEM((rows, width), F32)] * 3
+            + [pltpu.SemaphoreType.DMA((2, 3))]
+        )
+
+    def start(self):
+        self.first.start()
+
+    def cross(self):
+        self.first.wait()
+        self.half[...] = self.x[self.c] + self.from_sib[...]
+        self.second.start()
+
+    def back(self):
+        self.second.wait()
+        self.total[self.c] = self.half[...] + self.from_x[...]
+        self.third.start()
+
+    def finish(self):
+        self.third.wait()
+
+
+class Turn:
+    def __init__(self, src, dst, sems):
+        d, s = lax.axis_index("dp"), lax.axis_index("seq")
+        n_dp = lax.axis_size("dp")
+        here, target = 4 * d + s, s * n_dp + d
+        self.apart = here != target
+        self.source = {"dp": lax.rem(here, n_dp), "seq": here // n_dp}
+        self.copy = remote(
+            src, dst, (sems.at[0], sems.at[1]), 0, {"dp": target // 4, "seq": lax.rem(target, 4)}
+        )
+        self.src, self.dst = src, dst
+
+    def greet(self):
+        @pl.when(self.apart)
+        def _():
+            barrier = pltpu.get_barrier_semaphore()
+            pl.semaphore_signal(barrier, inc=1, device_id=self.source, device_id_type=MESH)
+
+        return jnp.where(self.apart, 1, 0)
+
+    def start(self):
+        pl.when(self.apart)(self.copy.start)
+
+        @pl.when(jnp.logical_not(self.apart))
+        def _():
+            self.dst[...] = self.src[...]
+
+    def finish(self):
+        pl.when(self.apart)(self.copy.wait)
+
+
+def rows_in_eights(x):
+    total = x[:8]
+    for k in range(1, x.shape[0] // 8):
+        total = total + x[8 * k : 8 * k + 8]
+    return total
 
 
 def backward_kernel(*refs):
-    (proj, act, coef, a2, skip, dl, hp, dy, branch_in, out_in, z_in) = refs[:11]
-    (dpre, dact, dflow, dalog, sums, branch_ref, out_ref, z_ref) = refs[11:19]
-    g_sc, g_a, g_b, q_a, q_b, r0, r1, r2, red = refs[19:28]
-    seq = SeqScatter(branch_in, *refs[28:32])
-    outs = DpScatter(out_in, *refs[32:36])
-    zs = DpScatter(z_in, *refs[36:40])
-    z_red, z_got, swap_sems = refs[40:]
-    swap = SeqSwap(z_red, z_got, swap_sems)
+    refs = list(refs)
+
+    def take(count):
+        taken = refs[:count]
+        del refs[:count]
+        return taken
+
+    (dl, hp, proj, act, coef, a2, skip, dy, dread, decay, conv_w) = take(11)
+    (tok, cot, gate, scale, flags) = take(5)
+    far_inputs = take(10)
+    in_weight, xproj_weight = far_inputs[4:6]
+    (result, tokg, in_ref, out_ref, a_ref, x0_ref, x1_ref, cv_ref, table_ref) = take(9)
+    g_sc, g_a, g_b, q_a, q_b, r0, r1, r2, red = take(9)
+    dpre, dc, dflow, dalog, sums = take(5)
+    slope, xpad, hidden, grad_z, w_x, w_z, xproj, dtw, hid_in, out_in, xs_in, local_sems = take(12)
+    conv_acc, dxin, gate_row = take(3)
+    seq1 = SeqScatter(hid_in, *take(4), out=far_inputs[7])
+    outs = DpScatter(out_in, *take(4), out=far_inputs[8])
+    zs = DpScatter(xs_in, *take(4), out=far_inputs[9])
+    out_red, out_got, turn_sems = take(3)
+    turn = Turn(out_red, out_got, turn_sems)
+    z_red, z_got, z_swap_sems = take(3)
+    z_swap = SeqSwap(z_red, z_got, z_swap_sems)
+    c7 = SeqReduce(*take(6))
+    smalls = []
+    for _ in range(5):
+        source = take(1)[0]
+        scatter = DpScatter(source, *take(4))
+        buf, sems = take(2)
+        smalls.append((source, scatter, buf, Spread(buf, sems)))
+    parts_a, parts_x, part_c = smalls[:2], smalls[2:4], smalls[4]
+    seq2 = SeqScatter(hid_in, *take(4))
+    xs = DpScatter(xs_in, *take(4))
+    x_red, x_got, x_swap_sems = take(3)
+    x_swap = SeqSwap(x_red, x_got, x_swap_sems)
+    row, rows_in, row_sems, table, table_sems, result_sems = take(6)
+
     j = pl.program_id(0)
     blocks = pl.num_programs(0) // 2
     length = dl.shape[1]
+    total = blocks * length
+    chans = dl.shape[2]
+    width = tok.shape[1]
     n = outs.n
+    n_dp = 2 * n
+    d_index, s_index = lax.axis_index("dp"), lax.axis_index("seq")
+
+    def loads():
+        own = pl.ds(pl.multiple_of(s_index * chans, 128), chans)
+        own_z = pl.ds(pl.multiple_of((4 + s_index) * chans, 128), chans)
+        pairs = [
+            (far_inputs[0], slope),
+            (far_inputs[1], xpad.at[pl.ds(16, total)]),
+            (far_inputs[2], hidden),
+            (far_inputs[3], grad_z),
+            (in_weight.at[:, own], w_x),
+            (in_weight.at[:, own_z], w_z),
+            (xproj_weight.at[:, own], xproj),
+            (far_inputs[6], dtw),
+            (far_inputs[7], hid_in),
+            (far_inputs[8], out_in),
+            (far_inputs[9], xs_in),
+        ]
+        return [pltpu.make_async_copy(a, b, local_sems.at[i]) for i, (a, b) in enumerate(pairs)]
+
+    def results():
+        pairs = []
+        for d in range(2):
+            buf = parts_a[d][2]
+            pairs += [(buf.at[q], a_ref.at[d, :, :, :, pl.ds(q * chans, chans)]) for q in range(4)]
+        pairs += [(parts_x[0][2], x0_ref), (parts_x[1][2], x1_ref), (part_c[2], cv_ref)]
+        return [pltpu.make_async_copy(a, b, result_sems.at[i]) for i, (a, b) in enumerate(pairs)]
+
+    near = [(outs, k) for k in range(n)] + [(zs, k) for k in range(n)]
+    start_at = [0, 0, 1, 3, 4, 6, 7, 8]
+    pair_at = [4, 5, 6, 7, 8, 8, 8, 8]
+
+    def step_of(plan, i):
+        return plan[i * 8 // (2 * n)]
+
+    unit = 2 * blocks // 8
 
     @pl.when(j == 0)
     def _():
-        greet_all()
-        seq.start()
-        outs.start()
-
-    @pl.when(j == 1)
+        greet_all(turn.greet())
+        seq1.start()
+        for copy in loads():
+            copy.start()
+        for d in range(2):
+            dc[d, :16, :] = jnp.zeros((16, chans), F32)
+            dc[d, total + 16 :, :] = jnp.zeros((16, chans), F32)
+        xpad[:16, :] = jnp.zeros((16, chans), BF)
+        xpad[total + 16 :, :] = jnp.zeros((16, chans), BF)
+        dalog[...] = jnp.zeros_like(dalog)
+        sums[...] = jnp.zeros_like(sums)
+        conv_acc[...] = jnp.zeros_like(conv_acc)
+
+    for i, (scatter, k) in enumerate(near):
+        if step_of(pair_at, i) < 8:
+            pl.when(j == unit * step_of(pair_at, i))(functools.partial(scatter.pair, k))
+        if step_of(start_at, i) < 8:
+            pl.when(j == unit * step_of(start_at, i))(scatter.near_copy(k).start)
+
+    @pl.when(j == 2 * unit)
     def _():
-        seq.cross()
-
-    for k in range(n):
-
-        @pl.when(j == 2 + (k * 2) // n)
-        def _(k=k):
-            outs.pair(k)
-            zs.near_copy(k).start()
-
-        @pl.when(j == 5 + (k * 2) // n)
-        def _(k=k):
-            zs.pair(k)
+        loads()[8].wait()
+        seq1.cross()
+
+    @pl.when(j == 3 * unit)
+    def _():
+        loads()[9].wait()
+        loads()[10].wait()
+
+
+    @pl.when(j == 5 * unit)
+    def _():
+        branch = seq1.finish()
+        result[...] = (tok[...].astype(F32) + gate[...] * branch).astype(BF)
+        gate_row[...] = jnp.sum(cot[...].astype(F32) * branch, axis=0, keepdims=True)
 
     @pl.when(lax.rem(j, blocks) == 0)
     def _():
         g_sc[...] = jnp.zeros_like(g_sc)
-        dalog[...] = jnp.zeros_like(dalog)
-        sums[...] = jnp.zeros_like(sums)
 
     def run(rev):
-        base = (j - blocks if rev else blocks - 1 - j) * length
-        dy_block = dy.at[pl.ds(pl.multiple_of(base, length), length)]
+        d = int(rev)
+        block = j - blocks if rev else blocks - 1 - j
+        base = pl.multiple_of(block * length, length)
+        here = pl.ds(base, length)
         backward_block(
-            rev, dl.at[0], act.at[0], coef.at[0], a2.at[0], proj.at[0], dy_block, skip.at[0], hp.at[0],
-            dpre.at[0], dact.at[0], dflow.at[0, 0], dalog.at[0], sums.at[0], g_sc,
-            ((g_a, q_a), (g_b, q_b)), (r0, r1, r2), red,
+            rev, dl.at[0], act.at[d, here], coef.at[0], a2.at[d],
+            proj.at[d, here], dy.at[here], skip.at[d], hp.at[0], dpre.at[d, here],
+            dc.at[d, pl.ds(pl.multiple_of(base + 16, 16), length)], dflow.at[d, block], dalog.at[d],
+            sums.at[d], g_sc, ((g_a, q_a), (g_b, q_b)), (r0, r1, r2), red,
         )
 
     pl.when(j < blocks)(lambda: run(False))
@@ -917,19 +989,217 @@
 
     @pl.when(j == 2 * blocks - 1)
     def _():
-        branch_ref[...] = seq.finish()
-        out_ref[...] = outs.finish().astype(BF)
+        late = [i for i in range(2 * n) if step_of(start_at, i) >= 8]
+        for i in late:
+            near[i][0].near_copy(near[i][1]).start()
+        for copy in loads()[:8]:
+            copy.wait()
+        for d in range(2):
+            value = dot_nt(dpre[d], dtw[d])
+            for b in range(blocks):
+                at = slice(b * length, (b + 1) * length)
+                square = jnp.concatenate(
+                    [jnp.zeros((128 - 2 * STATE, length), F32), dflow[d, b], dread[d, b]], axis=0
+                )
+                c7.x[d, at] = value[at] + square.T
+        c7.start()
+        late = [i for i in range(2 * n) if step_of(pair_at, i) >= 8]
+        quarter = len(late) // 4
+        rank = 128 - 2 * STATE
+        per_d = 128 // n_dp
+        for d in range(2):
+            source, scatter, _, _ = parts_a[d]
+            lines = dot_tn(proj[d].astype(BF), dpre[d])[:rank]
+            extra = [jnp.sum(sums[d, i], axis=0, keepdims=True) for i in range(2)]
+            lines = jnp.concatenate(
+                [lines, dalog[d] * decay[d]] + extra + [jnp.zeros((STATE - 2, chans), F32)], axis=0
+            ).astype(BF)
+            for b in range(n_dp):
+                source[b] = lines[b * per_d : (b + 1) * per_d]
+            scatter.start()
+        c7.cross()
+        for i in late[:quarter]:
+            near[i][0].pair(near[i][1])
+        for _, scatter, _, _ in parts_a:
+            for k in range(n):
+                scatter.pair(k)
+        c7.back()
+        for i in late[quarter : 2 * quarter]:
+            near[i][0].pair(near[i][1])
+        c7.finish()
+
+        rows_x = chans // n_dp
+        for d in range(2):
+            dproj = c7.total[d].astype(BF)
+            source, scatter, _, _ = parts_x[d]
+            grad = dot_tn(act[d], dproj).astype(BF)
+            for b in range(n_dp):
+                source[b] = grad[b * rows_x : (b + 1) * rows_x]
+            scatter.start()
+
+            def act_rows(c, carry, d=d):
+                at = pl.ds(pl.multiple_of(c * 128, 128), 128)
+                shifted = pl.ds(pl.multiple_of(c * 128 + 16, 16), 128)
+                value = dot_nt(c7.total[d, at].astype(BF), xproj[d]) + dc[d, shifted]
+                dc[d, shifted] = value * slope[d, at].astype(F32)
+                return carry
+
+            lax.fori_loop(0, total // 128, act_rows, 0)
+
+        step = 32
+
+        def conv_rows(c, carry):
+            base = pl.multiple_of(c * step, step)
+            window = pl.ds(base, step + 32)
+            x_w = xpad[window, :].astype(F32)
+            grad = jnp.zeros((step, chans), F32)
+            for d in range(2):
+                d_w = dc[d, window]
+                here = d_w[16 : 16 + step]
+                conv_acc[5 * d + 4] += rows_in_eights(here)
+                for tap in range(4):
+                    off = tap - 3 if d == 0 else 3 - tap
+                    conv_acc[5 * d + tap] += rows_in_eights(here * x_w[16 + off : 16 + off + step])
+                    grad = grad + conv_w[d, tap : tap + 1] * d_w[16 - off : 16 - off + step]
+            dxin[pl.ds(base, step), :] = grad.astype(BF)
+            return carry
+
+        lax.fori_loop(0, total // step, conv_rows, 0)
+        for i in late[2 * quarter :]:
+            near[i][0].pair(near[i][1])
+
+        rb = width // (4 * n_dp)
+        half = n_dp // 2
+        for h in range(2):
+            cols = slice(h * width // 2, (h + 1) * width // 2)
+            grad = dot_tn(hidden[:, cols], dxin[...]).astype(BF)
+            for b in range(half):
+                for q in range(4):
+                    first = (4 * b + q) * rb
+                    xs_in[h * half + b, q] = grad[first : first + rb]
+        xs.start()
+        for _, scatter, buf, spread in parts_a:
+            buf[spread.place] = scatter.finish().astype(BF)
+            spread.go_z()
+        seg = tok.shape[0]
+        for h in range(2):
+            cols = slice(h * width // 2, (h + 1) * width // 2)
+            grad = (dot_nt(dxin[...], w_x[cols, :]) + dot_nt(grad_z[...], w_z[cols, :])).astype(BF)
+            for q in range(4):
+                hid_in[q, :, cols] = grad[q * seg : (q + 1) * seg]
+        seq2.start()
+        for _, scatter, _, _ in parts_x:
+            for k in range(n):
+                scatter.pair(k)
+        source, scatter, _, _ = part_c
+        conv_lines = [jnp.sum(conv_acc[i], axis=0, keepdims=True) for i in range(10)]
+        conv_lines = jnp.concatenate(conv_lines + [jnp.zeros((6, chans), F32)], axis=0)
+        for b in range(n_dp):
+            source[b, :, :rows_x] = conv_lines[:, b * rows_x : (b + 1) * rows_x].astype(BF)
+            source[b, :, rows_x:] = jnp.zeros((16, 128 - rows_x), BF)
+        scatter.start()
+        seq2.cross()
+        out_red[...] = outs.finish().astype(BF)
+        turn.start()
+        for _, _, _, spread in parts_a:
+            spread.go_y()
         z_red[...] = zs.finish().astype(BF)
-        swap.start()
-        swap.finish()
-        z_ref[...] = z_got[...]
-
-
-def scan_backward(proj, act, coef, a2, skip, dl, hp, dy, branch, out_part, z_part, collective_id):
+        for k in range(n):
+            part_c[1].pair(k)
+        for _, scatter, buf, spread in parts_x:
+            buf[spread.place] = scatter.finish().astype(BF)
+            spread.go_z()
+
+        grad = seq2.finish()
+        z_swap.start()
+        for _, _, _, spread in parts_a:
+            spread.go_x()
+        tokens = tok[...].astype(F32)
+        centred = tokens - jnp.mean(tokens, axis=1, keepdims=True)
+        inv_std = lax.rsqrt(jnp.mean(centred * centred, axis=1, keepdims=True) + epsilon)
+        normed = centred * inv_std
+        grad_normed = grad * (1.0 + scale[...])
+        inner_product = jnp.mean(grad_normed * normed, axis=1, keepdims=True)
+        tokg[...] = (
+            cot[...].astype(F32)
+            + inv_std
+            * (grad_normed - jnp.mean(grad_normed, axis=1, keepdims=True) - normed * inner_product)
+        ).astype(BF)
+        row[:, :width] = jnp.sum(grad, axis=0, keepdims=True)
+        row[:, width : 2 * width] = jnp.sum(grad * normed, axis=0, keepdims=True)
+        row[:, 2 * width : 3 * width] = gate_row[...]
+        row[:, 3 * width :] = jnp.sum(grad * flags[...], axis=0, keepdims=True)
+        pair = (row_sems.at[0], row_sems.at[1])
+        row_copies = [
+            remote(row, rows_in.at[k], pair, k, {"seq": other})
+            for k, other in enumerate(seq_others())
+        ]
+        for copy in row_copies:
+            copy.start()
+        source, scatter, buf, spread_c = part_c
+        buf[spread_c.place] = scatter.finish().astype(BF)
+        spread_c.go_z()
+        for k in range(n // 2):
+            xs.pair(k)
+        for copy in row_copies:
+            copy.wait()
+        table[d_index] = row[...] + rows_in[1] + (rows_in[0] + rows_in[2])
+        pair = (table_sems.at[0], table_sems.at[1])
+        table_copies = [
+            remote(table.at[d_index], table.at[d_index], pair, k, {"dp": other})
+            for k, other in enumerate(dp_others())
+        ]
+        for copy in table_copies:
+            copy.start()
+        spreads_x = [item[3] for item in parts_x] + [spread_c]
+        for spread in spreads_x:
+            spread.go_y()
+        for _, _, _, spread in parts_a:
+            spread.go_sib()
+        for k in range(n // 2, n - 1):
+            xs.pair(k)
+        for spread in spreads_x:
+            spread.go_x()
+        xs.pair(n - 1)
+        turn.finish()
+        out_ref[...] = out_got[...]
+        z_swap.finish()
+        for q in range(4):
+            in_ref[:, (4 + q) * chans : (5 + q) * chans] = z_got[q]
+        for spread in spreads_x:
+            spread.go_sib()
+        for (_, _, buf, spread), d in zip(parts_a, range(2)):
+            spread.finish()
+            for copy in results()[4 * d : 4 * d + 4]:
+                copy.start()
+        for copy in table_copies:
+            copy.wait()
+        table_ref[...] = table[...]
+        x_red[...] = xs.finish().astype(BF)
+        x_swap.start()
+        for spread in spreads_x:
+            spread.finish()
+        for copy in results()[8:]:
+            copy.start()
+        x_swap.finish()
+        for q in range(4):
+            in_ref[:, q * chans : (q + 1) * chans] = x_got[q]
+        for copy in results():
+            copy.wait()
+
+
+def scan_backward(
+    dl, hp, proj, act, coef, a2, skip, dy, dread, decay, conv_w, branch, out_part, z_part,
+    tok, cot, gate, scale, flags, slope, xin, hidden, grad_z, in_weight, xproj_weight, dtw, collective_id, tile,
+):
     total, chans = dy.shape
-    blocks = total // TILE
+    blocks = total // tile
     n_dp = out_part.shape[0]
-    _, rows, width = branch.shape
+    n = n_dp // 2
+    rows, width = tok.shape
+    rb = width // (4 * n_dp)
+    rows_x = chans // n_dp
+    per_d = 128 // n_dp
 
     def place(j):
         d = j // blocks
@@ -940,64 +1210,102 @@
         d, b = place(j)
         return d, b, 0
 
-    def direction_of(j):
-        return j // blocks, 0, 0
-
     def cells(j):
         d, b = place(j)
         return d, b, 0, 0
 
-    whole = VMEM_SPEC
-    in_specs = [
-        pl.BlockSpec((1, TILE, 128), tokens_of),
-        pl.BlockSpec((1, TILE, chans), tokens_of),
-        pl.BlockSpec((1, TILE // U, 2 * STATE, U), cells),
-        pl.BlockSpec((1, STATE, chans), direction_of),
-        pl.BlockSpec((1, 1, chans), direction_of),
-        pl.BlockSpec((1, TILE, chans), tokens_of),
-        pl.BlockSpec((1, TILE * STATE, chans), tokens_of),
-    ] + [whole] * 4
-    out_specs = [
-        pl.BlockSpec((1, TILE, chans), tokens_of),
-        pl.BlockSpec((1, TILE, chans), tokens_of),
-        pl.BlockSpec((1, 1, STATE, TILE), cells),
-        pl.BlockSpec((1, STATE, chans), direction_of),
-        pl.BlockSpec((1, 2, U, chans), lambda j: (j // blocks, 0, 0, 0)),
-    ] + [whole] * 3
+    any_spec = pl.BlockSpec(memory_space=pl.ANY)
+    in_specs = (
+        [
+            pl.BlockSpec((1, tile, chans), tokens_of),
+            pl.BlockSpec((1, tile * STATE, chans), tokens_of),
+        ]
+        + [VMEM_SPEC] * 2
+        + [pl.BlockSpec((1, tile // U, 2 * STATE, U), cells)]
+        + [VMEM_SPEC] * 11
+        + [any_spec] * 10
+    )
     shape = jax.ShapeDtypeStruct
+    in_out = (4, n, 2)
     out_shape = [
-        shape((2, total, chans), BF),
-        shape((2, total, chans), F32),
-        shape((2, blocks, STATE, TILE), F32),
-        shape((2, STATE, chans), F32),
-        shape((2, 2, U, chans), F32),
-        shape((rows, width), F32),
+        shape((rows, width), BF),
+        shape((rows, width), BF),
+        shape((rb, 8 * chans), BF),
         shape(out_part.shape[1:], BF),
-        shape(z_part.shape[1:], BF),
+        shape((2, n, 2, per_d, 4 * chans), BF),
+        shape(in_out + (rows_x, 128), BF),
+        shape(in_out + (rows_x, 128), BF),
+        shape(in_out + (16, 128), BF),
+        shape((n_dp, 1, 4 * width), F32),
+    ]
+    dma = pltpu.SemaphoreType.DMA
+    vmem = pltpu.VMEM
+    scratch = [
+        vmem((STATE, chans), F32),
+        vmem((U * STATE, chans), BF),
+        vmem((U * STATE, chans), BF),
+        vmem((U * 8, chans), BF),
+        vmem((U * 8, chans), BF),
+    ]
+    scratch += [vmem((U, chans), F32)] * 3 + [vmem((U, STATE, 128), F32)]
+    scratch += [
+        vmem((2, total, chans), BF),
+        vmem((2, total + 32, chans), F32),
+        vmem((2, blocks, STATE, tile), F32),
+        vmem((2, STATE, chans), F32),
+        vmem((2, 2, U, chans), F32),
+    ]
+    scratch += [
+        vmem(slope.shape, BF),
+        vmem((total + 32, chans), BF),
+        vmem(hidden.shape, BF),
+        vmem(grad_z.shape, BF),
+        vmem((width, chans), BF),
+        vmem((width, chans), BF),
+        vmem((2, chans, 128), BF),
+        vmem(dtw.shape, BF),
+        vmem((4, rows, width), BF),
+        vmem(out_part.shape, BF),
+        vmem(z_part.shape, BF),
+        dma((11,)),
+    ]
+    scratch += [
+        vmem((10, 8, chans), F32),
+        vmem((total, chans), BF),
+        vmem((1, width), F32),
+    ]
+    scratch += SeqScatter.scratch(rows, width)
+    scratch += DpScatter.scratch(n_dp, out_part.shape[1:]) + DpScatter.scratch(n_dp, z_part.shape[1:])
+    scratch += [vmem(out_part.shape[1:], BF)] * 2 + [dma((2, 1))]
+    scratch += [vmem(z_part.shape[1:], BF)] * 2 + [dma((2, 3))]
+    scratch += SeqReduce.scratch(total, 128)
+    for block in [(per_d, chans)] * 2 + [(rows_x, 128)] * 2 + [(16, 128)]:
+        scratch += [vmem((n_dp,) + block, BF)] + DpScatter.scratch(n_dp, block)
+        scratch += Spread.scratch(n_dp, block)
+    scratch += SeqScatter.scratch(rows, width)
+    scratch += DpScatter.scratch(n_dp, z_part.shape[1:])
+    scratch += [vmem(z_part.shape[1:], BF)] * 2 + [dma((2, 3))]
+    scratch += [
+        vmem((1, 4 * width), F32),
+        vmem((3, 1, 4 * width), F32),
+        dma((2, 3)),
+        vmem((n_dp, 1, 4 * width), F32),
+        dma((2, n_dp)),
+        dma((11,)),
     ]
     return pl.pallas_call(
         backward_kernel,
         grid=(2 * blocks,),
         in_specs=in_specs,
-        out_specs=out_specs,
+        out_specs=[VMEM_SPEC] * 4 + [any_spec] * 4 + [VMEM_SPEC],
         out_shape=out_shape,
-        scratch_shapes=[
-            pltpu.VMEM((STATE, chans), F32),
-            pltpu.VMEM((U * STATE, chans), BF),
-            pltpu.VMEM((U * STATE, chans), BF),
-            pltpu.VMEM((U * 8, chans), BF),
-            pltpu.VMEM((U * 8, chans), BF),
-        ]
-        + [pltpu.VMEM((U, chans), F32)] * 3
-        + [pltpu.VMEM((U, STATE, 128), F32)]
-        + SeqScatter.scratch(rows, width)
-        + DpScatter.scratch(n_dp, out_part.shape[1:])
-        + DpScatter.scratch(n_dp, z_part.shape[1:])
-        + [pltpu.VMEM(z_part.shape[1:], BF)] * 2
-        + [pltpu.SemaphoreType.DMA((2, 3))],
-        compiler_params=comm_params(collective_id, 60),
+        scratch_shapes=scratch,
+        compiler_params=comm_params(collective_id, 62),
         name="scan_backward",
-    )(proj, act, coef, a2, skip, dl, hp, dy, branch, out_part, z_part)
+    )(
+        dl, hp, proj, act, coef, a2, skip, dy, dread, decay, conv_w, tok, cot, gate, scale, flags,
+        slope, xin, hidden, grad_z, in_weight, xproj_weight, dtw, branch, out_part, z_part,
+    )
 
 
 def time_embedding(step_ids, model_width):
@@ -1058,12 +1366,6 @@
     cotangent_all = lax.all_gather(cotangent[0], "seq", axis=0, tiled=True)
     path = lax.all_gather(scan_path[0], "seq", axis=0, tiled=True)
 
-    def norm(values):
-        values = values.astype(F32)
-        centred = values - jnp.mean(values, axis=1, keepdims=True)
-        inv_std = lax.rsqrt(jnp.mean(centred * centred, axis=1, keepdims=True) + epsilon)
-        return centred * inv_std, inv_std
-
     def flags_of(item):
         return (jnp.remainder(item, grid_widths[0]) == grid_widths[0] - 1).astype(F32)[:, None]
 
@@ -1080,12 +1382,8 @@
         conv_bias,
         xproj_weight,
     )
-    w_x, w_z = mine(in_weight, 1), mine(in_weight, 1, inner)
     w_out = mine(out_weight, 0)
     conv_w = mine(conv_weight, 2)
-    padded = jnp.pad(xin, ((rim, rim), (0, 0))).astype(F32)
-    starts = [list(range(taps)), [2 * rim - tap for tap in range(taps)]]
-    xproj = mine(xproj_weight, 1)
     proj = seq_reduce(part, 1)
     dtw = jnp.pad(mine(dt_weight, 2), ((0, 0), (0, 128 - rank), (0, 0)))
     dtb = mine(dt_bias, 1)
@@ -1093,129 +1391,50 @@
     decay2 = decay * LOG2E
     skips = mine(skip, 1)
 
+    tile = 128 if n_dp <= 8 else 32
     coef = jnp.swapaxes(proj[:, :, 128 - 2 * STATE :].reshape(2, length // U, U, 2 * STATE), 2, 3)
     held, delta, dread, branch, out_part, z_part, grad_z = scan_forward(
         proj, act, coef, dtw, dtb[:, None], decay2, skips[:, None], dy, silu_z, slope_z, hidden,
-        grad_branch, w_out,
+        grad_branch, w_out, tile,
     )
     total = n_dp * n_seq
 
-    def product(left, right):
-        return lax.dot_general(
-            left, right, (((0,), (0,)), ((), ())), preferred_element_type=F32
-        ).astype(BF)
-
     def in_blocks(grad):
         return grad.reshape(n_dp, n_seq, width // total, chans)
 
-    dpre, dact, dflow, dalog, sums, branch, out_rows, in_z = scan_backward(
-        proj, act, coef, decay2, skips[:, None], delta, held, dy,
+    result, grad_tok, in_rows, out_rows, lines, x0, x1, conv_lines, table = scan_backward(
+        delta, held, proj, act, coef, decay2, skips[:, None], dy, dread, decay, conv_w,
         branch.reshape(n_seq, seg_len, width),
         out_part.reshape(n_dp, chans // n_dp, width),
         in_blocks(z_part),
-        2,
+        tokens[0], cotangent[0], gate_term, scale_term, flags_of(scan_path[0]),
+        slope, xin, hidden, grad_z, in_weight, xproj_weight, dtw, 2, tile,
     )
-    out_grad = lax.ppermute(
-        out_rows,
-        ("dp", "seq"),
-        [(d * n_seq + s, s * n_dp + d) for d in range(n_dp) for s in range(n_seq)],
-    ).astype(F32)
-    tok_float = tokens[0].astype(F32)
-    cot_float = cotangent[0].astype(F32)
-    result = (tok_float + gate_term * branch).astype(BF)
-    gate_grad = jnp.sum(cot_float * branch, axis=0, keepdims=True)
-
-    coef_grad = jnp.concatenate([dflow, dread], axis=2)
-    coef_grad = jnp.swapaxes(coef_grad, 2, 3).reshape(2, length, 2 * STATE)
-    partial = jnp.stack(
-        [
-            lax.dot_general(dpre[d], dtw[d], (((1,), (1,)), ((), ())), preferred_element_type=F32)
-            for d in range(2)
-        ]
-    ) + jnp.pad(coef_grad, ((0, 0), (0, 0), (128 - 2 * STATE, 0)))
-    dproj = seq_reduce(partial, 3).astype(BF)
-    dalog = dalog * decay
-    sums = jnp.sum(sums, axis=2)
-    grad_conv, small, xproj_grads = [], [], []
-    for d in range(2):
-        grad_act = (
-            lax.dot_general(dproj[d], xproj[d], (((1,), (1,)), ((), ())), preferred_element_type=F32)
-            + dact[d]
-        )
-        dconv = grad_act * slope[d]
-        grad_conv.append(dconv)
-        xproj_grads.append(
-            lax.dot_general(
-                dproj[d], act[d], (((0,), (0,)), ((), ())), preferred_element_type=F32
-            )
-        )
-        dtw_grad = lax.dot_general(
-            proj[d].astype(BF), dpre[d], (((0,), (0,)), ((), ())), preferred_element_type=F32
-        )[:rank]
-        conv_rows = jnp.stack(
-            [jnp.sum(dconv * padded[first : first + length], axis=0) for first in starts[d]]
-        )
-        vectors = jnp.concatenate([jnp.sum(dconv, axis=0)[None], sums[d]], axis=0)
-        small.append(jnp.concatenate([dtw_grad, dalog[d], conv_rows, vectors], axis=0))
-    dxin = 0.0
-    for d in range(2):
-        for tap in range(taps):
-            first = starts[d][tap]
-            dxin = dxin + jnp.pad(
-                conv_w[d, tap] * grad_conv[d], ((first, 2 * rim - first), (0, 0))
-            )
-    dxin = dxin[rim : rim + length].astype(BF)
-    grad_hidden = (
-        lax.dot_general(dxin, w_x, (((1,), (1,)), ((), ())), preferred_element_type=F32)
-        + lax.dot_general(grad_z, w_z, (((1,), (1,)), ((), ())), preferred_element_type=F32)
-    ).astype(BF)
-    rows = jnp.concatenate(
-        [xproj_grads[0], small[0], xproj_grads[1], small[1]], axis=0
-    )
-    n_rows = rows.shape[0]
-    rows = jnp.pad(rows.astype(BF), ((0, -n_rows % (16 * n_dp)), (0, 0)))
-    in_x, rows, grad_tok, table = last_exchange(
-        grad_hidden.reshape(n_seq, seg_len, width),
-        in_blocks(product(hidden, dxin)),
-        rows.reshape(n_dp, -1, chans),
-        tokens[0],
-        cotangent[0],
-        flags_of(scan_path[0]),
-        scale_term,
-        gate_grad,
-        4,
-    )
-    in_grad = jnp.concatenate([in_x, in_z], axis=0)
-    in_grad = jnp.swapaxes(in_grad, 0, 1).reshape(-1, 2 * inner).astype(F32)
     table = table.reshape(n_dp, -1)
     edge_grad = jnp.sum(table[:, 3 * width :], axis=0)
     mod_columns = lax.dynamic_slice_in_dim(table[:, : 3 * width], dp_index * columns, columns, 1)
     ada_b_grad = jnp.sum(mod_columns, axis=0)
     ada_w_grad = jnp.dot(embedded.astype(F32).T, mod_columns, precision=highest)
-
-    rows = jnp.transpose(rows, (2, 1, 3, 0, 4)).reshape(-1, inner)[:n_rows]
-    rows = rows.reshape(2, -1, inner).astype(F32)
-    cuts = [128, 128 + rank, 128 + rank + STATE, 128 + rank + STATE + taps]
-    xproj_grad = jnp.swapaxes(rows[:, : cuts[0]], 1, 2)
-    dtw_grad = rows[:, cuts[0] : cuts[1]]
-    alog_grad = jnp.swapaxes(rows[:, cuts[1] : cuts[2]], 1, 2)
-    convw_grad = rows[:, cuts[2] : cuts[3]]
-    last = cuts[3]
+    lines = lines.reshape(2, 128, inner).astype(F32)
+    alog_grad = jnp.swapaxes(lines[:, rank : rank + STATE], 1, 2)
+    xproj_grad = jnp.stack([item.reshape(inner, 128) for item in (x0, x1)]).astype(F32)
+    conv_lines = jnp.moveaxis(conv_lines[..., : chans // n_dp], 3, 0).reshape(16, inner).astype(F32)
+    conv_lines = conv_lines[: 2 * (taps + 1)].reshape(2, taps + 1, inner)
     return (
         result[None],
         grad_tok[None],
         ada_w_grad,
         ada_b_grad,
         edge_grad,
-        in_grad,
-        convw_grad,
-        rows[:, last],
+        in_rows.astype(F32),
+        conv_lines[:, :taps],
+        conv_lines[:, taps],
         xproj_grad,
-        dtw_grad,
-        rows[:, last + 1],
+        lines[:, :rank],
+        lines[:, rank + STATE],
         alog_grad,
-        rows[:, last + 2],
-        out_grad,
+        lines[:, rank + STATE + 1],
+        out_rows.astype(F32),
     )
 
 

time: 401 us -> 297 us (0.74); the launches traced: 397 us -> 297 us
  Pallas kernels: 274 us -> 239 us
  local copies, waits for them, and re-layouts: 50.3 us -> 21.1 us
  matrix products: 27.1 us -> 4.82 us
  waiting for transfers between devices: 8.18 us -> 0.68 us
  other arithmetic: 14.5 us -> 10.4 us
    pallas_call x1 -> x0, Pallas kernels: 91.1 us -> none  [last_exchange(): pl.pallas_call(last_kernel, out_shape=shapes, in_specs=[VMEM_SPEC] * 8, o...]
    pallas_call x1, Pallas kernels: 77.4 us -> 150 us  [scan_backward(): pl.pallas_call(backward_kernel, grid=(2 * blocks,), in_specs=in_specs, ou...]
    dot_general x11 -> x0, matrix products: 22.3 us -> none  [the longest x2 9 us: shards(): lax.dot_general(dproj[d], xproj[d], (((1,), (1,)), ((), ())), preferred_e...]
    pallas_call x2 -> x1, Pallas kernels: 22.6 us -> 11.3 us  [seq_reduce(): pl.pallas_call(reduce_kernel, out_shape=jax.ShapeDtypeStruct(x.shape, F32...]
    transpose x4 -> x1, local copies, waits for them, and re-layouts: 10.2 us -> 0.77 us  [shards(): alog_grad = jnp.swapaxes(lines[:, rank:rank + STATE], 1, 2)]
    unnamed x67 -> x40, local copies, waits for them, and re-layouts: 14.5 us -> 5.67 us
    ppermute x1 -> x0, waiting for transfers between devices: 7.5 us -> none  [shards(): lax.ppermute(out_rows, ('dp', 'seq'), [(d * n_seq + s, s * n_dp + d) for...]
    convert_element_type x2 -> x1, local copies, waits for them, and re-layouts: 7.04 us -> 0.01 us  [shards(): jnp.moveaxis(conv_lines[..., :chans // n_dp], 3, 0).reshape(16, inner)]
  transfers between devices with their start and end apart: 2 -> 1, of which waited for: 1 -> 0; matrix products, arithmetic and copies ran while one was open for 5% -> 5% of each run, Pallas kernels for 5% -> 7%
where the time goes in v1:
time: 297 us
  Pallas kernels  239 us (80%)
  local copies, waits for them, and re-layouts  21.1 us (7%)
  between operations  15 us (5%)
  other arithmetic  10.4 us (4%)
  blocking collectives  5.65 us (2%)
  matrix products  4.82 us (2%)
    pallas_call x1, Pallas kernels, scan_backward(): pl.pallas_call(backward_kernel, grid=(2 * blocks,), in_specs=in_specs, ou...  150 us
    pallas_call x1, Pallas kernels, scan_forward(): pl.pallas_call(forward_kernel, grid=(2 * blocks,), in_specs=in_specs, out...  38 us
    pallas_call x1, Pallas kernels, gather_tokens(): pl.pallas_call(functools.partial(gather_kernel, n_dp), out_shape=[jax.Sha...  21.1 us
    pallas_call x1, Pallas kernels, prepare(): pl.pallas_call(pre_kernel, grid_spec=pltpu.PrefetchScalarGridSpec(num_sca...  18.9 us
    pallas_call x1, Pallas kernels, seq_reduce(): pl.pallas_call(reduce_kernel, out_shape=jax.ShapeDtypeStruct(x.shape, F32...  11.3 us
    dynamic_slice x4, local copies, waits for them, and re-layouts, mine(): lax.dynamic_slice_in_dim(weight, first + seq_index * chans, chans, dim)  6.26 us
  transfers between devices with their start and end apart: 1, of which 0 were waited for; matrix products, arithmetic and copies ran while one was open for 5% of the time, Pallas kernels for 7%

profile of v1, /device:TPU:11, one launch (start us, length us, event | category | flops | bytes accessed | tf_op | source)
XLA Modules:
  0.0 296.9 jit_solution(4749948378824281018)
XLA Ops:
  7.3 0.7 all-gather.4.cloned.1.call-update
  8.6 5.6 %all-gather.1 = s32[1,512]{1,0:T(1,128)S(1)} all-gather(s32[1,128]{1,0:T(1,128)} %param.21), channel_id=3, replica_groups=mesh['dp'=8,'seq'=4] {'seq'}, dimensions={1}, use_global_device_ids=true | all-gather | bytes 2560 | tf_op jit(solution)/shard_map/all_gather | solution.py:1367
  14.3 0.2 broadcast_remainder_fusion
  14.5 0.9 copy.45.flags
  15.3 0.7 convert_element_type.40
  16.0 0.2 multiply_cosine_fusion
  16.2 1.2 convolution_add_fusion
  17.5 21.1 %gather_tokens.1 = (bf16[4,128,1536]{2,1,0:T(8,128)(2,1)S(1)}, f32[8,1,576]{2,1,0:T(1,128)S(1)}) custom-call(bf16[128,1536]{1,0:T(8,128)(2,1)S(1)} %bitcast.46, f32[8,1,576]{2,1,0:T(1,128)S(1)} %broadcast_in_dim.32.mod_ref), custom_call_target="tpu_custom_call" | custom-call | tf_op jit(solution)/shard_map/gather_tokens/pallas_call | solution.py:547
  38.6 1.1 copy-done.4
  39.8 0.1 reshape.106.mod
  39.9 0.6 broadcast_in_dim.35.edge
  40.5 0.7 constant_dynamic-slice_fusion.2
  41.2 0.6 broadcast_in_dim.37.skip.refs_6_
  41.8 0.6 broadcast_in_dim.36.dtb
  42.4 0.1 remainder_bitcast_fusion
  42.5 0.1 copy.47
  42.6 1.0 constant_dynamic-slice_fusion.4
  43.6 0.8 pad.4.dtw.refs_22_
  44.4 1.3 constant_dynamic-slice_fusion.refs_10_
  45.7 1.6 broadcast_multiply_fusion
  47.3 0.6 fusion.1.refs_15_
  48.0 3.2 %constant_dynamic-slice_fusion.1.w_out = bf16[768,1536]{1,0:T(8,128)(2,1)} fusion(bf16[3072,1536]{1,0:T(8,128)(2,1)} %w_out.1, s32[]{:T(128)S(6)} %select_n.35), kind=kLoop, calls=%fused_computation.29 | loop fusion | bytes 4718596 | tf_op jit(solution)/shard_map/dynamic_slice | solution.py:1356
  51.2 0.6 fusion.8
  51.8 18.9 %prepare.1 = (bf16[512,1536]{1,0:T(8,128)(2,1)}, bf16[512,1536]{1,0:T(8,128)(2,1)}, bf16[512,768]{1,0:T(8,128)(2,1)}, f32[512,768]{1,0:T(8,128)}, f32[512,768]{1...) custom-call(s32[1]{0:T(128)} %bitcast.s_ref, ...), custom_call_target="tpu_custom_call" | custom-call | tf_op jit(solution)/shard_map/prepare/pallas_call | solution.py:467
  70.7 1.0 copy-done.5
  71.7 11.3 %seq_reduce.1.proj.refs_2_ = f32[2,512,128]{2,1,0:T(8,128)S(1)} custom-call(f32[2,512,128]{2,1,0:T(8,128)S(1)} %copy-done.5), custom_call_target="tpu_custom_call" | custom-call | tf_op jit(solution)/shard_map/seq_reduce/pallas_call | solution.py:583
  83.0 0.2 slice.41
  83.2 1.3 copy.46
  84.6 38.0 %scan_forward.1 = (bf16[2,8192,768]{2,1,0:T(8,128)(2,1)}, f32[2,512,768]{2,1,0:T(8,128)}, f32[2,4,16,128]{3,2,1,0:T(8,128)}, bf16[512,1536]{1,0:T(8,128)(2,1)}, ...) custom-call(f32[2,512,128]{2,1,0:T(8,128)} %copy-done.2, ...), custom_call_target="tpu_custom_call" | custom-call | tf_op jit(solution)/shard_map/scan_forward/pallas_call | solution.py:351
  122.6 150.0 %scan_backward.1 = (bf16[128,1536]{1,0:T(8,128)(2,1)}, bf16[128,1536]{1,0:T(8,128)(2,1)}, bf16[48,6144]{1,0:T(8,128)(2,1)}, bf16[96,1536]{1,0:T(8,128)(2,1)}, bf...) custom-call(f32[2,512,768]{2,1,0:T(8,128)} %get-tuple-element.50.ref, ...), custom_call_target="tpu_custom_call" | custom-call | tf_op jit(solution)/shard_map/scan_backward/pallas_call | solution.py:1296
  272.6 1.8 bitcast_convert_fusion
  274.4 1.6 slice.61
  275.9 0.8 slice_bitcast_fusion
  276.8 0.1 copy.53
  276.9 0.2 reshape.116
  277.1 0.7 slice.59
  277.8 0.1 copy.74
  277.9 3.6 %fusion.2 = f32[1536,576]{0,1:T(8,128)} fusion(f32[8,4608]{1,0:T(8,128)S(1)} %slice.56, s32[]{:T(128)S(6)} %select_n.37, f32[8,768]{1,0:T(8,128)S(1)} %get-tuple-element.89, f32[8,768]{1,0:T(8,128)S(1)} %get-tuple-element.88), kind=kOutput, calls=%fused_computation.21 | convolution fusion | flops 85008384 | bytes 3608580 | tf_op jit(solution)/shard_map/dot_general | solution.py:1417
  281.5 0.7 dynamic-slice_reduce_fusion
  282.2 0.6 slice_reduce_fusion
  282.8 0.6 copy.75
  283.4 0.6 copy.76
  284.1 1.1 convert_element_type.43
  285.2 0.6 copy.77
  285.8 0.9 convert_element_type.48
  286.7 1.9 maximum_convert_fusion
  288.5 0.7 copy.81
  289.3 0.7 copy.82
  (43 shorter events, 0.3 us)
Async XLA Ops:
  7.2 9.0 %copy-start = (bf16[1536,576]{0,1:T(8,128)(2,1)S(1)}, bf16[1536,576]{0,1:T(8,128)(2,1)}, u32[]{:S(2)}) copy-start(bf16[1536,576]{0,1:T(8,128)(2,1)} %param.22) | copy-start | bytes 5308420
  7.2 35.2 %copy-start.16 = (s32[1,128]{1,0:T(1,128)S(1)}, s32[1,128]{1,0:T(1,128)}, u32[]{:S(2)}) copy-start(s32[1,128]{1,0:T(1,128)} %param.21) | copy-start | bytes 1540
  7.2 10.3 %copy-start.3 = (bf16[1,128,1536]{2,1,0:T(8,128)(2,1)S(1)}, bf16[1,128,1536]{2,1,0:T(8,128)(2,1)}, u32[]{:S(2)}) copy-start(bf16[1,128,1536]{2,1,0:T(8,128)(2,1)} %param.17) | copy-start | bytes 1179652
  7.2 32.6 %copy-start.15 = (f32[1536]{0:T(1024)S(1)}, f32[1536]{0:T(1024)}, u32[]{:S(2)}) copy-start(f32[1536]{0:T(1024)} %param.24) | copy-start | bytes 18436
  7.2 44.6 %all-gather.4.cloned.1.call-start = ((), (), s32[]{:S(2)}) async-start(), calls=%async_computation | async-start | bytes 1966080 | tf_op jit(solution)/shard_map/all_gather | solution.py:1366
  38.6 1.1 copy-start.4
  39.9 11.3 %copy-start.13 = (f32[1,4608]{1,0:T(1,128)}, f32[1,4608]{1,0:T(1,128)S(1)}, u32[]{:S(2)}) copy-start(f32[1,4608]{1,0:T(1,128)S(1)} %reshape.106.mod) | copy-start | bytes 55300
  70.6 1.0 copy-start.5
  83.0 1.6 copy-start.2
  274.4 2.4 copy-start.14
  275.9 1.9 copy-start.12
  277.9 6.1 %copy-start.8 = (bf16[48,6144]{1,0:T(8,128)(2,1)S(1)}, bf16[48,6144]{1,0:T(8,128)(2,1)}, u32[]{:S(2)}) copy-start(bf16[48,6144]{1,0:T(8,128)(2,1)} %get-tuple-element.62) | copy-start | bytes 1769476
  281.5 4.3 %copy-start.11 = (bf16[96,1536]{1,0:T(8,128)(2,1)S(1)}, bf16[96,1536]{1,0:T(8,128)(2,1)}, u32[]{:S(2)}) copy-start(bf16[96,1536]{1,0:T(8,128)(2,1)} %get-tuple-element.67) | copy-start | bytes 884740
  281.5 5.1 %copy-start.6 = (bf16[4,4,2,96,128]{4,3,2,1,0:T(8,128)(2,1)S(1)}, bf16[4,4,2,96,128]{4,3,2,1,0:T(8,128)(2,1)}, u32[]{:S(2)}) copy-start(bf16[4,4,2,96,128]{4,3,2,1,0:T(8,128)(2,1)} %get-tuple-element.64) | copy-start | bytes 2359300
  281.5 5.1 %copy-start.7 = (bf16[4,4,2,96,128]{4,3,2,1,0:T(8,128)(2,1)S(1)}, bf16[4,4,2,96,128]{4,3,2,1,0:T(8,128)(2,1)}, u32[]{:S(2)}) copy-start(bf16[4,4,2,96,128]{4,3,2,1,0:T(8,128)(2,1)} %get-tuple-element.65) | copy-start | bytes 2359300
  286.6 1.9 copy-start.10
  286.7 2.6 copy-start.9
  286.7 3.4 %copy-start.1 = (bf16[1536,576]{0,1:T(8,128)(2,1)S(1)}, bf16[1536,576]{0,1:T(8,128)(2,1)}, u32[]{:S(2)}) copy-start(bf16[1536,576]{0,1:T(8,128)(2,1)} %param.22) | copy-start | bytes 5308420
Sparse Core Ops, SparseCore 0:
  9.6 26.2 all-gather.3

commit v2 on v1

--- a/solution.py
+++ b/solution.py
@@ -242,7 +242,7 @@
 
 
 def forward_kernel(
-    proj, act, coef, dtw, dtb, a2, skip, dy, silu_z, slope_z, hidden, grad_branch, w_out,
+    s_ref, proj, act, coef, dtw, dtb, a2, skip, dy, silu_z, slope_z, hidden, grad_branch, w_out,
     hp, dl, dread, branch, out_part, z_part, grad_z,
     y, h_sc, hb_sc, h_a, h_b, r0, r1, r2, red, gated,
 ):
@@ -255,15 +255,15 @@
         h_sc[...] = jnp.zeros_like(h_sc)
         hb_sc[...] = jnp.zeros_like(hb_sc)
 
-    pre = dot(proj[0].astype(BF), dtw[0]) + dtb[0]
-    dl[0] = softplus(pre)
-
     def run(rev):
+        own = slice(int(rev), int(rev) + 1)
+        pre = dot(proj[0][:, : dtw.shape[1]].astype(BF), dtw[0]) + dtb[own]
+        dl[0] = softplus(pre)
         base = (2 * blocks - 1 - j if rev else j) * length
         dy_block = dy.at[pl.ds(pl.multiple_of(base, length), length)]
 
         def put_y(at, col, value):
-            value = value + skip[0, :, col] * act[0, at, col].astype(F32)
+            value = value + skip[own, col] * act[0, at, col].astype(F32)
             rows = pl.ds(pl.multiple_of(base + at.start, U), U)
             if rev:
                 value = value + y[rows, col]
@@ -303,7 +303,9 @@
             z_part[at, :] = dot_tn(hidden[:, at], grad_z[...]).astype(BF)
 
 
-def scan_forward(proj, act, coef, dtw, dtb, a2, skip, dy, silu_z, slope_z, hidden, grad_branch, w_out, tile):
+def scan_forward(
+    seq_index, proj, act, coef, dtw, dtb, a2, skip, dy, silu_z, slope_z, hidden, grad_branch, w_out, tile
+):
     total, chans = dy.shape
     width = w_out.shape[1]
     blocks = total // tile
@@ -313,14 +315,17 @@
         b = lax.rem(j, blocks)
         return d, b + d * (blocks - 1 - 2 * b)
 
-    def tokens_of(j):
+    def tokens_of(j, s):
         d, b = place(j)
         return d, b, 0
 
-    def direction_of(j):
+    def direction_of(j, s):
         return j // blocks, 0, 0
 
-    def cells(j):
+    def channels_of(j, s):
+        return j // blocks, 0, s[0]
+
+    def cells(j, s):
         d, b = place(j)
         return d, b, 0, 0
 
@@ -329,11 +334,12 @@
         pl.BlockSpec((1, tile, 128), tokens_of),
         pl.BlockSpec((1, tile, chans), tokens_of),
         pl.BlockSpec((1, tile // U, 2 * STATE, U), cells),
-        pl.BlockSpec((1, 128, chans), direction_of),
-        pl.BlockSpec((1, 1, chans), direction_of),
+        pl.BlockSpec((1, dtw.shape[1], chans), channels_of),
+        pl.BlockSpec((2, chans), lambda j, s: (0, s[0])),
         pl.BlockSpec((1, STATE, chans), direction_of),
-        pl.BlockSpec((1, 1, chans), direction_of),
-    ] + [whole] * 6
+        pl.BlockSpec((2, chans), lambda j, s: (0, s[0])),
+    ] + [whole] * 5
+    in_specs += [pl.BlockSpec((chans, width), lambda j, s: (s[0], 0))]
     out_specs = [
         pl.BlockSpec((1, tile * STATE, chans), tokens_of),
         pl.BlockSpec((1, tile, chans), tokens_of),
@@ -350,133 +356,25 @@
     ]
     return pl.pallas_call(
         forward_kernel,
-        grid=(2 * blocks,),
-        in_specs=in_specs,
-        out_specs=out_specs,
-        out_shape=out_shape,
-        scratch_shapes=[
-            pltpu.VMEM((total, chans), F32),
-            pltpu.VMEM((STATE, chans), F32),
-            pltpu.VMEM((STATE, chans), BF),
-            pltpu.VMEM((U * STATE, chans), BF),
-            pltpu.VMEM((U * STATE, chans), BF),
-        ]
-        + [pltpu.VMEM((U, chans), F32)] * 3
-        + [pltpu.VMEM((U, STATE, 128), F32), pltpu.VMEM((total, chans), BF)],
-        compiler_params=pltpu.CompilerParams(vmem_limit_bytes=60 << 20),
-        name="scan_forward",
-    )(proj, act, coef, dtw, dtb, a2, skip, dy, silu_z, slope_z, hidden, grad_branch, w_out)
-
-
-def pre_kernel(
-    s_ref, tok, cot, mod, flags, edge, w_x, w_z, w_out, conv_w, conv_b, xproj,
-    hidden, grad_branch, xin, dy, silu_z, slope_z, act, slope, part, pad,
-):
-    j = pl.program_id(0)
-    rows, width = tok.shape
-    total, chans = xin.shape
-    at = pl.ds(pl.multiple_of(j * rows, rows), rows)
-    shift, scale, gate = (mod[:, k * width : (k + 1) * width] for k in range(3))
-    tokens = tok[...].astype(F32)
-    centred = tokens - jnp.mean(tokens, axis=1, keepdims=True)
-    normed = centred * lax.rsqrt(jnp.mean(centred * centred, axis=1, keepdims=True) + epsilon)
-    hid = (normed * (1.0 + scale) + shift + flags[...] * edge[...]).astype(BF)
-    hidden[...] = hid
-    grad = (cot[...].astype(F32) * gate).astype(BF)
-    grad_branch[...] = grad
-    xin[at, :] = dot(hid, w_x[...]).astype(BF)
-    z = dot(hid, w_z[...])
-    sigma = jax.nn.sigmoid(z)
-    grad_gated = dot_nt(grad, w_out[...])
-    silu_z[...] = z * sigma
-    dy[...] = grad_gated * (z * sigma)
-    slope_z[...] = grad_gated * (sigma * (1.0 + z * (1.0 - sigma)))
-
-    @pl.when(j == pl.num_programs(0) - 1)
-    def _():
-        pad[:16, :] = jnp.zeros((16, chans), F32)
-        pad[total + 16 :, :] = jnp.zeros((16, chans), F32)
-        pad[16 : total + 16, :] = xin[...].astype(F32)
-        step = 64
-
-        def chunk(c, carry):
-            base = pl.multiple_of(c * step, step)
-            window = pad[pl.ds(base, step + 32), :]
-            here = pl.ds(base, step)
-            for d in range(2):
-                value = conv_b[d : d + 1, :]
-                for tap in range(4):
-                    first = 13 + tap if d == 0 else 19 - tap
-                    value = value + conv_w[d, tap : tap + 1, :] * window[first : first + step]
-                sig = jax.nn.sigmoid(value)
-                acted = (value * sig).astype(BF)
-                act[d, here, :] = acted
-                slope[d, here, :] = (sig * (1.0 + value * (1.0 - sig))).astype(BF)
-                part[d, here, :] = dot(acted, xproj[d])
-            return carry
-
-        lax.fori_loop(0, total // step, chunk, 0)
-
-
-def prepare(seq_index, tok, cot, mod, flags, edge, in_weight, out_weight, conv_w, conv_b, xproj):
-    total, width = tok.shape
-    inner = out_weight.shape[0]
-    chans = inner // 4
-    rows = 128
-
-    def by_rows(j, s):
-        return j, 0
-
-    def fixed(j, s):
-        return 0, 0
-
-    token_rows = pl.BlockSpec((rows, width), by_rows)
-    channel_rows = pl.BlockSpec((rows, chans), by_rows)
-    in_specs = [
-        token_rows,
-        token_rows,
-        pl.BlockSpec((1, 3 * width), fixed),
-        pl.BlockSpec((rows, 1), by_rows),
-        pl.BlockSpec((1, width), fixed),
-        pl.BlockSpec((width, chans), lambda j, s: (0, s[0])),
-        pl.BlockSpec((width, chans), lambda j, s: (0, 4 + s[0])),
-        pl.BlockSpec((chans, width), lambda j, s: (s[0], 0)),
-        pl.BlockSpec((2, 4, chans), lambda j, s: (0, 0, s[0])),
-        pl.BlockSpec((2, chans), lambda j, s: (0, s[0])),
-        pl.BlockSpec((2, chans, 128), lambda j, s: (0, s[0], 0)),
-    ]
-    out_specs = [token_rows, token_rows, pl.BlockSpec((total, chans), fixed)]
-    out_specs += [channel_rows] * 3
-    out_specs += [
-        pl.BlockSpec((2, total, chans), lambda j, s: (0, 0, 0)),
-        pl.BlockSpec((2, total, chans), lambda j, s: (0, 0, 0)),
-        pl.BlockSpec((2, total, 128), lambda j, s: (0, 0, 0)),
-    ]
-    shape = jax.ShapeDtypeStruct
-    out_shape = [
-        shape((total, width), BF),
-        shape((total, width), BF),
-        shape((total, chans), BF),
-        shape((total, chans), F32),
-        shape((total, chans), F32),
-        shape((total, chans), F32),
-        shape((2, total, chans), BF),
-        shape((2, total, chans), BF),
-        shape((2, total, 128), F32),
-    ]
-    return pl.pallas_call(
-        pre_kernel,
         grid_spec=pltpu.PrefetchScalarGridSpec(
             num_scalar_prefetch=1,
-            grid=(total // rows,),
+            grid=(2 * blocks,),
             in_specs=in_specs,
             out_specs=out_specs,
-            scratch_shapes=[pltpu.VMEM((total + 32, chans), F32)],
+            scratch_shapes=[
+                pltpu.VMEM((total, chans), F32),
+                pltpu.VMEM((STATE, chans), F32),
+                pltpu.VMEM((STATE, chans), BF),
+                pltpu.VMEM((U * STATE, chans), BF),
+                pltpu.VMEM((U * STATE, chans), BF),
+            ]
+            + [pltpu.VMEM((U, chans), F32)] * 3
+            + [pltpu.VMEM((U, STATE, 128), F32), pltpu.VMEM((total, chans), BF)],
         ),
         out_shape=out_shape,
         compiler_params=pltpu.CompilerParams(vmem_limit_bytes=60 << 20),
-        name="prepare",
-    )(seq_index, tok, cot, mod, flags, edge, in_weight, in_weight, out_weight, conv_w, conv_b, xproj)
+        name="scan_forward",
+    )(seq_index, proj, act, coef, dtw, dtb, a2, skip, dy, silu_z, slope_z, hidden, grad_branch, w_out)
 
 
 def sibling_of(s):
@@ -509,86 +407,6 @@
     return pltpu.CompilerParams(
         collective_id=collective_id, has_side_effects=True, vmem_limit_bytes=mib << 20
     )
-
-
-def gather_kernel(n_dp, tok_ref, mod_ref, all_ref, row_ref, send, recv, msend, mrecv, lsem):
-    d, s = lax.axis_index("dp"), lax.axis_index("seq")
-    sib, far = sibling_of(s), across_of(s)
-    others = [lax.rem(d + k, n_dp) for k in range(1, n_dp)]
-    greet([{"seq": sib}, {"seq": far}] + [{"dp": other} for other in others])
-    sems = (send, recv)
-    to_far = remote(tok_ref, all_ref.at[s], sems, 0, {"seq": far})
-    to_sib = remote(tok_ref, all_ref.at[s], sems, 1, {"seq": sib})
-    own = pltpu.make_async_copy(tok_ref, all_ref.at[s], lsem.at[0])
-    own_row = pltpu.make_async_copy(mod_ref.at[d], row_ref.at[d], lsem.at[1])
-    to_far.start()
-    rows = []
-    for k, other in enumerate(others):
-        copy = remote(mod_ref.at[other], row_ref.at[d], (msend, mrecv), k, {"dp": other})
-        copy.start()
-        rows.append(copy)
-    to_sib.start()
-    own.start()
-    own_row.start()
-    to_far.wait()
-    forward = remote(all_ref.at[far], all_ref.at[far], sems, 2, {"seq": sib})
-    forward.start()
-    for copy in rows:
-        copy.wait()
-    own.wait()
-    own_row.wait()
-    to_sib.wait()
-    forward.wait()
-
-
-def gather_tokens(tokens, mod_rows):
-    n_dp = mod_rows.shape[0]
-    dma = pltpu.SemaphoreType.DMA
-    return pl.pallas_call(
-        functools.partial(gather_kernel, n_dp),
-        out_shape=[
-            jax.ShapeDtypeStruct((4,) + tokens.shape, tokens.dtype),
-            jax.ShapeDtypeStruct(mod_rows.shape, mod_rows.dtype),
-        ],
-        in_specs=[VMEM_SPEC] * 2,
-        out_specs=[VMEM_SPEC] * 2,
-        scratch_shapes=[dma((3,)), dma((3,)), dma((n_dp,)), dma((n_dp,)), dma((2,))],
-        compiler_params=comm_params(0),
-        name="gather_tokens",
-    )(tokens, mod_rows)
-
-
-def reduce_kernel(x_ref, out_ref, from_sib, half, from_x, send, recv):
-    s = lax.axis_index("seq")
-    sib, far = sibling_of(s), across_of(s)
-    c = lax.rem(s, 2)
-    greet([{"seq": sib}, {"seq": far}])
-    sems = (send, recv)
-    first = remote(x_ref.at[1 - c], from_sib, sems, 0, {"seq": sib})
-    first.start()
-    first.wait()
-    half[...] = x_ref[c] + from_sib[...]
-    second = remote(half, from_x, sems, 1, {"seq": far})
-    second.start()
-    second.wait()
-    out_ref[c] = half[...] + from_x[...]
-    third = remote(out_ref.at[c], out_ref.at[c], sems, 2, {"seq": sib})
-    third.start()
-    third.wait()
-
-
-def seq_reduce(x, collective_id):
-    _, rows, width = x.shape
-    dma = pltpu.SemaphoreType.DMA
-    return pl.pallas_call(
-        reduce_kernel,
-        out_shape=jax.ShapeDtypeStruct(x.shape, F32),
-        in_specs=[VMEM_SPEC],
-        out_specs=VMEM_SPEC,
-        scratch_shapes=[pltpu.VMEM((rows, width), F32)] * 3 + [dma((3,)), dma((3,))],
-        compiler_params=comm_params(collective_id),
-        name="seq_reduce",
-    )(x)
 
 
 class DpScatter:
@@ -840,6 +658,247 @@
         pl.when(self.apart)(self.copy.wait)
 
 
+def first_kernel(*refs):
+    refs = list(refs)
+
+    def take(count):
+        taken = refs[:count]
+        del refs[:count]
+        return taken
+
+    tok, cot, flag, emb, ada_b, edge = take(6)
+    in_weight, out_weight, conv_weight, conv_bias, xproj_weight, ada_weight, a_log = take(7)
+    hidden_o, branch_o, xin_o, act_o, slope_o, proj_o, dy_o, silu_o, slope_z_o, mod_o, a2_o = take(11)
+    w_x, w_z, w_out, conv_w, conv_b, xproj, ada_w, rates, load_sems = take(9)
+    toks, cots, flags, rows_out, rows_in = take(5)
+    hidden, grad_branch, xin, z, act, slope, dy, silu_z, slope_z, pad = take(10)
+    tok_sems, cot_sems, flag_sems, row_sems, own_sems, store_sems = take(6)
+    c3 = SeqReduce(*take(6))
+    d, s = lax.axis_index("dp"), lax.axis_index("seq")
+    sib, far = sibling_of(s), across_of(s)
+    diag = across_of(sib)
+    n_dp = lax.axis_size("dp")
+    seg, width = tok.shape
+    total, chans = xin.shape
+
+    own = pl.ds(pl.multiple_of(s * chans, 128), chans)
+    own_z = pl.ds(pl.multiple_of((4 + s) * chans, 128), chans)
+    loads = [
+        (ada_weight, ada_w),
+        (a_log.at[:, :, own], rates),
+        (in_weight.at[:, own], w_x),
+        (in_weight.at[:, own_z], w_z),
+        (conv_weight.at[:, :, own], conv_w),
+        (conv_bias.at[:, own], conv_b),
+        (xproj_weight.at[:, own], xproj),
+        (out_weight.at[own], w_out),
+    ]
+    loads = [pltpu.make_async_copy(a, b, load_sems.at[i]) for i, (a, b) in enumerate(loads)]
+    for copy in loads:
+        copy.start()
+    greet_all()
+
+    def spread_out(src, dst, sems):
+        pair = (sems.at[0], sems.at[1])
+        to_far = remote(src, dst.at[s], pair, 0, {"seq": far})
+        to_sib = remote(src, dst.at[s], pair, 1, {"seq": sib})
+        forward = remote(dst.at[far], dst.at[far], pair, 2, {"seq": sib})
+        return to_far, to_sib, forward
+
+    tok_far, tok_sib, tok_forward = spread_out(tok, toks, tok_sems)
+    cot_far, cot_sib, cot_forward = spread_out(cot, cots, cot_sems)
+    tok_far.start()
+    tok_sib.start()
+    pair = (flag_sems.at[0], flag_sems.at[1])
+    flag_copies = [
+        remote(flag, flags.at[s], pair, k, {"seq": other}) for k, other in enumerate(seq_others())
+    ]
+    for copy in flag_copies:
+        copy.start()
+    locals_ = [(tok, toks.at[s]), (cot, cots.at[s]), (flag, flags.at[s])]
+    locals_ = [pltpu.make_async_copy(a, b, own_sems.at[i]) for i, (a, b) in enumerate(locals_)]
+    for copy in locals_:
+        copy.start()
+
+    loads[0].wait()
+    part = dot_nt(emb[...], ada_w[...]) + ada_b[...]
+    columns = part.shape[1]
+    for i in range(n_dp):
+        rows_out[i] = part[i : i + 1]
+    pair = (row_sems.at[0], row_sems.at[1])
+    row_copies = [
+        remote(rows_out.at[other], rows_in.at[d], pair, k, {"dp": other})
+        for k, other in enumerate(dp_others())
+    ]
+    for copy in row_copies:
+        copy.start()
+    cot_far.start()
+    cot_sib.start()
+    rows_in[d] = rows_out[d]
+    loads[1].wait()
+    for k in range(2):
+        a2_o[k] = -LOG2E * jnp.exp(rates[k])
+    for copy in row_copies:
+        copy.wait()
+    for i in range(n_dp):
+        mod_o[:, i * columns : (i + 1) * columns] = rows_in[i]
+    for copy in flag_copies:
+        copy.wait()
+    for copy in locals_:
+        copy.wait()
+    for copy in loads[2:4]:
+        copy.wait()
+
+    def project(block):
+        at = pl.ds(pl.multiple_of(block * seg, seg), seg)
+        tokens = toks[block].astype(F32)
+        centred = tokens - jnp.mean(tokens, axis=1, keepdims=True)
+        normed = centred * lax.rsqrt(jnp.mean(centred * centred, axis=1, keepdims=True) + epsilon)
+        marks = flags[block].T[:, :1]
+        hid = normed * (1.0 + mod_o[:, width : 2 * width]) + mod_o[:, :width] + marks * edge[...]
+        hid = hid.astype(BF)
+        hidden[at, :] = hid
+        xin[at, :] = dot(hid, w_x[...]).astype(BF)
+        z[at, :] = dot(hid, w_z[...])
+
+    project(s)
+    tok_sib.wait()
+    project(sib)
+    tok_far.wait()
+    tok_forward.start()
+    project(far)
+    tok_forward.wait()
+    project(diag)
+
+    stores = [
+        (hidden, hidden_o), (xin, xin_o), (act, act_o), (slope, slope_o), (c3.total, proj_o),
+        (grad_branch, branch_o), (dy, dy_o), (silu_z, silu_o), (slope_z, slope_z_o),
+    ]
+    stores = [pltpu.make_async_copy(a, b, store_sems.at[i]) for i, (a, b) in enumerate(stores)]
+    stores[0].start()
+    stores[1].start()
+    pad[:16, :] = jnp.zeros((16, chans), F32)
+    pad[total + 16 :, :] = jnp.zeros((16, chans), F32)
+    pad[16 : total + 16, :] = xin[...].astype(F32)
+    for copy in loads[4:]:
+        copy.wait()
+    step = 64
+
+    def chunk(c, carry):
+        base = pl.multiple_of(c * step, step)
+        window = pad[pl.ds(base, step + 32), :]
+        here = pl.ds(base, step)
+        for k in range(2):
+            value = conv_b[k : k + 1, :]
+            for tap in range(4):
+                first = 13 + tap if k == 0 else 19 - tap
+                value = value + conv_w[k, tap : tap + 1, :] * window[first : first + step]
+            sig = jax.nn.sigmoid(value)
+            acted = (value * sig).astype(BF)
+            act[k, here, :] = acted
+            slope[k, here, :] = (sig * (1.0 + value * (1.0 - sig))).astype(BF)
+            c3.x[k, here, :] = dot(acted, xproj[k])
+        return carry
+
+    lax.fori_loop(0, total // step, chunk, 0)
+    c3.start()
+    stores[2].start()
+    stores[3].start()
+
+    def gate_back(block):
+        at = pl.ds(pl.multiple_of(block * seg, seg), seg)
+        grad = (cots[block].astype(F32) * mod_o[:, 2 * width :]).astype(BF)
+        grad_branch[at, :] = grad
+        grad_gated = dot_nt(grad, w_out[...])
+        value = z[at, :]
+        sigma = jax.nn.sigmoid(value)
+        silu_z[at, :] = value * sigma
+        dy[at, :] = grad_gated * (value * sigma)
+        slope_z[at, :] = grad_gated * (sigma * (1.0 + value * (1.0 - sigma)))
+
+    cot_far.wait()
+    cot_forward.start()
+    gate_back(s)
+    c3.cross()
+    cot_sib.wait()
+    gate_back(sib)
+    gate_back(far)
+    cot_forward.wait()
+    gate_back(diag)
+    for copy in stores[5:]:
+        copy.start()
+    c3.back()
+    c3.finish()
+    stores[4].start()
+    for copy in stores:
+        copy.wait()
+
+
+def first_part(
+    tok, cot, flag, emb, ada_b, edge, in_weight, out_weight, conv_weight, conv_bias, xproj_weight,
+    ada_w, a_log, collective_id,
+):
+    seg, width = tok.shape
+    total = 4 * seg
+    chans = out_weight.shape[0] // 4
+    n_dp = emb.shape[0]
+    columns = ada_w.shape[0]
+    any_spec = pl.BlockSpec(memory_space=pl.ANY)
+    shape = jax.ShapeDtypeStruct
+    out_shape = [
+        shape((total, width), BF),
+        shape((total, width), BF),
+        shape((total, chans), BF),
+        shape((2, total, chans), BF),
+        shape((2, total, chans), BF),
+        shape((2, total, 128), F32),
+        shape((total, chans), F32),
+        shape((total, chans), F32),
+        shape((total, chans), F32),
+        shape((1, 3 * width), F32),
+        shape((2, STATE, chans), F32),
+    ]
+    dma = pltpu.SemaphoreType.DMA
+    vmem = pltpu.VMEM
+    scratch = [
+        vmem((width, chans), BF),
+        vmem((width, chans), BF),
+        vmem((chans, width), BF),
+        vmem((2, 4, chans), F32),
+        vmem((2, chans), F32),
+        vmem((2, chans, 128), BF),
+        vmem(ada_w.shape, BF),
+        vmem((2, STATE, chans), F32),
+        dma((8,)),
+        vmem((4, seg, width), BF),
+        vmem((4, seg, width), BF),
+        vmem((4, 8, 128), F32),
+        vmem((n_dp, 1, columns), F32),
+        vmem((n_dp, 1, columns), F32),
+        vmem((total, width), BF),
+        vmem((total, width), BF),
+        vmem((total, chans), BF),
+        vmem((total, chans), F32),
+        vmem((2, total, chans), BF),
+        vmem((2, total, chans), BF),
+    ]
+    scratch += [vmem((total, chans), F32)] * 3 + [vmem((total + 32, chans), F32)]
+    scratch += [dma((2, 3)), dma((2, 3)), dma((2, 3)), dma((2, n_dp)), dma((3,)), dma((9,))]
+    scratch += SeqReduce.scratch(total, 128)
+    return pl.pallas_call(
+        first_kernel,
+        in_specs=[VMEM_SPEC] * 6 + [any_spec] * 7,
+        out_specs=[any_spec] * 9 + [VMEM_SPEC] * 2,
+        out_shape=out_shape,
+        scratch_shapes=scratch,
+        compiler_params=comm_params(collective_id, 60),
+        name="first_part",
+    )(
+        tok, cot, flag, emb, ada_b, edge, in_weight, out_weight, conv_weight, conv_bias, xproj_weight,
+        ada_w, a_log,
+    )
+
+
 def rows_in_eights(x):
     total = x[:8]
     for k in range(1, x.shape[0] // 8):
@@ -855,18 +914,19 @@
         del refs[:count]
         return taken
 
-    (dl, hp, proj, act, coef, a2, skip, dy, dread, decay, conv_w) = take(11)
+    (dl, hp, proj, act, coef, a2, dy, dread) = take(8)
     (tok, cot, gate, scale, flags) = take(5)
-    far_inputs = take(10)
+    far_inputs = take(12)
+    dt_weight, conv_weight, skip_all = far_inputs[6:9]
     in_weight, xproj_weight = far_inputs[4:6]
     (result, tokg, in_ref, out_ref, a_ref, x0_ref, x1_ref, cv_ref, table_ref) = take(9)
     g_sc, g_a, g_b, q_a, q_b, r0, r1, r2, red = take(9)
     dpre, dc, dflow, dalog, sums = take(5)
-    slope, xpad, hidden, grad_z, w_x, w_z, xproj, dtw, hid_in, out_in, xs_in, local_sems = take(12)
+    slope, xpad, hidden, grad_z, w_x, w_z, xproj, dtw, conv_w, skip, hid_in, out_in, xs_in, local_sems = take(14)
     conv_acc, dxin, gate_row = take(3)
-    seq1 = SeqScatter(hid_in, *take(4), out=far_inputs[7])
-    outs = DpScatter(out_in, *take(4), out=far_inputs[8])
-    zs = DpScatter(xs_in, *take(4), out=far_inputs[9])
+    seq1 = SeqScatter(hid_in, *take(4), out=far_inputs[9])
+    outs = DpScatter(out_in, *take(4), out=far_inputs[10])
+    zs = DpScatter(xs_in, *take(4), out=far_inputs[11])
     out_red, out_got, turn_sems = take(3)
     turn = Turn(out_red, out_got, turn_sems)
     z_red, z_got, z_swap_sems = take(3)
@@ -906,10 +966,12 @@
             (in_weight.at[:, own], w_x),
             (in_weight.at[:, own_z], w_z),
             (xproj_weight.at[:, own], xproj),
-            (far_inputs[6], dtw),
-            (far_inputs[7], hid_in),
-            (far_inputs[8], out_in),
-            (far_inputs[9], xs_in),
+            (dt_weight.at[:, :, own], dtw.at[:, pl.ds(0, dt_weight.shape[1])]),
+            (conv_weight.at[:, :, own], conv_w),
+            (far_inputs[9], hid_in),
+            (far_inputs[10], out_in),
+            (far_inputs[11], xs_in),
+            (skip_all.at[:, own], skip),
         ]
         return [pltpu.make_async_copy(a, b, local_sems.at[i]) for i, (a, b) in enumerate(pairs)]
 
@@ -936,11 +998,13 @@
         seq1.start()
         for copy in loads():
             copy.start()
+        loads()[12].wait()
         for d in range(2):
             dc[d, :16, :] = jnp.zeros((16, chans), F32)
             dc[d, total + 16 :, :] = jnp.zeros((16, chans), F32)
         xpad[:16, :] = jnp.zeros((16, chans), BF)
         xpad[total + 16 :, :] = jnp.zeros((16, chans), BF)
+        dtw[:, dt_weight.shape[1] :, :] = jnp.zeros((2, 128 - dt_weight.shape[1], chans), BF)
         dalog[...] = jnp.zeros_like(dalog)
         sums[...] = jnp.zeros_like(sums)
         conv_acc[...] = jnp.zeros_like(conv_acc)
@@ -953,13 +1017,13 @@
 
     @pl.when(j == 2 * unit)
     def _():
-        loads()[8].wait()
+        loads()[9].wait()
         seq1.cross()
 
     @pl.when(j == 3 * unit)
     def _():
-        loads()[9].wait()
         loads()[10].wait()
+        loads()[11].wait()
 
 
     @pl.when(j == 5 * unit)
@@ -979,7 +1043,7 @@
         here = pl.ds(base, length)
         backward_block(
             rev, dl.at[0], act.at[d, here], coef.at[0], a2.at[d],
-            proj.at[d, here], dy.at[here], skip.at[d], hp.at[0], dpre.at[d, here],
+            proj.at[d, here], dy.at[here], skip.at[pl.ds(d, 1)], hp.at[0], dpre.at[d, here],
             dc.at[d, pl.ds(pl.multiple_of(base + 16, 16), length)], dflow.at[d, block], dalog.at[d],
             sums.at[d], g_sc, ((g_a, q_a), (g_b, q_b)), (r0, r1, r2), red,
         )
@@ -992,7 +1056,7 @@
         late = [i for i in range(2 * n) if step_of(start_at, i) >= 8]
         for i in late:
             near[i][0].near_copy(near[i][1]).start()
-        for copy in loads()[:8]:
+        for copy in loads()[:9]:
             copy.wait()
         for d in range(2):
             value = dot_nt(dpre[d], dtw[d])
@@ -1012,7 +1076,7 @@
             lines = dot_tn(proj[d].astype(BF), dpre[d])[:rank]
             extra = [jnp.sum(sums[d, i], axis=0, keepdims=True) for i in range(2)]
             lines = jnp.concatenate(
-                [lines, dalog[d] * decay[d]] + extra + [jnp.zeros((STATE - 2, chans), F32)], axis=0
+                [lines, dalog[d] * (a2[d] * LN2)] + extra + [jnp.zeros((STATE - 2, chans), F32)], axis=0
             ).astype(BF)
             for b in range(n_dp):
                 source[b] = lines[b * per_d : (b + 1) * per_d]
@@ -1189,8 +1253,9 @@
 
 
 def scan_backward(
-    dl, hp, proj, act, coef, a2, skip, dy, dread, decay, conv_w, branch, out_part, z_part,
-    tok, cot, gate, scale, flags, slope, xin, hidden, grad_z, in_weight, xproj_weight, dtw, collective_id, tile,
+    dl, hp, proj, act, coef, a2, dy, dread, branch, out_part, z_part,
+    tok, cot, gate, scale, flags, slope, xin, hidden, grad_z, in_weight, xproj_weight, dt_weight, conv_weight, skip,
+    collective_id, tile,
 ):
     total, chans = dy.shape
     blocks = total // tile
@@ -1222,8 +1287,8 @@
         ]
         + [VMEM_SPEC] * 2
         + [pl.BlockSpec((1, tile // U, 2 * STATE, U), cells)]
-        + [VMEM_SPEC] * 11
-        + [any_spec] * 10
+        + [VMEM_SPEC] * 8
+        + [any_spec] * 12
     )
     shape = jax.ShapeDtypeStruct
     in_out = (4, n, 2)
@@ -1263,11 +1328,13 @@
         vmem((width, chans), BF),
         vmem((width, chans), BF),
         vmem((2, chans, 128), BF),
-        vmem(dtw.shape, BF),
+        vmem((2, 128, chans), BF),
+        vmem((2, 4, chans), F32),
+        vmem((2, chans), F32),
         vmem((4, rows, width), BF),
         vmem(out_part.shape, BF),
         vmem(z_part.shape, BF),
-        dma((11,)),
+        dma((13,)),
     ]
     scratch += [
         vmem((10, 8, chans), F32),
@@ -1303,8 +1370,9 @@
         compiler_params=comm_params(collective_id, 62),
         name="scan_backward",
     )(
-        dl, hp, proj, act, coef, a2, skip, dy, dread, decay, conv_w, tok, cot, gate, scale, flags,
-        slope, xin, hidden, grad_z, in_weight, xproj_weight, dtw, branch, out_part, z_part,
+        dl, hp, proj, act, coef, a2, dy, dread, tok, cot, gate, scale, flags, slope, xin, hidden,
+        grad_z, in_weight, xproj_weight, dt_weight, conv_weight, skip, branch, out_part,
+        z_part,
     )
 
 
@@ -1352,50 +1420,23 @@
     length = seg_len * n_seq
     chans = inner // n_seq
 
-    def mine(weight, dim, first=0):
-        return lax.dynamic_slice_in_dim(weight, first + seq_index * chans, chans, dim)
+    def flags_of(item):
+        return (jnp.remainder(item, grid_widths[0]) == grid_widths[0] - 1).astype(F32)
 
     embedded = jax.nn.silu(time_embedding(timesteps, width)).astype(BF)
-    modulation_part = jnp.dot(embedded, ada_weight, preferred_element_type=F32) + ada_bias
-    gathered, modulation_own = gather_tokens(tokens[0], modulation_part[:, None, :])
-    tokens_all = gathered.reshape(length, width)
-    modulation_own = modulation_own.reshape(1, -1)
-    scale_term = modulation_own[:, width : 2 * width]
-    gate_term = modulation_own[:, 2 * width :]
-
-    cotangent_all = lax.all_gather(cotangent[0], "seq", axis=0, tiled=True)
-    path = lax.all_gather(scan_path[0], "seq", axis=0, tiled=True)
-
-    def flags_of(item):
-        return (jnp.remainder(item, grid_widths[0]) == grid_widths[0] - 1).astype(F32)[:, None]
-
-    hidden, grad_branch, xin, dy, silu_z, slope_z, act, slope, part = prepare(
-        seq_index.astype(jnp.int32)[None],
-        tokens_all,
-        cotangent_all,
-        modulation_own,
-        flags_of(path),
-        edge[None],
-        in_weight,
-        out_weight,
-        conv_weight,
-        conv_bias,
-        xproj_weight,
+    own_flags = flags_of(scan_path)
+    hidden, grad_branch, xin, act, slope, proj, dy, silu_z, slope_z, modulation, decay2 = first_part(
+        tokens[0], cotangent[0], jnp.broadcast_to(own_flags, (8, seg_len)), embedded, ada_bias[None],
+        edge[None], in_weight, out_weight, conv_weight, conv_bias, xproj_weight, ada_weight.T,
+        jnp.swapaxes(a_log, 1, 2), 0,
     )
-    w_out = mine(out_weight, 0)
-    conv_w = mine(conv_weight, 2)
-    proj = seq_reduce(part, 1)
-    dtw = jnp.pad(mine(dt_weight, 2), ((0, 0), (0, 128 - rank), (0, 0)))
-    dtb = mine(dt_bias, 1)
-    decay = -jnp.exp(jnp.swapaxes(mine(a_log, 1), 1, 2))
-    decay2 = decay * LOG2E
-    skips = mine(skip, 1)
-
+    scale_term = modulation[:, width : 2 * width]
+    gate_term = modulation[:, 2 * width :]
     tile = 128 if n_dp <= 8 else 32
     coef = jnp.swapaxes(proj[:, :, 128 - 2 * STATE :].reshape(2, length // U, U, 2 * STATE), 2, 3)
     held, delta, dread, branch, out_part, z_part, grad_z = scan_forward(
-        proj, act, coef, dtw, dtb[:, None], decay2, skips[:, None], dy, silu_z, slope_z, hidden,
-        grad_branch, w_out, tile,
+        seq_index.astype(jnp.int32)[None], proj, act, coef, dt_weight, dt_bias, decay2,
+        skip, dy, silu_z, slope_z, hidden, grad_branch, out_weight, tile,
     )
     total = n_dp * n_seq
 
@@ -1403,12 +1444,13 @@
         return grad.reshape(n_dp, n_seq, width // total, chans)
 
     result, grad_tok, in_rows, out_rows, lines, x0, x1, conv_lines, table = scan_backward(
-        delta, held, proj, act, coef, decay2, skips[:, None], dy, dread, decay, conv_w,
+        delta, held, proj, act, coef, decay2, dy, dread,
         branch.reshape(n_seq, seg_len, width),
         out_part.reshape(n_dp, chans // n_dp, width),
         in_blocks(z_part),
-        tokens[0], cotangent[0], gate_term, scale_term, flags_of(scan_path[0]),
-        slope, xin, hidden, grad_z, in_weight, xproj_weight, dtw, 2, tile,
+        tokens[0], cotangent[0], gate_term, scale_term, own_flags[0][:, None],
+        slope, xin, hidden, grad_z, in_weight, xproj_weight, dt_weight, conv_weight, skip,
+        2, tile,
     )
     table = table.reshape(n_dp, -1)
     edge_grad = jnp.sum(table[:, 3 * width :], axis=0)

time: 297 us -> 261 us (0.88)
  between operations: 15 us -> 1.43 us
  Pallas kernels: 239 us -> 231 us
  blocking collectives: 5.65 us -> 0 us
  local copies, waits for them, and re-layouts: 21.1 us -> 15.6 us
    pallas_call x4 -> x2, Pallas kernels: 89.2 us -> 76 us  [the longest x1 38.3 us: first_part(): pl.pallas_call(first_kernel, in_specs=[VMEM_SPEC] * 6 + [any_spec] * 7, o...]
    dynamic_slice x4 -> x0, local copies, waits for them, and re-layouts: 6.26 us -> none  [mine(): lax.dynamic_slice_in_dim(weight, first + seq_index * chans, chans, dim)]
    all_gather x1 -> x0, blocking collectives: 5.65 us -> none  [shards(): path = lax.all_gather(scan_path[0], 'seq', axis=0, tiled=True)]
    pallas_call x1, Pallas kernels: 150 us -> 155 us  [scan_backward(): pl.pallas_call(backward_kernel, grid=(2 * blocks,), in_specs=in_specs, ou...]
  transfers between devices with their start and end apart: 1 -> 0, of which waited for: 0 -> 0; matrix products, arithmetic and copies ran while one was open for 5% -> 0% of each run, Pallas kernels for 7% -> 0%
where the time goes in v2:
time: 261 us; the launch traced here: 260 us
  Pallas kernels  231 us (89%)
  local copies, waits for them, and re-layouts  15.6 us (6%)
  other arithmetic  8.64 us (3%)
  matrix products  3.57 us (1%)
    pallas_call x1, Pallas kernels, scan_backward(): pl.pallas_call(backward_kernel, grid=(2 * blocks,), in_specs=in_specs, ou...  155 us
    pallas_call x1, Pallas kernels, first_part(): pl.pallas_call(first_kernel, in_specs=[VMEM_SPEC] * 6 + [any_spec] * 7, o...  38.3 us
    pallas_call x1, Pallas kernels, scan_forward(): pl.pallas_call(forward_kernel, grid_spec=pltpu.PrefetchScalarGridSpec(num...  37.7 us

profile of v2, /device:TPU:11, one launch (start us, length us, event | category | flops | bytes accessed | tf_op | source)
XLA Modules:
  0.0 260.1 jit_solution(13283229371965415243)
XLA Ops:
  1.3 0.7 convert_element_type.31
  2.0 0.8 fusion.6
  2.7 0.8 fusion.7
  3.5 1.3 broadcast_in_dim.27.refs_4_
  4.8 0.6 broadcast_in_dim.26.refs_2_
  5.4 1.3 broadcast_in_dim.28.refs_5_
  6.7 0.2 multiply_cosine_fusion
  6.9 0.6 multiply_convert_fusion.refs_3_
  7.5 0.7 copy.35.refs_12_
  8.2 38.3 %first_part.1 = (bf16[512,1536]{1,0:T(8,128)(2,1)}, bf16[512,1536]{1,0:T(8,128)(2,1)}, bf16[512,768]{1,0:T(8,128)(2,1)}, bf16[2,512,768]{2,1,0:T(8,128)(2,1)}, b...) custom-call(bf16[128,1536]{1,0:T(8,128)(2,1)} %bitcast.46, ...), custom_call_target="tpu_custom_call" | custom-call | tf_op jit(solution)/shard_map/first_part/pallas_call | solution.py:888
  46.6 1.3 fusion.4
  47.9 1.2 slice.41
  49.1 1.3 copy.34
  50.5 37.7 %scan_forward.1 = (bf16[2,8192,768]{2,1,0:T(8,128)(2,1)}, f32[2,512,768]{2,1,0:T(8,128)}, f32[2,4,16,128]{3,2,1,0:T(8,128)}, bf16[512,1536]{1,0:T(8,128)(2,1)}, ...) custom-call(s32[1]{0:T(128)} %bitcast.s_ref, ...), custom_call_target="tpu_custom_call" | custom-call | tf_op jit(solution)/shard_map/scan_forward/pallas_call | solution.py:357
  88.2 154.9 %scan_backward.1 = (bf16[128,1536]{1,0:T(8,128)(2,1)}, bf16[128,1536]{1,0:T(8,128)(2,1)}, bf16[48,6144]{1,0:T(8,128)(2,1)}, bf16[96,1536]{1,0:T(8,128)(2,1)}, bf...) custom-call(f32[2,512,768]{2,1,0:T(8,128)} %get-tuple-element.49.ref, ...), custom_call_target="tpu_custom_call" | custom-call | tf_op jit(solution)/shard_map/scan_backward/pallas_call | solution.py:1363
  243.1 0.0 copy-start.8
  243.1 0.0 copy-start.6
  243.1 0.0 copy-start.3
  243.1 1.0 slice_bitcast_fusion.1
  244.1 0.1 copy.36
  244.2 0.2 reshape.70
  244.5 0.7 slice.57
  245.2 0.0 copy-start
  245.2 0.6 copy.47
  245.8 0.0 copy-done.8
  245.8 0.1 copy.46
  245.9 0.6 slice_reduce_fusion
  246.5 0.7 dynamic-slice_reduce_fusion
  247.2 0.0 copy-done.6
  247.2 0.9 convert_element_type.38
  248.0 0.0 copy-done.3
  248.0 1.1 convert_element_type.33
  249.1 0.0 copy-done
  249.1 0.5 bitcast_convert_fusion
  249.6 0.6 copy_bitcast_fusion.1
  250.3 0.8 slice_bitcast_fusion
  251.1 0.0 copy-start.2
  251.1 1.6 slice.59
  252.6 0.0 copy-done.1
  252.6 0.5 copy-done.2
  253.2 0.0 copy-start.7
  253.2 1.9 maximum_convert_fusion
  255.0 0.0 copy-done.7
  255.0 3.6 %fusion = f32[1536,576]{0,1:T(8,128)} fusion(bf16[8,1536]{1,0:T(8,128)(2,1)S(1)} %copy-done.7, f32[8,4608]{1,0:T(8,128)S(1)} %slice.54, s32[]{:T(128)S(6)} %select_n.14), kind=kOutput, calls=%fused_computation.15 | convolution fusion | flops 84934656 | bytes 3584004 | tf_op jit(solution)/shard_map/dot_general | solution.py:1459
  258.6 0.0 copy-done.5
  258.6 0.7 copy.51
  259.4 0.0 copy-done.4
  259.4 0.7 copy.52
  (8 shorter events, 0.1 us)
Async XLA Ops:
  243.1 2.7 %copy-start.8 = (f32[8,1,6144]{2,1,0:T(1,128)S(1)}, f32[8,1,6144]{2,1,0:T(1,128)}, u32[]{:S(2)}) copy-start(f32[8,1,6144]{2,1,0:T(1,128)} %get-tuple-element.61) | copy-start | bytes 589828
  243.1 4.1 %copy-start.6 = (bf16[96,1536]{1,0:T(8,128)(2,1)S(1)}, bf16[96,1536]{1,0:T(8,128)(2,1)}, u32[]{:S(2)}) copy-start(bf16[96,1536]{1,0:T(8,128)(2,1)} %get-tuple-element.67) | copy-start | bytes 884740
  243.1 4.9 %copy-start.3 = (bf16[48,6144]{1,0:T(8,128)(2,1)S(1)}, bf16[48,6144]{1,0:T(8,128)(2,1)}, u32[]{:S(2)}) copy-start(bf16[48,6144]{1,0:T(8,128)(2,1)} %get-tuple-element.62) | copy-start | bytes 1769476
  245.2 4.0 %copy-start = (bf16[2,4,2,16,3072]{4,3,2,1,0:T(8,128)(2,1)S(1)}, bf16[2,4,2,16,3072]{4,3,2,1,0:T(8,128)(2,1)}, u32[]{:S(2)}) copy-start(bf16[2,4,2,16,3072]{4,3,2,1,0:T(8,128)(2,1)} %get-tuple-element.66) | copy-start | bytes 4718596
  251.1 1.6 copy-start.1
  251.1 2.1 copy-start.2
  253.2 1.9 copy-start.7
  255.0 3.6 %copy-start.5 = (bf16[128,1536]{1,0:T(8,128)(2,1)S(1)}, bf16[128,1536]{1,0:T(8,128)(2,1)}, u32[]{:S(2)}) copy-start(bf16[128,1536]{1,0:T(8,128)(2,1)} %get-tuple-element.59) | copy-start | bytes 1179652
  255.0 4.3 %copy-start.4 = (bf16[128,1536]{1,0:T(8,128)(2,1)S(1)}, bf16[128,1536]{1,0:T(8,128)(2,1)}, u32[]{:S(2)}) copy-start(bf16[128,1536]{1,0:T(8,128)(2,1)} %get-tuple-element.60) | copy-start | bytes 1179652

commit v3 on v2

--- a/solution.py
+++ b/solution.py
@@ -242,13 +242,14 @@
 
 
 def forward_kernel(
-    s_ref, proj, act, coef, dtw, dtb, a2, skip, dy, silu_z, slope_z, hidden, grad_branch, w_out,
-    hp, dl, dread, branch, out_part, z_part, grad_z,
+    s_ref, proj, act, coef, dtw, dtb, a2, skip, dy, silu_z, slope_z, hidden, w_out,
+    hp, dl, dread, branch, sorted_gated, z_part, grad_z,
     y, h_sc, hb_sc, h_a, h_b, r0, r1, r2, red, gated,
 ):
     j = pl.program_id(0)
     blocks = pl.num_programs(0) // 2
     length, chans = dl.shape[1:]
+    n_dp = lax.axis_size("dp")
 
     @pl.when(lax.rem(j, blocks) == 0)
     def _():
@@ -284,7 +285,12 @@
         def rows_of(c, carry):
             at = pl.ds(pl.multiple_of(c * 64, 64), 64)
             value = y[at, :]
-            gated[at, :] = (value * silu_z[at, :]).astype(BF)
+            opened = value * silu_z[at, :]
+            gated[at, :] = opened.astype(BF)
+            piece = 4 * sorted_gated.shape[2] // n_dp
+            for q in range(4):
+                pieces = [opened[:, b * piece : (b + 1) * piece] for b in range(q, n_dp, 4)]
+                sorted_gated[q, at, :] = jnp.concatenate(pieces, axis=1).astype(BF)
             grad_z[at, :] = (value * slope_z[at, :]).astype(BF)
             return carry
 
@@ -296,15 +302,12 @@
             branch[at, :] = dot(gated[at, :], w_out[...]).astype(BF)
 
         for c in range(2):
-            at = slice(c * chans // 2, (c + 1) * chans // 2)
-            out_part[at, :] = dot_tn(gated[:, at], grad_branch[...]).astype(BF)
-        for c in range(2):
             at = slice(c * width // 2, (c + 1) * width // 2)
             z_part[at, :] = dot_tn(hidden[:, at], grad_z[...]).astype(BF)
 
 
 def scan_forward(
-    seq_index, proj, act, coef, dtw, dtb, a2, skip, dy, silu_z, slope_z, hidden, grad_branch, w_out, tile
+    seq_index, proj, act, coef, dtw, dtb, a2, skip, dy, silu_z, slope_z, hidden, w_out, tile
 ):
     total, chans = dy.shape
     width = w_out.shape[1]
@@ -338,7 +341,7 @@
         pl.BlockSpec((2, chans), lambda j, s: (0, s[0])),
         pl.BlockSpec((1, STATE, chans), direction_of),
         pl.BlockSpec((2, chans), lambda j, s: (0, s[0])),
-    ] + [whole] * 5
+    ] + [whole] * 4
     in_specs += [pl.BlockSpec((chans, width), lambda j, s: (s[0], 0))]
     out_specs = [
         pl.BlockSpec((1, tile * STATE, chans), tokens_of),
@@ -350,7 +353,7 @@
         jax.ShapeDtypeStruct((2, total, chans), F32),
         jax.ShapeDtypeStruct((2, blocks, STATE, tile), F32),
         jax.ShapeDtypeStruct((total, width), BF),
-        jax.ShapeDtypeStruct((chans, width), BF),
+        jax.ShapeDtypeStruct((4, total, chans // 4), BF),
         jax.ShapeDtypeStruct((width, chans), BF),
         jax.ShapeDtypeStruct((total, chans), BF),
     ]
@@ -374,7 +377,7 @@
         out_shape=out_shape,
         compiler_params=pltpu.CompilerParams(vmem_limit_bytes=60 << 20),
         name="scan_forward",
-    )(seq_index, proj, act, coef, dtw, dtb, a2, skip, dy, silu_z, slope_z, hidden, grad_branch, w_out)
+    )(seq_index, proj, act, coef, dtw, dtb, a2, skip, dy, silu_z, slope_z, hidden, w_out)
 
 
 def sibling_of(s):
@@ -396,11 +399,11 @@
     )
 
 
-def greet(peers, more=0):
+def greet(peers):
     barrier = pltpu.get_barrier_semaphore()
     for peer in peers:
         pl.semaphore_signal(barrier, inc=1, device_id=peer, device_id_type=MESH)
-    pl.semaphore_wait(barrier, len(peers) + more)
+    pl.semaphore_wait(barrier, len(peers))
 
 
 def comm_params(collective_id, mib=48):
@@ -410,6 +413,83 @@
 
 
 class DpScatter:
+    def __init__(self, x, got, acc, far, sems, out=None):
+        self.x, self.got, self.acc, self.far = x, got, acc, far
+        self.out = x if out is None else out
+        self.sems = sems
+        d = lax.axis_index("dp")
+        n = lax.axis_size("dp") // 2
+        self.n = n
+        self.y = lax.rem(d, 2)
+        self.z = d // 2
+        self.order = sorted(range(n), key=lambda m: (m & -m or n, -m))
+
+    def flipped(self, mask):
+        z = self.z
+        for bit in range(mask.bit_length()):
+            if mask >> bit & 1:
+                z = z + 2**bit * (1 - 2 * lax.rem(self.z // 2**bit, 2))
+        return z
+
+    @staticmethod
+    def scratch(n_dp, block):
+        n = n_dp // 2
+        dma = pltpu.SemaphoreType.DMA
+        return [pltpu.VMEM((n,) + block, BF)] * 3 + [dma((4, n))]
+
+    def near_copy(self, k):
+        z = self.flipped(self.order[k])
+        return pltpu.make_async_remote_copy(
+            src_ref=self.out.at[2 * z + 1 - self.y],
+            dst_ref=self.got.at[k],
+            send_sem=self.sems.at[0, k],
+            recv_sem=self.sems.at[1, k],
+            device_id={"dp": 2 * self.z + 1 - self.y},
+            device_id_type=MESH,
+        )
+
+    def far_copy(self, k):
+        mask = self.order[k]
+        return pltpu.make_async_remote_copy(
+            src_ref=self.acc.at[k],
+            dst_ref=self.far.at[k],
+            send_sem=self.sems.at[2, k],
+            recv_sem=self.sems.at[3, k],
+            device_id={"dp": 2 * self.flipped(mask & -mask) + self.y},
+            device_id_type=MESH,
+        )
+
+    def start(self):
+        for k in range(self.n):
+            self.near_copy(k).start()
+
+    def pair(self, k):
+        mask = self.order[k]
+        self.near_copy(k).wait()
+        z = self.flipped(mask)
+        total = self.x[2 * z + self.y].astype(F32) + self.got[k].astype(F32)
+        bit = 1
+        while mask and bit < mask & -mask:
+            other = self.order.index(mask + bit)
+            self.far_copy(other).wait()
+            total = total + self.far[other].astype(F32)
+            bit *= 2
+        self.acc[k] = total.astype(BF)
+        if mask:
+            self.far_copy(k).start()
+
+    def finish(self):
+        total = self.acc[self.n - 1].astype(F32)
+        bit = 1
+        while bit < self.n:
+            other = self.order.index(bit)
+            self.far_copy(other).wait()
+            total = total + self.far[other].astype(F32)
+            bit *= 2
+        return total
+
+
+class DpDirect:
     def __init__(self, x, got, acc, far, sems, out=None):
         self.x, self.got, self.acc, self.far = x, got, acc, far
         self.out = x if out is None else out
@@ -521,9 +601,12 @@
             for k in (2, 1, 3)
         ]
 
-    def start(self):
+    def send(self):
         for copy in self.copies:
             copy.start()
+
+    def start(self):
+        self.send()
         self.dst[self.s] = self.src[self.s]
 
     def finish(self):
@@ -542,8 +625,8 @@
     return [lax.rem(s + k, 4) for k in (1, 2, 3)]
 
 
-def greet_all(more=0):
-    greet([{"seq": other} for other in seq_others()] + [{"dp": other} for other in dp_others()], more)
+def greet_all():
+    greet([{"seq": other} for other in seq_others()] + [{"dp": other} for other in dp_others()])
 
 
 class Spread:
@@ -555,7 +638,8 @@
         pair = (sems.at[0], sems.at[1])
         block, column, mine, other = buf.at[s, z, y], buf.at[s, :, y], buf.at[s], buf.at[far]
         self.along_z = [
-            remote(block, block, pair, k, {"dp": 2 * lax.rem(z + k + 1, n) + y}) for k in range(n - 1)
+            remote(block, block, pair, k, {"dp": 2 * lax.rem(z + k + 1, n) + y})
+            for k in range(n - 1)
         ]
         self.along_y = remote(column, column, pair, n - 1, {"dp": 2 * z + 1 - y})
         self.along_x = remote(mine, mine, pair, n, {"seq": far})
@@ -606,7 +690,8 @@
     def scratch(rows, width):
         return (
             [pltpu.VMEM((2, rows, width), F32)] * 2
-            + [pltpu.VMEM((rows, width), F32)] * 3
+            + [pltpu.VMEM((rows, width), F32)]
+            + [pltpu.VMEM((rows, width), BF)] * 2
             + [pltpu.SemaphoreType.DMA((2, 3))]
         )
 
@@ -615,47 +700,16 @@
 
     def cross(self):
         self.first.wait()
-        self.half[...] = self.x[self.c] + self.from_sib[...]
+        self.half[...] = (self.x[self.c] + self.from_sib[...]).astype(BF)
         self.second.start()
 
     def back(self):
         self.second.wait()
-        self.total[self.c] = self.half[...] + self.from_x[...]
+        self.total[self.c] = self.half[...].astype(F32) + self.from_x[...].astype(F32)
         self.third.start()
 
     def finish(self):
         self.third.wait()
-
-
-class Turn:
-    def __init__(self, src, dst, sems):
-        d, s = lax.axis_index("dp"), lax.axis_index("seq")
-        n_dp = lax.axis_size("dp")
-        here, target = 4 * d + s, s * n_dp + d
-        self.apart = here != target
-        self.source = {"dp": lax.rem(here, n_dp), "seq": here // n_dp}
-        self.copy = remote(
-            src, dst, (sems.at[0], sems.at[1]), 0, {"dp": target // 4, "seq": lax.rem(target, 4)}
-        )
-        self.src, self.dst = src, dst
-
-    def greet(self):
-        @pl.when(self.apart)
-        def _():
-            barrier = pltpu.get_barrier_semaphore()
-            pl.semaphore_signal(barrier, inc=1, device_id=self.source, device_id_type=MESH)
-
-        return jnp.where(self.apart, 1, 0)
-
-    def start(self):
-        pl.when(self.apart)(self.copy.start)
-
-        @pl.when(jnp.logical_not(self.apart))
-        def _():
-            self.dst[...] = self.src[...]
-
-    def finish(self):
-        pl.when(self.apart)(self.copy.wait)
 
 
 def first_kernel(*refs):
@@ -916,7 +970,7 @@
 
     (dl, hp, proj, act, coef, a2, dy, dread) = take(8)
     (tok, cot, gate, scale, flags) = take(5)
-    far_inputs = take(12)
+    far_inputs = take(13)
     dt_weight, conv_weight, skip_all = far_inputs[6:9]
     in_weight, xproj_weight = far_inputs[4:6]
     (result, tokg, in_ref, out_ref, a_ref, x0_ref, x1_ref, cv_ref, table_ref) = take(9)
@@ -925,17 +979,17 @@
     slope, xpad, hidden, grad_z, w_x, w_z, xproj, dtw, conv_w, skip, hid_in, out_in, xs_in, local_sems = take(14)
     conv_acc, dxin, gate_row = take(3)
     seq1 = SeqScatter(hid_in, *take(4), out=far_inputs[9])
-    outs = DpScatter(out_in, *take(4), out=far_inputs[10])
+    outs = DpScatter(out_in, *take(4))
     zs = DpScatter(xs_in, *take(4), out=far_inputs[11])
-    out_red, out_got, turn_sems = take(3)
-    turn = Turn(out_red, out_got, turn_sems)
+    gates, gate_sems = take(2)
+    g_swap = SeqSwap(far_inputs[10], gates, gate_sems)
     z_red, z_got, z_swap_sems = take(3)
     z_swap = SeqSwap(z_red, z_got, z_swap_sems)
     c7 = SeqReduce(*take(6))
     smalls = []
     for _ in range(5):
         source = take(1)[0]
-        scatter = DpScatter(source, *take(4))
+        scatter = DpDirect(source, *take(4))
         buf, sems = take(2)
         smalls.append((source, scatter, buf, Spread(buf, sems)))
     parts_a, parts_x, part_c = smalls[:2], smalls[2:4], smalls[4]
@@ -954,6 +1008,7 @@
     n = outs.n
     n_dp = 2 * n
     d_index, s_index = lax.axis_index("dp"), lax.axis_index("seq")
+    rows_x = chans // n_dp
 
     def loads():
         own = pl.ds(pl.multiple_of(s_index * chans, 128), chans)
@@ -961,7 +1016,7 @@
         pairs = [
             (far_inputs[0], slope),
             (far_inputs[1], xpad.at[pl.ds(16, total)]),
-            (far_inputs[2], hidden),
+            (far_inputs[12], hidden),
             (far_inputs[3], grad_z),
             (in_weight.at[:, own], w_x),
             (in_weight.at[:, own_z], w_z),
@@ -969,9 +1024,10 @@
             (dt_weight.at[:, :, own], dtw.at[:, pl.ds(0, dt_weight.shape[1])]),
             (conv_weight.at[:, :, own], conv_w),
             (far_inputs[9], hid_in),
-            (far_inputs[10], out_in),
+            (far_inputs[10].at[s_index], gates.at[s_index]),
             (far_inputs[11], xs_in),
             (skip_all.at[:, own], skip),
+            (far_inputs[2], hidden),
         ]
         return [pltpu.make_async_copy(a, b, local_sems.at[i]) for i, (a, b) in enumerate(pairs)]
 
@@ -983,20 +1039,21 @@
         pairs += [(parts_x[0][2], x0_ref), (parts_x[1][2], x1_ref), (part_c[2], cv_ref)]
         return [pltpu.make_async_copy(a, b, result_sems.at[i]) for i, (a, b) in enumerate(pairs)]
 
-    near = [(outs, k) for k in range(n)] + [(zs, k) for k in range(n)]
-    start_at = [0, 0, 1, 3, 4, 6, 7, 8]
-    pair_at = [4, 5, 6, 7, 8, 8, 8, 8]
-
-    def step_of(plan, i):
-        return plan[i * 8 // (2 * n)]
+    near = [(zs, k) for k in range(n)] + [(outs, k) for k in range(n)]
+    pair_at = [2, 4, 5, 7, 8, 8, 8, 8]
+
+    def step_of(i):
+        return pair_at[i * 8 // (2 * n)]
 
     unit = 2 * blocks // 8
 
     @pl.when(j == 0)
     def _():
-        greet_all(turn.greet())
+        greet_all()
+        g_swap.send()
         seq1.start()
-        for copy in loads():
+        zs.start()
+        for copy in loads()[:13]:
             copy.start()
         loads()[12].wait()
         for d in range(2):
@@ -1009,21 +1066,26 @@
         sums[...] = jnp.zeros_like(sums)
         conv_acc[...] = jnp.zeros_like(conv_acc)
 
-    for i, (scatter, k) in enumerate(near):
-        if step_of(pair_at, i) < 8:
-            pl.when(j == unit * step_of(pair_at, i))(functools.partial(scatter.pair, k))
-        if step_of(start_at, i) < 8:
-            pl.when(j == unit * step_of(start_at, i))(scatter.near_copy(k).start)
-
     @pl.when(j == 2 * unit)
     def _():
-        loads()[9].wait()
+        for copy in loads()[9:12]:
+            copy.wait()
         seq1.cross()
 
     @pl.when(j == 3 * unit)
     def _():
-        loads()[10].wait()
-        loads()[11].wait()
+        g_swap.finish()
+        loads()[2].wait()
+        for q in range(4):
+            grad = dot_tn(gates[q], hidden[...]).astype(BF)
+            for b in range(n_dp // 4):
+                out_in[n_dp // 4 * q + b] = grad[b * rows_x : (b + 1) * rows_x]
+        outs.start()
+        loads()[13].start()
+
+    for i, (scatter, k) in enumerate(near):
+        if step_of(i) < 8:
+            pl.when(j == unit * step_of(i))(functools.partial(scatter.pair, k))
 
 
     @pl.when(j == 5 * unit)
@@ -1053,11 +1115,17 @@
 
     @pl.when(j == 2 * blocks - 1)
     def _():
-        late = [i for i in range(2 * n) if step_of(start_at, i) >= 8]
-        for i in late:
-            near[i][0].near_copy(near[i][1]).start()
-        for copy in loads()[:9]:
-            copy.wait()
+        late = [near[i] for i in range(2 * n) if step_of(i) >= 8]
+
+        def pairs():
+            for _ in range(len(late) // 4):
+                scatter, k = late[pairs.done]
+                pairs.done += 1
+                scatter.pair(k)
+
+        pairs.done = 0
+        for i in (0, 1, 3, 4, 5, 6, 7, 8, 13):
+            loads()[i].wait()
         for d in range(2):
             value = dot_nt(dpre[d], dtw[d])
             for b in range(blocks):
@@ -1067,8 +1135,6 @@
                 )
                 c7.x[d, at] = value[at] + square.T
         c7.start()
-        late = [i for i in range(2 * n) if step_of(pair_at, i) >= 8]
-        quarter = len(late) // 4
         rank = 128 - 2 * STATE
         per_d = 128 // n_dp
         for d in range(2):
@@ -1082,17 +1148,13 @@
                 source[b] = lines[b * per_d : (b + 1) * per_d]
             scatter.start()
         c7.cross()
-        for i in late[:quarter]:
-            near[i][0].pair(near[i][1])
-        for _, scatter, _, _ in parts_a:
-            for k in range(n):
-                scatter.pair(k)
+        pairs()
+        z_red[...] = zs.finish().astype(BF)
+        z_swap.start()
         c7.back()
-        for i in late[quarter : 2 * quarter]:
-            near[i][0].pair(near[i][1])
+        pairs()
         c7.finish()
 
-        rows_x = chans // n_dp
         for d in range(2):
             dproj = c7.total[d].astype(BF)
             source, scatter, _, _ = parts_x[d]
@@ -1109,7 +1171,7 @@
                 return carry
 
             lax.fori_loop(0, total // 128, act_rows, 0)
-
+        pairs()
         step = 32
 
         def conv_rows(c, carry):
@@ -1129,8 +1191,14 @@
             return carry
 
         lax.fori_loop(0, total // step, conv_rows, 0)
-        for i in late[2 * quarter :]:
-            near[i][0].pair(near[i][1])
+        source, scatter, _, _ = part_c
+        conv_lines = [jnp.sum(conv_acc[i], axis=0, keepdims=True) for i in range(10)]
+        conv_lines = jnp.concatenate(conv_lines + [jnp.zeros((6, chans), F32)], axis=0)
+        for b in range(n_dp):
+            source[b, :, :rows_x] = conv_lines[:, b * rows_x : (b + 1) * rows_x].astype(BF)
+            source[b, :, rows_x:] = jnp.zeros((16, 128 - rows_x), BF)
+        scatter.start()
+        pairs()
 
         rb = width // (4 * n_dp)
         half = n_dp // 2
@@ -1142,9 +1210,9 @@
                     first = (4 * b + q) * rb
                     xs_in[h * half + b, q] = grad[first : first + rb]
         xs.start()
-        for _, scatter, buf, spread in parts_a:
-            buf[spread.place] = scatter.finish().astype(BF)
-            spread.go_z()
+        for _, scatter, _, _ in parts_a:
+            for k in range(n):
+                scatter.pair(k)
         seg = tok.shape[0]
         for h in range(2):
             cols = slice(h * width // 2, (h + 1) * width // 2)
@@ -1152,43 +1220,29 @@
             for q in range(4):
                 hid_in[q, :, cols] = grad[q * seg : (q + 1) * seg]
         seq2.start()
-        for _, scatter, _, _ in parts_x:
+        for _, scatter, _, _ in parts_x + [part_c]:
             for k in range(n):
                 scatter.pair(k)
-        source, scatter, _, _ = part_c
-        conv_lines = [jnp.sum(conv_acc[i], axis=0, keepdims=True) for i in range(10)]
-        conv_lines = jnp.concatenate(conv_lines + [jnp.zeros((6, chans), F32)], axis=0)
-        for b in range(n_dp):
-            source[b, :, :rows_x] = conv_lines[:, b * rows_x : (b + 1) * rows_x].astype(BF)
-            source[b, :, rows_x:] = jnp.zeros((16, 128 - rows_x), BF)
-        scatter.start()
         seq2.cross()
-        out_red[...] = outs.finish().astype(BF)
-        turn.start()
-        for _, _, _, spread in parts_a:
-            spread.go_y()
-        z_red[...] = zs.finish().astype(BF)
-        for k in range(n):
-            part_c[1].pair(k)
-        for _, scatter, buf, spread in parts_x:
-            buf[spread.place] = scatter.finish().astype(BF)
-            spread.go_z()
+        for k in range(n // 4):
+            xs.pair(k)
+
+        def gathered(parts):
+            for _, scatter, buf, spread in parts:
+                buf[spread.place] = scatter.finish().astype(BF)
+                spread.go_z()
+
+        gathered(parts_a)
+        gathered(parts_x + [part_c])
+        out_ref[...] = outs.finish().astype(BF)
+        for k in range(n // 4, n // 2):
+            xs.pair(k)
 
         grad = seq2.finish()
-        z_swap.start()
-        for _, _, _, spread in parts_a:
-            spread.go_x()
         tokens = tok[...].astype(F32)
         centred = tokens - jnp.mean(tokens, axis=1, keepdims=True)
         inv_std = lax.rsqrt(jnp.mean(centred * centred, axis=1, keepdims=True) + epsilon)
         normed = centred * inv_std
-        grad_normed = grad * (1.0 + scale[...])
-        inner_product = jnp.mean(grad_normed * normed, axis=1, keepdims=True)
-        tokg[...] = (
-            cot[...].astype(F32)
-            + inv_std
-            * (grad_normed - jnp.mean(grad_normed, axis=1, keepdims=True) - normed * inner_product)
-        ).astype(BF)
         row[:, :width] = jnp.sum(grad, axis=0, keepdims=True)
         row[:, width : 2 * width] = jnp.sum(grad * normed, axis=0, keepdims=True)
         row[:, 2 * width : 3 * width] = gate_row[...]
@@ -1200,10 +1254,17 @@
         ]
         for copy in row_copies:
             copy.start()
-        source, scatter, buf, spread_c = part_c
-        buf[spread_c.place] = scatter.finish().astype(BF)
-        spread_c.go_z()
-        for k in range(n // 2):
+        grad_normed = grad * (1.0 + scale[...])
+        inner_product = jnp.mean(grad_normed * normed, axis=1, keepdims=True)
+        tokg[...] = (
+            cot[...].astype(F32)
+            + inv_std
+            * (grad_normed - jnp.mean(grad_normed, axis=1, keepdims=True) - normed * inner_product)
+        ).astype(BF)
+        spreads = [item[3] for item in parts_a + parts_x + [part_c]]
+        for spread in spreads:
+            spread.go_y()
+        for k in range(n // 2, 3 * n // 4):
             xs.pair(k)
         for copy in row_copies:
             copy.wait()
@@ -1215,56 +1276,45 @@
         ]
         for copy in table_copies:
             copy.start()
-        spreads_x = [item[3] for item in parts_x] + [spread_c]
-        for spread in spreads_x:
-            spread.go_y()
-        for _, _, _, spread in parts_a:
-            spread.go_sib()
-        for k in range(n // 2, n - 1):
+        for k in range(3 * n // 4, n):
             xs.pair(k)
-        for spread in spreads_x:
+        for spread in spreads:
             spread.go_x()
-        xs.pair(n - 1)
-        turn.finish()
-        out_ref[...] = out_got[...]
+        x_red[...] = xs.finish().astype(BF)
+        x_swap.start()
         z_swap.finish()
         for q in range(4):
             in_ref[:, (4 + q) * chans : (5 + q) * chans] = z_got[q]
-        for spread in spreads_x:
-            spread.go_sib()
-        for (_, _, buf, spread), d in zip(parts_a, range(2)):
-            spread.finish()
-            for copy in results()[4 * d : 4 * d + 4]:
-                copy.start()
         for copy in table_copies:
             copy.wait()
         table_ref[...] = table[...]
-        x_red[...] = xs.finish().astype(BF)
-        x_swap.start()
-        for spread in spreads_x:
-            spread.finish()
-        for copy in results()[8:]:
-            copy.start()
+        for spread in spreads:
+            spread.go_sib()
         x_swap.finish()
         for q in range(4):
             in_ref[:, q * chans : (q + 1) * chans] = x_got[q]
+        for spread in spreads:
+            spread.finish()
+        for copy in results():
+            copy.start()
         for copy in results():
             copy.wait()
 
 
 def scan_backward(
-    dl, hp, proj, act, coef, a2, dy, dread, branch, out_part, z_part,
+    dl, hp, proj, act, coef, a2, dy, dread, branch, sorted_gated, grad_branch, z_part,
     tok, cot, gate, scale, flags, slope, xin, hidden, grad_z, in_weight, xproj_weight, dt_weight, conv_weight, skip,
     collective_id, tile,
 ):
     total, chans = dy.shape
     blocks = total // tile
-    n_dp = out_part.shape[0]
+    n_dp = z_part.shape[0]
     n = n_dp // 2
     rows, width = tok.shape
     rb = width // (4 * n_dp)
     rows_x = chans // n_dp
     per_d = 128 // n_dp
+    out_block = (rows_x, width)
 
     def place(j):
         d = j // blocks
@@ -1288,7 +1338,7 @@
         + [VMEM_SPEC] * 2
         + [pl.BlockSpec((1, tile // U, 2 * STATE, U), cells)]
         + [VMEM_SPEC] * 8
-        + [any_spec] * 12
+        + [any_spec] * 13
     )
     shape = jax.ShapeDtypeStruct
     in_out = (4, n, 2)
@@ -1296,7 +1346,7 @@
         shape((rows, width), BF),
         shape((rows, width), BF),
         shape((rb, 8 * chans), BF),
-        shape(out_part.shape[1:], BF),
+        shape(out_block, BF),
         shape((2, n, 2, per_d, 4 * chans), BF),
         shape(in_out + (rows_x, 128), BF),
         shape(in_out + (rows_x, 128), BF),
@@ -1332,9 +1382,9 @@
         vmem((2, 4, chans), F32),
         vmem((2, chans), F32),
         vmem((4, rows, width), BF),
-        vmem(out_part.shape, BF),
+        vmem((n_dp,) + out_block, BF),
         vmem(z_part.shape, BF),
-        dma((13,)),
+        dma((14,)),
     ]
     scratch += [
         vmem((10, 8, chans), F32),
@@ -1342,8 +1392,8 @@
         vmem((1, width), F32),
     ]
     scratch += SeqScatter.scratch(rows, width)
-    scratch += DpScatter.scratch(n_dp, out_part.shape[1:]) + DpScatter.scratch(n_dp, z_part.shape[1:])
-    scratch += [vmem(out_part.shape[1:], BF)] * 2 + [dma((2, 1))]
+    scratch += DpScatter.scratch(n_dp, out_block) + DpScatter.scratch(n_dp, z_part.shape[1:])
+    scratch += [vmem(sorted_gated.shape, BF), dma((2, 3))]
     scratch += [vmem(z_part.shape[1:], BF)] * 2 + [dma((2, 3))]
     scratch += SeqReduce.scratch(total, 128)
     for block in [(per_d, chans)] * 2 + [(rows_x, 128)] * 2 + [(16, 128)]:
@@ -1371,8 +1421,8 @@
         name="scan_backward",
     )(
         dl, hp, proj, act, coef, a2, dy, dread, tok, cot, gate, scale, flags, slope, xin, hidden,
-        grad_z, in_weight, xproj_weight, dt_weight, conv_weight, skip, branch, out_part,
-        z_part,
+        grad_z, in_weight, xproj_weight, dt_weight, conv_weight, skip, branch,
+        sorted_gated, z_part, grad_branch,
     )
 
 
@@ -1434,9 +1484,9 @@
     gate_term = modulation[:, 2 * width :]
     tile = 128 if n_dp <= 8 else 32
     coef = jnp.swapaxes(proj[:, :, 128 - 2 * STATE :].reshape(2, length // U, U, 2 * STATE), 2, 3)
-    held, delta, dread, branch, out_part, z_part, grad_z = scan_forward(
+    held, delta, dread, branch, sorted_gated, z_part, grad_z = scan_forward(
         seq_index.astype(jnp.int32)[None], proj, act, coef, dt_weight, dt_bias, decay2,
-        skip, dy, silu_z, slope_z, hidden, grad_branch, out_weight, tile,
+        skip, dy, silu_z, slope_z, hidden, out_weight, tile,
     )
     total = n_dp * n_seq
 
@@ -1446,7 +1496,8 @@
     result, grad_tok, in_rows, out_rows, lines, x0, x1, conv_lines, table = scan_backward(
         delta, held, proj, act, coef, decay2, dy, dread,
         branch.reshape(n_seq, seg_len, width),
-        out_part.reshape(n_dp, chans // n_dp, width),
+        sorted_gated,
+        grad_branch,
         in_blocks(z_part),
         tokens[0], cotangent[0], gate_term, scale_term, own_flags[0][:, None],
         slope, xin, hidden, grad_z, in_weight, xproj_weight, dt_weight, conv_weight, skip,

time: 261 us -> 225 us (0.86)
  Pallas kernels: 231 us -> 194 us
    pallas_call x1, Pallas kernels: 155 us -> 122 us  [scan_backward(): pl.pallas_call(backward_kernel, grid=(2 * blocks,), in_specs=in_specs, ou...]
    pallas_call x1, Pallas kernels: 38.3 us -> 35.5 us  [first_part(): pl.pallas_call(first_kernel, in_specs=[VMEM_SPEC] * 6 + [any_spec] * 7, o...]
where the time goes in v3:
time: 225 us; the launch traced here: 223 us
  Pallas kernels  194 us (86%)
  local copies, waits for them, and re-layouts  15.5 us (7%)
  other arithmetic  8.64 us (4%)
  matrix products  3.57 us (2%)
    pallas_call x1, Pallas kernels, scan_backward(): pl.pallas_call(backward_kernel, grid=(2 * blocks,), in_specs=in_specs, ou...  122 us
    pallas_call x1, Pallas kernels, scan_forward(): pl.pallas_call(forward_kernel, grid_spec=pltpu.PrefetchScalarGridSpec(num...  36.2 us
    pallas_call x1, Pallas kernels, first_part(): pl.pallas_call(first_kernel, in_specs=[VMEM_SPEC] * 6 + [any_spec] * 7, o...  35.5 us

profile of v3, /device:TPU:11, one launch (start us, length us, event | category | flops | bytes accessed | tf_op | source)
XLA Modules:
  0.0 223.1 jit_solution(2462174836529447968)
XLA Ops:
  1.3 0.7 convert_element_type.31
  2.0 0.8 fusion.6
  2.7 0.8 fusion.7
  3.5 1.3 broadcast_in_dim.27.refs_4_
  4.8 0.6 broadcast_in_dim.26.refs_2_
  5.4 1.3 broadcast_in_dim.28.refs_5_
  6.7 0.2 multiply_cosine_fusion
  6.9 0.6 multiply_convert_fusion.refs_3_
  7.5 0.7 copy.35.refs_12_
  8.2 35.5 %first_part.1 = (bf16[512,1536]{1,0:T(8,128)(2,1)}, bf16[512,1536]{1,0:T(8,128)(2,1)}, bf16[512,768]{1,0:T(8,128)(2,1)}, bf16[2,512,768]{2,1,0:T(8,128)(2,1)}, b...) custom-call(bf16[128,1536]{1,0:T(8,128)(2,1)} %bitcast.44, ...), custom_call_target="tpu_custom_call" | custom-call | tf_op jit(solution)/shard_map/first_part/pallas_call | solution.py:942
  43.8 1.3 fusion.4
  45.1 1.2 slice.41
  46.4 1.3 copy.34
  47.7 36.2 %scan_forward.1 = (bf16[2,8192,768]{2,1,0:T(8,128)(2,1)}, f32[2,512,768]{2,1,0:T(8,128)}, f32[2,4,16,128]{3,2,1,0:T(8,128)}, bf16[512,1536]{1,0:T(8,128)(2,1)}, ...) custom-call(s32[1]{0:T(128)} %bitcast.s_ref, ...), custom_call_target="tpu_custom_call" | custom-call | tf_op jit(solution)/shard_map/scan_forward/pallas_call | solution.py:360
  83.9 122.2 %scan_backward.1 = (bf16[128,1536]{1,0:T(8,128)(2,1)}, bf16[128,1536]{1,0:T(8,128)(2,1)}, bf16[48,6144]{1,0:T(8,128)(2,1)}, bf16[96,1536]{1,0:T(8,128)(2,1)}, bf...) custom-call(f32[2,512,768]{2,1,0:T(8,128)} %get-tuple-element.48.ref, ...), custom_call_target="tpu_custom_call" | custom-call | tf_op jit(solution)/shard_map/scan_backward/pallas_call | solution.py:1413
  206.1 0.0 copy-start.8
  206.1 0.0 copy-start.6
  206.2 1.0 slice_bitcast_fusion.1
  207.1 0.0 copy-start.3
  207.2 0.1 copy.36
  207.3 0.2 reshape.66
  207.5 0.7 slice.57
  208.2 0.6 copy.47
  208.8 0.0 copy-done.8
  208.8 0.1 copy.46
  208.9 0.0 copy-start
  208.9 0.6 slice_reduce_fusion
  209.5 0.7 dynamic-slice_reduce_fusion
  210.2 0.0 copy-done.6
  210.2 0.9 convert_element_type.38
  211.1 0.0 copy-done.3
  211.1 1.1 convert_element_type.33
  212.2 0.0 copy-done
  212.2 0.5 bitcast_convert_fusion
  212.7 0.6 copy_bitcast_fusion.1
  213.3 0.8 slice_bitcast_fusion
  214.1 0.0 copy-start.1
  214.1 0.0 copy-start.2
  214.1 1.6 slice.59
  215.7 0.0 copy-done.1
  215.7 0.5 copy-done.2
  216.2 1.9 maximum_convert_fusion
  218.1 0.0 copy-done.7
  218.1 3.6 %fusion = f32[1536,576]{0,1:T(8,128)} fusion(bf16[8,1536]{1,0:T(8,128)(2,1)S(1)} %copy-done.7, f32[8,4608]{1,0:T(8,128)S(1)} %slice.54, s32[]{:T(128)S(6)} %select_n.14), kind=kOutput, calls=%fused_computation.15 | convolution fusion | flops 84934656 | bytes 3584004 | tf_op jit(solution)/shard_map/dot_general | solution.py:1510
  221.6 0.0 copy-done.5
  221.6 0.7 copy.51
  222.4 0.0 copy-done.4
  222.4 0.7 copy.52
  (8 shorter events, 0.1 us)
Async XLA Ops:
  206.1 2.7 %copy-start.8 = (f32[8,1,6144]{2,1,0:T(1,128)S(1)}, f32[8,1,6144]{2,1,0:T(1,128)}, u32[]{:S(2)}) copy-start(f32[8,1,6144]{2,1,0:T(1,128)} %get-tuple-element.61) | copy-start | bytes 589828
  206.1 4.1 %copy-start.6 = (bf16[96,1536]{1,0:T(8,128)(2,1)S(1)}, bf16[96,1536]{1,0:T(8,128)(2,1)}, u32[]{:S(2)}) copy-start(bf16[96,1536]{1,0:T(8,128)(2,1)} %get-tuple-element.67) | copy-start | bytes 884740
  207.1 3.9 %copy-start.3 = (bf16[48,6144]{1,0:T(8,128)(2,1)S(1)}, bf16[48,6144]{1,0:T(8,128)(2,1)}, u32[]{:S(2)}) copy-start(bf16[48,6144]{1,0:T(8,128)(2,1)} %get-tuple-element.62) | copy-start | bytes 1769476
  208.9 3.3 %copy-start = (bf16[2,4,2,16,3072]{4,3,2,1,0:T(8,128)(2,1)S(1)}, bf16[2,4,2,16,3072]{4,3,2,1,0:T(8,128)(2,1)}, u32[]{:S(2)}) copy-start(bf16[2,4,2,16,3072]{4,3,2,1,0:T(8,128)(2,1)} %get-tuple-element.66) | copy-start | bytes 4718596
  214.1 1.6 copy-start.1
  214.1 2.1 copy-start.2
  216.2 1.9 copy-start.7
  218.1 3.6 %copy-start.5 = (bf16[128,1536]{1,0:T(8,128)(2,1)S(1)}, bf16[128,1536]{1,0:T(8,128)(2,1)}, u32[]{:S(2)}) copy-start(bf16[128,1536]{1,0:T(8,128)(2,1)} %get-tuple-element.59) | copy-start | bytes 1179652
  218.1 4.3 %copy-start.4 = (bf16[128,1536]{1,0:T(8,128)(2,1)S(1)}, bf16[128,1536]{1,0:T(8,128)(2,1)}, u32[]{:S(2)}) copy-start(bf16[128,1536]{1,0:T(8,128)(2,1)} %get-tuple-element.60) | copy-start | bytes 1179652

commit v4 on v3

--- a/solution.py
+++ b/solution.py
@@ -242,14 +242,22 @@
 
 
 def forward_kernel(
-    s_ref, proj, act, coef, dtw, dtb, a2, skip, dy, silu_z, slope_z, hidden, w_out,
+    s_ref, proj, act, coef, dtw, dtb, a2, skip, dy, silu_all, slope_all, hidden_all, out_weight,
     hp, dl, dread, branch, sorted_gated, z_part, grad_z,
-    y, h_sc, hb_sc, h_a, h_b, r0, r1, r2, red, gated,
+    y, h_sc, hb_sc, h_a, h_b, r0, r1, r2, red, gated, silu_z, slope_z, hidden, w_out, sems,
 ):
     j = pl.program_id(0)
     blocks = pl.num_programs(0) // 2
     length, chans = dl.shape[1:]
     n_dp = lax.axis_size("dp")
+    own_rows = pl.ds(pl.multiple_of(s_ref[0] * chans, 128), chans)
+    late = [(silu_all, silu_z), (slope_all, slope_z), (hidden_all, hidden), (out_weight.at[own_rows], w_out)]
+    late = [pltpu.make_async_copy(a, b, sems.at[i]) for i, (a, b) in enumerate(late)]
+
+    @pl.when(j == 0)
+    def _():
+        for copy in late:
+            copy.start()
 
     @pl.when(lax.rem(j, blocks) == 0)
     def _():
@@ -281,6 +289,8 @@
     @pl.when(j == 2 * blocks - 1)
     def _():
         total = y.shape[0]
+        for copy in late:
+            copy.wait()
 
         def rows_of(c, carry):
             at = pl.ds(pl.multiple_of(c * 64, 64), 64)
@@ -341,8 +351,7 @@
         pl.BlockSpec((2, chans), lambda j, s: (0, s[0])),
         pl.BlockSpec((1, STATE, chans), direction_of),
         pl.BlockSpec((2, chans), lambda j, s: (0, s[0])),
-    ] + [whole] * 4
-    in_specs += [pl.BlockSpec((chans, width), lambda j, s: (s[0], 0))]
+    ] + [whole] + [pl.BlockSpec(memory_space=pl.ANY)] * 4
     out_specs = [
         pl.BlockSpec((1, tile * STATE, chans), tokens_of),
         pl.BlockSpec((1, tile, chans), tokens_of),
@@ -372,7 +381,10 @@
                 pltpu.VMEM((U * STATE, chans), BF),
             ]
             + [pltpu.VMEM((U, chans), F32)] * 3
-            + [pltpu.VMEM((U, STATE, 128), F32), pltpu.VMEM((total, chans), BF)],
+            + [pltpu.VMEM((U, STATE, 128), F32), pltpu.VMEM((total, chans), BF)]
+            + [pltpu.VMEM((total, chans), F32)] * 2
+            + [pltpu.VMEM((total, width), BF), pltpu.VMEM((chans, width), BF)]
+            + [pltpu.SemaphoreType.DMA((4,))],
         ),
         out_shape=out_shape,
         compiler_params=pltpu.CompilerParams(vmem_limit_bytes=60 << 20),
@@ -722,7 +734,7 @@
 
     tok, cot, flag, emb, ada_b, edge = take(6)
     in_weight, out_weight, conv_weight, conv_bias, xproj_weight, ada_weight, a_log = take(7)
-    hidden_o, branch_o, xin_o, act_o, slope_o, proj_o, dy_o, silu_o, slope_z_o, mod_o, a2_o = take(11)
+    hidden_o, branch_o, xin_o, act_o, slope_o, proj_o, dy_o, silu_o, slope_z_o, mod_o, a2_o, coef_o = take(12)
     w_x, w_z, w_out, conv_w, conv_b, xproj, ada_w, rates, load_sems = take(9)
     toks, cots, flags, rows_out, rows_in = take(5)
     hidden, grad_branch, xin, z, act, slope, dy, silu_z, slope_z, pad = take(10)
@@ -884,6 +896,11 @@
     c3.back()
     c3.finish()
     stores[4].start()
+    for k in range(2):
+        for t in range(total // 128):
+            square = c3.total[k, t * 128 : (t + 1) * 128].T
+            for g in range(128 // U):
+                coef_o[k, t * (128 // U) + g] = square[128 - 2 * STATE :, g * U : (g + 1) * U]
     for copy in stores:
         copy.wait()
 
@@ -911,6 +928,7 @@
         shape((total, chans), F32),
         shape((1, 3 * width), F32),
         shape((2, STATE, chans), F32),
+        shape((2, total // U, 2 * STATE, U), F32),
     ]
     dma = pltpu.SemaphoreType.DMA
     vmem = pltpu.VMEM
@@ -942,7 +960,7 @@
     return pl.pallas_call(
         first_kernel,
         in_specs=[VMEM_SPEC] * 6 + [any_spec] * 7,
-        out_specs=[any_spec] * 9 + [VMEM_SPEC] * 2,
+        out_specs=[any_spec] * 9 + [VMEM_SPEC] * 3,
         out_shape=out_shape,
         scratch_shapes=scratch,
         compiler_params=comm_params(collective_id, 60),
@@ -973,7 +991,7 @@
     far_inputs = take(13)
     dt_weight, conv_weight, skip_all = far_inputs[6:9]
     in_weight, xproj_weight = far_inputs[4:6]
-    (result, tokg, in_ref, out_ref, a_ref, x0_ref, x1_ref, cv_ref, table_ref) = take(9)
+    (result, tokg, in_ref, out_ref, a_ref, x0_ref, x1_ref, convw_ref, convb_ref, table_ref) = take(10)
     g_sc, g_a, g_b, q_a, q_b, r0, r1, r2, red = take(9)
     dpre, dc, dflow, dalog, sums = take(5)
     slope, xpad, hidden, grad_z, w_x, w_z, xproj, dtw, conv_w, skip, hid_in, out_in, xs_in, local_sems = take(14)
@@ -997,7 +1015,7 @@
     xs = DpScatter(xs_in, *take(4))
     x_red, x_got, x_swap_sems = take(3)
     x_swap = SeqSwap(x_red, x_got, x_swap_sems)
-    row, rows_in, row_sems, table, table_sems, result_sems = take(6)
+    row, rows_in, row_sems, table, table_sems, result_sems, conv_all = take(7)
 
     j = pl.program_id(0)
     blocks = pl.num_programs(0) // 2
@@ -1036,7 +1054,7 @@
         for d in range(2):
             buf = parts_a[d][2]
             pairs += [(buf.at[q], a_ref.at[d, :, :, :, pl.ds(q * chans, chans)]) for q in range(4)]
-        pairs += [(parts_x[0][2], x0_ref), (parts_x[1][2], x1_ref), (part_c[2], cv_ref)]
+        pairs += [(parts_x[0][2], x0_ref), (parts_x[1][2], x1_ref)]
         return [pltpu.make_async_copy(a, b, result_sems.at[i]) for i, (a, b) in enumerate(pairs)]
 
     near = [(zs, k) for k in range(n)] + [(outs, k) for k in range(n)]
@@ -1297,6 +1315,13 @@
             spread.finish()
         for copy in results():
             copy.start()
+        for b in range(4 * n_dp):
+            q, place = b // n_dp, b % n_dp
+            piece = part_c[2][q, place // 2, place % 2][:, :rows_x].astype(F32)
+            conv_all[:, b * rows_x : (b + 1) * rows_x] = piece
+        for d in range(2):
+            convw_ref[d] = conv_all[5 * d : 5 * d + 4]
+            convb_ref[d : d + 1] = conv_all[5 * d + 4 : 5 * d + 5]
         for copy in results():
             copy.wait()
 
@@ -1350,7 +1375,8 @@
         shape((2, n, 2, per_d, 4 * chans), BF),
         shape(in_out + (rows_x, 128), BF),
         shape(in_out + (rows_x, 128), BF),
-        shape(in_out + (16, 128), BF),
+        shape((2, 4, 4 * chans), F32),
+        shape((2, 4 * chans), F32),
         shape((n_dp, 1, 4 * width), F32),
     ]
     dma = pltpu.SemaphoreType.DMA
@@ -1408,13 +1434,14 @@
         dma((2, 3)),
         vmem((n_dp, 1, 4 * width), F32),
         dma((2, n_dp)),
-        dma((11,)),
+        dma((10,)),
+        vmem((16, 4 * chans), F32),
     ]
     return pl.pallas_call(
         backward_kernel,
         grid=(2 * blocks,),
         in_specs=in_specs,
-        out_specs=[VMEM_SPEC] * 4 + [any_spec] * 4 + [VMEM_SPEC],
+        out_specs=[VMEM_SPEC] * 4 + [any_spec] * 3 + [VMEM_SPEC] * 3,
         out_shape=out_shape,
         scratch_shapes=scratch,
         compiler_params=comm_params(collective_id, 62),
@@ -1475,7 +1502,7 @@
 
     embedded = jax.nn.silu(time_embedding(timesteps, width)).astype(BF)
     own_flags = flags_of(scan_path)
-    hidden, grad_branch, xin, act, slope, proj, dy, silu_z, slope_z, modulation, decay2 = first_part(
+    hidden, grad_branch, xin, act, slope, proj, dy, silu_z, slope_z, modulation, decay2, coef = first_part(
         tokens[0], cotangent[0], jnp.broadcast_to(own_flags, (8, seg_len)), embedded, ada_bias[None],
         edge[None], in_weight, out_weight, conv_weight, conv_bias, xproj_weight, ada_weight.T,
         jnp.swapaxes(a_log, 1, 2), 0,
@@ -1483,7 +1510,6 @@
     scale_term = modulation[:, width : 2 * width]
     gate_term = modulation[:, 2 * width :]
     tile = 128 if n_dp <= 8 else 32
-    coef = jnp.swapaxes(proj[:, :, 128 - 2 * STATE :].reshape(2, length // U, U, 2 * STATE), 2, 3)
     held, delta, dread, branch, sorted_gated, z_part, grad_z = scan_forward(
         seq_index.astype(jnp.int32)[None], proj, act, coef, dt_weight, dt_bias, decay2,
         skip, dy, silu_z, slope_z, hidden, out_weight, tile,
@@ -1493,7 +1519,7 @@
     def in_blocks(grad):
         return grad.reshape(n_dp, n_seq, width // total, chans)
 
-    result, grad_tok, in_rows, out_rows, lines, x0, x1, conv_lines, table = scan_backward(
+    result, grad_tok, in_rows, out_rows, lines, x0, x1, convw_grad, convb_grad, table = scan_backward(
         delta, held, proj, act, coef, decay2, dy, dread,
         branch.reshape(n_seq, seg_len, width),
         sorted_gated,
@@ -1511,8 +1537,6 @@
     lines = lines.reshape(2, 128, inner).astype(F32)
     alog_grad = jnp.swapaxes(lines[:, rank : rank + STATE], 1, 2)
     xproj_grad = jnp.stack([item.reshape(inner, 128) for item in (x0, x1)]).astype(F32)
-    conv_lines = jnp.moveaxis(conv_lines[..., : chans // n_dp], 3, 0).reshape(16, inner).astype(F32)
-    conv_lines = conv_lines[: 2 * (taps + 1)].reshape(2, taps + 1, inner)
     return (
         result[None],
         grad_tok[None],
@@ -1520,8 +1544,8 @@
         ada_b_grad,
         edge_grad,
         in_rows.astype(F32),
-        conv_lines[:, :taps],
-        conv_lines[:, taps],
+        convw_grad,
+        convb_grad,
         xproj_grad,
         lines[:, :rank],
         lines[:, rank + STATE],

time: 225 us -> 221 us (0.982)
  local copies, waits for them, and re-layouts: 15.5 us -> 12.6 us
where the time goes in v4:
time: 221 us; the launch traced here: 220 us
  Pallas kernels  193 us (87%)
  local copies, waits for them, and re-layouts  12.6 us (6%)
  other arithmetic  9.58 us (4%)
  matrix products  3.57 us (2%)
    pallas_call x1, Pallas kernels, scan_backward(): pl.pallas_call(backward_kernel, grid=(2 * blocks,), in_specs=in_specs, ou...  122 us
    pallas_call x1, Pallas kernels, first_part(): pl.pallas_call(first_kernel, in_specs=[VMEM_SPEC] * 6 + [any_spec] * 7, o...  36.3 us
    pallas_call x1, Pallas kernels, scan_forward(): pl.pallas_call(forward_kernel, grid_spec=pltpu.PrefetchScalarGridSpec(num...  34 us

profile of v4, /device:TPU:11, one launch (start us, length us, event | category | flops | bytes accessed | tf_op | source)
XLA Modules:
  0.0 219.7 jit_solution(1892822150830137266)
XLA Ops:
  1.3 0.7 convert_element_type.26
  2.0 0.8 fusion.6
  2.7 0.8 fusion.7
  3.5 1.3 broadcast_in_dim.27.refs_4_
  4.8 0.6 broadcast_in_dim.26.refs_2_
  5.4 1.3 broadcast_in_dim.28.refs_5_
  6.7 0.2 multiply_cosine_fusion
  6.9 0.6 multiply_convert_fusion.refs_3_
  7.5 0.7 copy.31.refs_12_
  8.2 36.3 %first_part.1 = (bf16[512,1536]{1,0:T(8,128)(2,1)}, bf16[512,1536]{1,0:T(8,128)(2,1)}, bf16[512,768]{1,0:T(8,128)(2,1)}, bf16[2,512,768]{2,1,0:T(8,128)(2,1)}, b...) custom-call(bf16[128,1536]{1,0:T(8,128)(2,1)} %bitcast.34, ...), custom_call_target="tpu_custom_call" | custom-call | tf_op jit(solution)/shard_map/first_part/pallas_call | solution.py:960
  44.6 1.3 fusion.4
  45.9 34.0 %scan_forward.1 = (bf16[2,8192,768]{2,1,0:T(8,128)(2,1)}, f32[2,512,768]{2,1,0:T(8,128)}, f32[2,4,16,128]{3,2,1,0:T(8,128)}, bf16[512,1536]{1,0:T(8,128)(2,1)}, ...) custom-call(s32[1]{0:T(128)} %bitcast.s_ref, ...), custom_call_target="tpu_custom_call" | custom-call | tf_op jit(solution)/shard_map/scan_forward/pallas_call | solution.py:369
  79.9 122.3 %scan_backward.1 = (bf16[128,1536]{1,0:T(8,128)(2,1)}, bf16[128,1536]{1,0:T(8,128)(2,1)}, bf16[48,6144]{1,0:T(8,128)(2,1)}, bf16[96,1536]{1,0:T(8,128)(2,1)}, bf...) custom-call(f32[2,512,768]{2,1,0:T(8,128)} %get-tuple-element.51.ref, ...), custom_call_target="tpu_custom_call" | custom-call | tf_op jit(solution)/shard_map/scan_backward/pallas_call | solution.py:1440
  202.1 0.0 copy-start.3
  202.1 1.1 copy.39
  203.2 0.0 copy-start
  203.2 0.6 slice_reduce_fusion
  203.8 0.7 dynamic-slice_reduce_fusion
  204.5 1.8 convert_element_type.32
  206.4 0.0 copy-done.3
  206.4 1.1 convert_element_type.28
  207.5 0.0 copy-done
  207.5 0.5 bitcast_convert_fusion
  208.0 0.6 copy_bitcast_fusion.1
  208.6 0.8 slice_bitcast_fusion
  209.4 0.0 copy-start.1
  209.4 0.0 copy-start.2
  209.4 1.6 slice.34
  210.9 0.0 copy-done.1
  210.9 0.5 copy-done.2
  211.5 0.0 copy-start.6
  211.5 1.9 maximum_convert_fusion
  213.3 0.0 copy-done.6
  213.4 0.0 copy-start.5
  213.4 0.0 copy-start.4
  213.4 3.6 %fusion = f32[1536,576]{0,1:T(8,128)} fusion(bf16[8,1536]{1,0:T(8,128)(2,1)S(1)} %copy-done.6, f32[8,4608]{1,0:T(8,128)S(1)} %slice.32, s32[]{:T(128)S(6)} %select_n.14), kind=kOutput, calls=%fused_computation.12 | convolution fusion | flops 84934656 | bytes 3584004 | tf_op jit(solution)/shard_map/dot_general | solution.py:1536
  216.9 0.0 copy-done.5
  216.9 0.0 copy-start.7
  216.9 0.0 copy-start.8
  216.9 0.7 copy.45
  217.7 0.0 copy-done.4
  217.7 0.7 copy.46
  218.4 0.0 copy-done.7
  218.4 0.6 copy.47
  219.1 0.0 copy-done.8
  219.1 0.6 copy.48
  (3 shorter events, 0.1 us)
Async XLA Ops:
  202.1 4.2 %copy-start.3 = (bf16[48,6144]{1,0:T(8,128)(2,1)S(1)}, bf16[48,6144]{1,0:T(8,128)(2,1)}, u32[]{:S(2)}) copy-start(bf16[48,6144]{1,0:T(8,128)(2,1)} %get-tuple-element.65) | copy-start | bytes 1769476
  203.2 4.2 %copy-start = (bf16[2,4,2,16,3072]{4,3,2,1,0:T(8,128)(2,1)S(1)}, bf16[2,4,2,16,3072]{4,3,2,1,0:T(8,128)(2,1)}, u32[]{:S(2)}) copy-start(bf16[2,4,2,16,3072]{4,3,2,1,0:T(8,128)(2,1)} %get-tuple-element.70) | copy-start | bytes 4718596
  209.4 1.6 copy-start.1
  209.4 2.1 copy-start.2
  211.5 1.9 copy-start.6
  213.4 3.6 %copy-start.5 = (bf16[128,1536]{1,0:T(8,128)(2,1)S(1)}, bf16[128,1536]{1,0:T(8,128)(2,1)}, u32[]{:S(2)}) copy-start(bf16[128,1536]{1,0:T(8,128)(2,1)} %get-tuple-element.62) | copy-start | bytes 1179652
  213.4 4.3 %copy-start.4 = (bf16[128,1536]{1,0:T(8,128)(2,1)S(1)}, bf16[128,1536]{1,0:T(8,128)(2,1)}, u32[]{:S(2)}) copy-start(bf16[128,1536]{1,0:T(8,128)(2,1)} %get-tuple-element.63) | copy-start | bytes 1179652
  216.9 1.5 copy-start.7
  216.9 2.1 copy-start.8
